TPU v7x, 512 devices: a whole 4x4x16 slice. The times are simulated.
512 devices in a mesh: chan: 16 (over z_hi, y, core), lon: 32 (over x, z_lo).
Axes of the slice: x: 4, y: 4, z: 16 (z_hi: 2, z_lo: 8; z = z_hi * 8 + z_lo), core: 2. Of those that a mesh axis runs over, the one named last changes fastest.
Arguments:
- patches: bfloat16 [32, 128, 256, 128], P('chan', None, 'lon'), may hold values from -6 to 6
- embed_weight: bfloat16 [32, 128, 256], P('chan'), may hold values from -0.5 to 0.5
- channel_embed: bfloat16 [32, 256], P('chan'), may hold values from -6 to 6
- agg_query: float32 [256], replicated, may hold values from -160 to 160
- norm_gains: float32 [5, 256], replicated, may hold values from 0.25 to 1.75
- qkv_weight: bfloat16 [2, 256, 768], P(None, None, 'lon'), may hold values from -0.375 to 0.375
- proj_weight: bfloat16 [2, 256, 256], P(None, 'lon'), may hold values from -0.375 to 0.375
- up_weight: bfloat16 [2, 256, 1024], P(None, None, 'lon'), may hold values from -0.375 to 0.375
- down_weight: bfloat16 [2, 1024, 256], P(None, 'lon'), may hold values from -0.1875 to 0.1875
- decode_weight: bfloat16 [32, 256, 128], P('chan'), may hold values from -0.375 to 0.375
Outputs:
- decoded: bfloat16 [32, 128, 256, 128], P('chan', None, 'lon')
All inputs are finite; a program needn't handle non-finite values.
Results may differ from a plain program's by a relative error of at most 0.018.
Values may be sent and summed in bfloat16 or wider, within the bound.
No kernel may reach another device: no remote copies, remote signals or barrier semaphores. Data moves between devices by JAX's collectives and lax.ppermute only.
A program may use at most 64 MiB of HBM per device.

v0:
```python
import jax
import jax.numpy as jnp
from jax import lax
from jax.sharding import PartitionSpec as P

HEADS = 8
WC = 8


EPS = 1e-05


def laid_out(pieces, dim):
    pieces = jnp.moveaxis(pieces, 0, dim)
    shape = pieces.shape
    return pieces.reshape(*shape[:dim], shape[dim] * shape[dim + 1], *shape[dim + 2 :])


def gather_packed(arrays, axis, dims):
    ravelled = jnp.concatenate([a.reshape(-1) for a in arrays])
    lines, at, gathered = (lax.all_gather(ravelled, axis), 0, [])
    for a, dim in zip(arrays, dims):
        pieces = lines[:, at : at + a.size].reshape(-1, *a.shape)
        gathered.append(laid_out(pieces, dim))
        at += a.size
    return tuple(gathered)


def rows_first(arrays, axis, dims):
    turned = [jnp.moveaxis(a, dim, 0) for a, dim in zip(arrays, dims)]
    widths = [t[0].size for t in turned]
    both = jnp.concatenate([t.reshape(-1, w) for t, w in zip(turned, widths)], axis=1)
    filled = lax.all_gather(both, axis, axis=0, tiled=True)
    pieces = jnp.split(filled, [sum(widths[:k]) for k in range(1, len(widths))], axis=1)
    return tuple(
        (
            jnp.moveaxis(b.reshape(-1, *t.shape[1:]), 0, dim)
            for b, t, dim in zip(pieces, turned, dims)
        )
    )


def from_everyone(array, axis):
    size = lax.axis_size(axis)
    return lax.all_to_all(
        jnp.broadcast_to(array[None], (size, *array.shape)), axis, 0, 0, tiled=True
    )


def of_everyone(array, axis):
    everything = from_everyone(array, axis)
    return jnp.max(everything, axis=0)


def sent_together(arrays, axis, dim, along):
    columns = [a.reshape(*a.shape[:along], -1) for a in arrays]
    both = jnp.concatenate(columns, axis=along)
    filled, at, gathered = (lax.psum_scatter(both, axis, scatter_dimension=dim, tiled=True), 0, [])
    for a, column in zip(arrays, columns):
        piece = filled[..., at : at + column.shape[along]]
        gathered.append(piece.reshape(*piece.shape[:along], *a.shape[along:]))
        at += column.shape[along]
    return tuple(gathered)


def from_behind(value, axis, steps):
    count = lax.axis_size(axis)
    pairs = [(source, (source + steps) % count) for source in range(count)]
    return lax.ppermute(value, axis, pairs)


def as_sent(array):

    def short(part):
        return part.astype(jnp.bfloat16) if part.dtype == jnp.float32 else part

    return jax.tree.map(short, array)


def gathered_copies(array, axis, dim):
    pieces = from_everyone(array, axis)
    return laid_out(pieces, dim)


def layer_norm(values, gain):
    mean = jnp.mean(values, axis=-1, keepdims=True)
    centred = values - mean
    spread = jnp.mean(centred * centred, axis=-1, keepdims=True)
    return centred * lax.rsqrt(spread + EPS) * gain


def to_windows(grid):
    rows, cols, width = grid.shape
    count = cols // WC
    return (
        grid.reshape(rows, count, WC, width).transpose(1, 0, 2, 3).reshape(count, rows * WC, width)
    )


def from_windows(windows, rows):
    count, length, width = windows.shape
    return (
        windows.reshape(count, rows, WC, width)
        .transpose(1, 0, 2, 3)
        .reshape(rows, count * WC, width)
    )


def window_block(windows, gain_attn, gain_mlp, weights):
    w_qkv, w_proj, w_up, w_down = weights
    count, length, width = windows.shape
    head_dim = width // HEADS
    flat = windows.reshape(count * length, width)
    normed = layer_norm(flat, gain_attn).astype(jnp.bfloat16)
    qkv = jnp.dot(normed, w_qkv, preferred_element_type=jnp.float32).astype(jnp.bfloat16)
    qkv = qkv.reshape(count, length, 3, HEADS, head_dim)
    scores = jnp.einsum(
        "nqhd,nkhd->nhqk", qkv[:, :, 0], qkv[:, :, 1], preferred_element_type=jnp.float32
    ) * head_dim ** (-0.5)
    probs = jax.nn.softmax(scores, axis=-1).astype(jnp.bfloat16)
    mixed = jnp.einsum(
        "nhqk,nkhd->nqhd", probs, qkv[:, :, 2], preferred_element_type=jnp.float32
    ).astype(jnp.bfloat16)
    mixed = mixed.reshape(count * length, width)
    state = flat + jnp.dot(mixed, w_proj, preferred_element_type=jnp.float32)
    normed = layer_norm(state, gain_mlp).astype(jnp.bfloat16)
    hidden = jax.nn.gelu(jnp.dot(normed, w_up, preferred_element_type=jnp.float32)).astype(
        jnp.bfloat16
    )
    state = state + jnp.dot(hidden, w_down, preferred_element_type=jnp.float32)
    return state.reshape(count, length, width)


def block_weights(layer, qkv_weight, proj_weight, up_weight, down_weight):
    pieces = (qkv_weight[layer], proj_weight[layer], up_weight[layer], down_weight[layer])
    groups = lax.axis_size("chan")
    index = lax.axis_index("chan")
    part = qkv_weight.shape[1] // groups
    start = index * part
    parts = (
        lax.dynamic_slice_in_dim(pieces[0], start, part, 0),
        lax.dynamic_slice_in_dim(pieces[1], start, part, 1),
        lax.dynamic_slice_in_dim(pieces[2], start, part, 0),
        lax.dynamic_slice_in_dim(pieces[3], start, part, 1),
    )
    parts = gather_packed((parts[0], parts[1], parts[2], parts[3]), "lon", (1, 0, 1, 0))
    return rows_first((parts[0], parts[1], parts[2], parts[3]), "chan", (0, 1, 0, 1))


def body(
    patches,
    embed_weight,
    channel_embed,
    agg_query,
    norm_gains,
    qkv_weight,
    proj_weight,
    up_weight,
    down_weight,
    decode_weight,
):
    chans, rows, cols, width_p = patches.shape
    width = embed_weight.shape[2]
    count = rows * cols
    groups = lax.axis_size("chan")
    owned = count // groups
    own_rows = rows // groups
    flat = patches.reshape(chans, count, width_p)
    embedded = jnp.einsum("ctp,cpe->cte", flat, embed_weight, preferred_element_type=jnp.float32)
    embedded = embedded + channel_embed.astype(jnp.float32)[:, None, :]
    scores = jnp.einsum(
        "cte,e->ct", embedded, agg_query, precision=lax.Precision.HIGHEST
    ) * width ** (-0.5)
    local_top = jnp.max(scores, axis=0)
    top = of_everyone(local_top, "chan")
    shares = jnp.exp(scores - top[None])
    numer = jnp.einsum("ct,cte->te", shares, embedded, precision=lax.Precision.HIGHEST)
    denom = jnp.sum(shares, axis=0)
    numer, denom = tuple(
        (
            part.astype(jnp.float32)
            for part in sent_together(
                (numer.astype(jnp.bfloat16), denom.astype(jnp.bfloat16)), "chan", 0, 1
            )
        )
    )
    state = (numer / denom[:, None]).reshape(own_rows, cols, width)
    weights = block_weights(0, qkv_weight, proj_weight, up_weight, down_weight)
    state = from_windows(
        window_block(to_windows(state), norm_gains[0], norm_gains[1], weights), own_rows
    )
    half = WC // 2
    edge = from_behind(state[:, :half].astype(jnp.bfloat16), "lon", -1).astype(jnp.float32)
    moved = jnp.concatenate([state[:, half:], edge], axis=1)
    weights = block_weights(1, qkv_weight, proj_weight, up_weight, down_weight)
    moved = from_windows(
        window_block(to_windows(moved), norm_gains[2], norm_gains[3], weights), own_rows
    )
    back = from_behind(as_sent(moved[:, cols - half :]), "lon", 1)
    state = jnp.concatenate([back, moved[:, : cols - half]], axis=1)
    final = layer_norm(state.reshape(owned, width), norm_gains[4]).astype(jnp.bfloat16)
    decoded = jnp.einsum(
        "te,cep->ctp",
        gathered_copies(final, "chan", 0),
        decode_weight,
        preferred_element_type=jnp.float32,
    ).astype(jnp.bfloat16)
    return decoded.reshape(chans, rows, cols, width_p)


def solution(mesh):
    placed = (
        P("chan", None, "lon", None),
        P("chan", None, None),
        P("chan", None),
        P(),
        P(),
        P(None, None, "lon"),
        P(None, "lon", None),
        P(None, None, "lon"),
        P(None, "lon", None),
        P("chan", None, None),
    )
    return jax.shard_map(
        body, mesh=mesh, in_specs=placed, out_specs=P("chan", None, "lon", None), check_vma=False
    )
```

profile of v0, /device:TPU:1, one launch (start us, length us, event | category | flops | bytes accessed | tf_op | source)
XLA Modules:
  0.0 429.3 jit_solution(6664844522010455776)
XLA Ops:
  6.5 0.7 convert_element_type.95
  7.3 0.3 copy-done
  7.6 1.3 convolution_add_fusion
  9.0 1.9 fusion.113
  10.9 0.7 broadcast_in_dim.4
  11.5 19.2 %all-to-all-start = ((f32[16,1,1024]{2,1,0:T(1,128)}), f32[16,1,1024]{2,1,0:T(1,128)S(1)}, u32[]{:S(2)}, u32[]{:S(2)}) async-start(f32[16,1,1024]{2,1,0:T(1,128)} %broadcast_in_dim.4), calls=%async_computation | async-start | bytes 131072 | tf_op jit(solution)/shard_map/all_to_all | solution.py:45
  31.6 13.7 %all-to-all-done = f32[16,1,1024]{2,1,0:T(1,128)S(1)} async-done(((f32[16,1,1024]{2,1,0:T(1,128)}), f32[16,1,1024]{2,1,0:T(1,128)S(1)}, u32[]{:S(2)}, u32[]{:S(2)}) %all-to-all-start) | async-done | bytes 65568 | tf_op jit(solution)/shard_map/all_to_all | solution.py:45
  45.4 0.3 copy.102
  45.7 10.7 %fusion.2 = bf16[1024,1,256]{2,1,0:T(2,128)(2,1)S(1)} fusion(f32[2,1024,1]{0,2,1:T(1,128)S(1)} %copy.102, f32[2,1024,256]{2,1,0:T(8,128)S(1)} %convolution_add_fusion), kind=kOutput, calls=%fused_computation.2 | convolution fusion | flops 6291456 | bytes 2629632 | tf_op jit(solution)/shard_map/ct,cte->te/dot_general | solution.py:177
  56.8 1.0 pad_maximum_fusion
  58.0 107.9 %all-gather.2 = bf16[32,1,1536]{2,1,0:T(2,128)(2,1)S(1)} all-gather(bf16[1,1,1536]{2,1,0:T(2,128)(2,1)S(1)} %reshape.351), channel_id=2, replica_groups=mesh['chan'=16,'lon'=32] {'lon'}, dimensions={0}, use_global_device_ids=true | all-gather | bytes 101376 | tf_op jit(solution)/shard_map/all_gather | solution.py:21
  167.3 0.7 pad_maximum_fusion.1
  168.6 106.5 %all-gather.3 = bf16[32,1,1536]{2,1,0:T(2,128)(2,1)S(1)} all-gather(bf16[1,1,1536]{2,1,0:T(2,128)(2,1)S(1)} %reshape.353), channel_id=3, replica_groups=mesh['chan'=16,'lon'=32] {'lon'}, dimensions={0}, use_global_device_ids=true | all-gather | bytes 101376 | tf_op jit(solution)/shard_map/all_gather | solution.py:21
  276.4 0.7 pad_maximum_fusion.2
  277.1 0.8 convert_reduce_fusion
  278.0 0.9 fusion.101
  278.9 0.9 multiply_reduce_fusion.4
  280.0 1.4 convolution_convert_fusion.2
  281.5 0.3 fusion.109
  282.3 0.3 fusion.110
  282.8 0.5 fusion.10
  283.3 4.0 collective-permute-start
  287.3 1.0 collective-permute-done
  288.7 87.6 %all-gather.9.cloned.1.call-done = bf16[256,3072]{1,0:T(8,128)(2,1)} async-done(((bf16[16,3072]{1,0:T(8,128)(2,1)}), bf16[256,3072]{1,0:T(8,128)(2,1)}) %all-gather.9.cloned.1.call-update) | async-done | bytes 1572880 | tf_op jit(solution)/shard_map/all_gather | solution.py:33
  376.4 1.3 convolution_convert_fusion.1
  378.1 0.3 fusion.111
  378.6 0.3 fusion.112
  379.1 0.5 fusion.9
  379.7 1.9 collective-permute-start.1
  381.6 11.4 %collective-permute-done.1 = bf16[8,4,256]{2,1,0:T(4,128)(2,1)S(1)} collective-permute-done((bf16[8,4,256]{2,1,0:T(4,128)(2,1)S(1)}, bf16[8,4,256]{2,1,0:T(4,128)(2,1)S(1)}, u32[]{:S(2)}, u32[]{:S(2)}) %collective-permute-start.1) | collective-permute-done | bytes 16416 | tf_op jit(solution)/shard_map/ppermute | solution.py:69
  393.5 28.1 %all_to_all.11 = bf16[16,64,256]{2,1,0:T(8,128)(2,1)S(1)} all-to-all(bf16[16,64,256]{2,1,0:T(8,128)(2,1)S(1)} %broadcast_in_dim.5), channel_id=1, replica_groups=mesh['chan'=16,'lon'=32] {'chan'}, dimensions={0} | all-to-all | bytes 1048576 | tf_op jit(solution)/shard_map/all_to_all | solution.py:45
  421.7 1.1 fusion.4
  (121 shorter events, 7.3 us)
Async XLA Ops:
  6.5 1.1 copy-start
  6.5 2.4 copy-start.9
  8.9 21.9 %copy-start.3 = (bf16[2,256,32]{1,2,0:T(8,128)(2,1)S(1)}, bf16[2,256,32]{1,2,0:T(8,128)(2,1)}, u32[]{:S(2)}) copy-start(bf16[2,256,32]{1,2,0:T(8,128)(2,1)} %param.17) | copy-start | bytes 98308
  8.9 21.9 %copy-start.5 = (bf16[2,256,24]{1,2,0:T(8,128)(2,1)S(1)}, bf16[2,256,24]{1,2,0:T(8,128)(2,1)}, u32[]{:S(2)}) copy-start(bf16[2,256,24]{1,2,0:T(8,128)(2,1)} %param.15) | copy-start | bytes 73732
  8.9 21.9 %copy-start.4 = (bf16[2,32,256]{2,1,0:T(8,128)(2,1)S(1)}, bf16[2,32,256]{2,1,0:T(8,128)(2,1)}, u32[]{:S(2)}) copy-start(bf16[2,32,256]{2,1,0:T(8,128)(2,1)} %param.18) | copy-start | bytes 98308
  9.0 22.6 %copy-start.7 = (bf16[2,8,256]{2,1,0:T(8,128)(2,1)S(1)}, bf16[2,8,256]{2,1,0:T(8,128)(2,1)}, u32[]{:S(2)}) copy-start(bf16[2,8,256]{2,1,0:T(8,128)(2,1)} %param.16) | copy-start | bytes 24580
  11.5 33.8 %all-to-all-start = ((f32[16,1,1024]{2,1,0:T(1,128)}), f32[16,1,1024]{2,1,0:T(1,128)S(1)}, u32[]{:S(2)}, u32[]{:S(2)}) async-start(f32[16,1,1024]{2,1,0:T(1,128)} %broadcast_in_dim.4), calls=%async_computation | async-start | bytes 131072 | tf_op jit(solution)/shard_map/all_to_all | solution.py:45
  30.8 246.4 %reduce-scatter.2.cloned.1.call-start = ((), (), s32[]{:S(2)}) async-start(), calls=%async_computation.3 | async-start | bytes 835584 | tf_op jit(solution)/shard_map/reduce_scatter | solution.py:58
  57.8 222.2 %all-gather.7.cloned.1.call-start = ((), (), s32[]{:S(2)}) async-start(), calls=%async_computation.4 | async-start | bytes 1671168 | tf_op jit(solution)/shard_map/all_gather | solution.py:33
  167.9 109.2 %copy-start.8 = (f32[5,256]{1,0:T(8,128)S(1)}, f32[5,256]{1,0:T(8,128)}, u32[]{:S(2)}) copy-start(f32[5,256]{1,0:T(8,128)} %param.14) | copy-start | bytes 15364
  168.0 208.4 %all-gather.9.cloned.1.call-start = ((), (), s32[]{:S(2)}) async-start(), calls=%async_computation.5 | async-start | bytes 1671168 | tf_op jit(solution)/shard_map/all_gather | solution.py:33
  279.9 2.3 copy-start.1
  279.9 2.3 copy-start.10
  283.3 5.0 %collective-permute-start = (bf16[8,4,256]{2,1,0:T(4,128)(2,1)S(1)}, bf16[8,4,256]{2,1,0:T(4,128)(2,1)S(1)}, u32[]{:S(2)}, u32[]{:S(2)}) collective-permute-start(bf16[8,4,256]{2,1,0:T(4,128)(2,1)S(1)} %slice.191), channel_id=1, source_target_pairs={{0,31},{1,0},{2,1},{3,2},{4,3},{5,4},{6,5},{7,6},{8,7},{9,8},{10,9... | collective-permute-start | bytes 49160 | tf_op jit(solution)/shard_map/ppermute | solution.py:69
  376.4 2.3 copy-start.6
  379.1 42.5 %copy-start.2 = (bf16[2,256,128]{2,1,0:T(8,128)(2,1)S(1)}, bf16[2,256,128]{2,1,0:T(8,128)(2,1)}, u32[]{:S(2)}) copy-start(bf16[2,256,128]{2,1,0:T(8,128)(2,1)} %param.19) | copy-start | bytes 393220
  379.7 13.3 %collective-permute-start.1 = (bf16[8,4,256]{2,1,0:T(4,128)(2,1)S(1)}, bf16[8,4,256]{2,1,0:T(4,128)(2,1)S(1)}, u32[]{:S(2)}, u32[]{:S(2)}) collective-permute-start(bf16[8,4,256]{2,1,0:T(4,128)(2,1)S(1)} %slice.190), channel_id=1, source_target_pairs={{0,1},{1,2},{2,3},{3,4},{4,5},{5,6},{6,7},{7,8},{8,9},{9,10},{10,1... | collective-permute-start | bytes 49160 | tf_op jit(solution)/shard_map/ppermute | solution.py:69
Sparse Core Ops, SparseCore 0:
  57.9 95.1 reduce-scatter.1
  168.1 85.8 all-gather.6
  277.2 99.0 all-gather.8
where the time goes:
time: 430 us; the launch traced here: 429 us
  blocking collectives  243 us (57%)
  waiting for transfers between devices  114 us (27%)
  starting transfers between devices  25.3 us (6%)
  matrix products  20.7 us (5%)
  between operations  13.7 us (3%)
  other arithmetic  6.91 us (2%)
  local copies, waits for them, and re-layouts  6.39 us (1%)
    all_gather x2, blocking collectives, gather_packed(): lines, at, gathered = (lax.all_gather(ravelled, axis), 0, [])  214 us
    all_gather x2, waiting for transfers between devices, rows_first(): filled = lax.all_gather(both, axis, axis=0, tiled=True)  87.6 us
    all_to_all x1, blocking collectives, from_everyone(): lax.all_to_all(jnp.broadcast_to(array[None], (size, *array.shape)), axis,...  28.1 us
    all_to_all x1, starting transfers between devices, from_everyone(): lax.all_to_all(jnp.broadcast_to(array[None], (size, *array.shape)), axis,...  19.2 us
    all_to_all x1, waiting for transfers between devices, from_everyone(): lax.all_to_all(jnp.broadcast_to(array[None], (size, *array.shape)), axis,...  13.7 us
    ppermute x2, waiting for transfers between devices, from_behind(): return lax.ppermute(value, axis, pairs)  12.4 us
    dot_general x1, matrix products, body(): jnp.einsum('ct,cte->te', shares, embedded, precision=lax.Precision.HIGHEST)  10.7 us
  transfers between devices with their start and end apart: 6, of which 4 were waited for; matrix products, arithmetic and copies ran while one was open for 3% of the time, Pallas kernels for 0%

commit v1 on v0

v1 whole, which is shorter than its diff:
```python
import functools

import jax
import jax.numpy as jnp
from jax import lax
from jax.experimental import pallas as pl
from jax.experimental.pallas import tpu as pltpu
from jax.sharding import Mesh, PartitionSpec as P

HEADS = 8
WC = 8
EPS = 1e-05
F32 = jnp.float32
BF16 = jnp.bfloat16
GROUP = ("y", "core")
RING = ("zh", "zl")
EXTRA = 16


def dot_nt(a, b):
    return lax.dot_general(a, b, (((1,), (1,)), ((), ())), preferred_element_type=F32)


def dot_nn(a, b):
    return lax.dot_general(a, b, (((1,), (0,)), ((), ())), preferred_element_type=F32)


def thirds(x):
    hi = x.astype(BF16).astype(F32)
    mid = (x - hi).astype(BF16).astype(F32)
    return hi, mid, (x - hi) - mid


def in_rows(rows, count):
    at = lax.broadcasted_iota(jnp.int32, (count, rows[0].shape[1]), 0)
    out = jnp.zeros((count, rows[0].shape[1]), F32)
    for k, row in enumerate(rows):
        out = jnp.where(at == k, row, out)
    return out


def columns_of(rows):
    n = rows.shape[0]
    full = jnp.concatenate([rows, jnp.zeros((128 - n, 128), F32)], axis=0)
    return full.T


def embed_kernel(patches, weight, chan, query, out):
    tokens = patches.shape[1]
    own = tokens // out.shape[0]
    q = query[...]
    parts = in_rows(thirds(q), 16).astype(BF16)
    scale = q.shape[1] ** (-0.5)
    scores = []
    for c in range(2):
        proj = jnp.sum(dot_nt(parts, weight[c]), axis=0, keepdims=True)
        bias = jnp.sum(chan[c : c + 1, :].astype(F32) * q, axis=1, keepdims=True)
        split = in_rows(thirds(proj), 16).astype(BF16)
        terms = dot_nt(split, patches[c])
        scores.append((jnp.sum(terms, axis=0, keepdims=True) + bias) * scale)
    top = jnp.maximum(scores[0], scores[1])
    first = jnp.exp(scores[0] - top)
    total = first + jnp.exp(scores[1] - top)
    share = first / total
    extra = in_rows(thirds(top) + thirds(total), EXTRA).astype(BF16)
    chan0 = chan[0:1, :].astype(F32)
    chan1 = chan[1:2, :].astype(F32)
    for j in range(out.shape[0]):
        lo, hi = j * own, (j + 1) * own
        e0 = dot_nn(patches[0, lo:hi, :], weight[0]) + chan0
        e1 = dot_nn(patches[1, lo:hi, :], weight[1]) + chan1
        w = jnp.broadcast_to(share[:, lo:hi], (own, own)).T
        w = jnp.concatenate([w, w], axis=1)
        out[j, :own, :] = (e1 + w * (e0 - e1)).astype(BF16)
        out[j, own:, :own] = extra[:, lo:hi]
        out[j, own:, own:] = jnp.zeros((EXTRA, out.shape[2] - own), BF16)


def top_and_total(block):
    x = block.astype(F32)
    return x[0:1] + (x[1:2] + x[2:3]), x[3:4] + (x[4:5] + x[5:6])


def merged(averages, tops, totals):
    top = functools.reduce(jnp.maximum, tops)
    shares = [t * jnp.exp(m - top) for m, t in zip(tops, totals)]
    total = functools.reduce(jnp.add, shares)
    weights = columns_of(in_rows([s / total for s in shares], 8))
    out = None
    for d, average in enumerate(averages):
        term = weights[:, d : d + 1] * average
        out = term if out is None else out + term
    return out, top, total


def combine_kernel(got, sent, own, own_rows):
    count = got.shape[0]
    n = own.shape[0]
    stats = [top_and_total(got[d, n:, :n]) for d in range(count)]
    averages = [got[d, :n, :].astype(F32) for d in range(count)]
    state, top, total = merged(averages, [s[0] for s in stats], [s[1] for s in stats])
    own[...] = state
    own_rows[...] = in_rows([top, total], 8)
    sent[:n, :] = state.astype(BF16)
    sent[n:, :n] = in_rows(thirds(top) + thirds(total), EXTRA).astype(BF16)
    sent[n:, n:] = jnp.zeros((EXTRA, sent.shape[1] - n), BF16)


def norm(v, gain):
    mean = jnp.mean(v, axis=-1, keepdims=True)
    centred = v - mean
    spread = jnp.mean(centred * centred, axis=-1, keepdims=True)
    return centred * lax.rsqrt(spread + EPS) * gain


def attention_weights(layer, mine, other, qkv_rows, proj_rows):
    first_core = lax.axis_index("core") == 0
    x_at, zl_at = lax.axis_index("x"), lax.axis_index("zl")
    lo = 48 * layer
    for xs in range(4):
        for slot, back in enumerate(ZL_BACK):
            lon = ((x_at + (4 - xs)) & 3) * 8 + ((zl_at + (16 - back)) & 7)
            piece = xs * 8 + slot
            a = mine[piece, lo : lo + 16, :].astype(F32)
            b = other[piece, lo : lo + 16, :].astype(F32)
            head = jnp.where(first_core, a, b)
            tail = jnp.where(first_core, b, a)
            at = pl.multiple_of(lon * 24, 8)
            qkv_rows[pl.ds(at, 16), :] = head
            qkv_rows[pl.ds(at + 16, 8), :] = tail[:8]
            proj_rows[pl.ds(pl.multiple_of(lon * 8, 8), 8), :] = tail[8:]
    return qkv_rows[...].astype(BF16), proj_rows[...].astype(BF16)


def mlp_weights(layer, mine, other):
    lo = 48 * layer
    width = mine.shape[2]

    def rows(at):
        return jnp.concatenate(
            [w[:, at : at + 16, :].reshape(-1, width) for w in (mine, other)], axis=0
        )

    return rows(lo + 16), rows(lo + 32)


def attend(q, keys, values, allowed):
    width = q.shape[1]
    per_head = width // HEADS
    scale = per_head ** (-0.5)
    lane_head = lax.broadcasted_iota(jnp.int32, keys.shape, 1) // per_head
    mixed = None
    for h in range(HEADS):
        here = lane_head == h
        k = jnp.where(here, keys, 0.0).astype(BF16)
        v = jnp.where(here, values, 0.0).astype(BF16)
        s = jnp.where(allowed, dot_nt(q, k) * scale, -jnp.inf)
        e = jnp.exp(s - jnp.max(s, axis=1, keepdims=True))
        p = (e / jnp.sum(e, axis=1, keepdims=True)).astype(BF16)
        part = dot_nn(p, v)
        mixed = part if mixed is None else mixed + part
    return mixed.astype(BF16)


def gelu(x):
    return jax.nn.gelu(x, approximate=True)


def after_attention(x, mixed, gain, w_proj, w_up, w_down):
    x1 = x + dot_nn(mixed, w_proj)
    normed = norm(x1, gain).astype(BF16)
    hidden = gelu(dot_nt(normed, w_up)).astype(BF16)
    return x1 + dot_nn(hidden, w_down)


def token_at(shape, dim):
    t = lax.broadcasted_iota(jnp.int32, shape, dim)
    return t // 64, (t & 7) // 4, t


def half_tokens(x, half):
    to = lax.broadcasted_iota(jnp.int32, (64, 128), 0)
    source = lax.broadcasted_iota(jnp.int32, (64, 128), 1)
    pick = (to // 4) * 8 + half * 4 + (to & 3) == source
    return dot_nn(jnp.where(pick, 1.0, 0.0).astype(BF16), x).astype(BF16)


def block0_kernel(own, own_rows, got, gains, mine, other, state, west, east, qkv_rows, proj_rows):
    n, width = own.shape
    got_top, got_total = top_and_total(got[n:, :n])
    rows = own_rows[...]
    x, _, _ = merged(
        [own[...], got[:n, :].astype(F32)], [rows[0:1], got_top], [rows[1:2], got_total]
    )
    w_qkv, w_proj = attention_weights(0, mine, other, qkv_rows, proj_rows)
    w_up, w_down = mlp_weights(0, mine, other)
    a = norm(x, gains[0:1, :]).astype(BF16)
    qkv = dot_nt(a, w_qkv).astype(BF16).astype(F32)
    allowed = token_at((n, n), 0)[0] == token_at((n, n), 1)[0]
    mixed = attend(
        qkv[:, :width].astype(BF16), qkv[:, width : 2 * width], qkv[:, 2 * width :], allowed
    )
    x = after_attention(x, mixed, gains[1:2, :], w_proj, w_up, w_down)
    state[...] = x
    short = x.astype(BF16)
    west[...] = half_tokens(short, 0)
    east[...] = half_tokens(short, 1)


def block1_kernel(state, from_west, from_east, gains, mine, other, out, qkv_rows, proj_rows):
    n, width = state.shape
    x = state[...]
    w_qkv, w_proj = attention_weights(1, mine, other, qkv_rows, proj_rows)
    w_up, w_down = mlp_weights(1, mine, other)
    sides = jnp.concatenate([from_west[...].astype(F32), from_east[...].astype(F32)], axis=0)
    gain = gains[2:3, :]
    a = norm(x, gain).astype(BF16)
    b = norm(sides, gain).astype(BF16)
    qkv = dot_nt(a, w_qkv).astype(BF16).astype(F32)
    side_kv = dot_nt(b, w_qkv[width:, :]).astype(BF16).astype(F32)
    keys = jnp.concatenate([qkv[:, width : 2 * width], side_kv[:, :width]], axis=0)
    values = jnp.concatenate([qkv[:, 2 * width :], side_kv[:, width:]], axis=0)
    q_block, q_half, _ = token_at((n, 2 * n), 0)
    k_block, k_half, k_at = token_at((n, 2 * n), 1)
    side = k_at - n
    k_block = jnp.where(k_at < n, k_block, (side & 63) // 32)
    k_half = jnp.where(k_at < n, k_half, side // 64)
    allowed = (q_block == k_block) & (q_half == k_half)
    mixed = attend(qkv[:, :width].astype(BF16), keys, values, allowed)
    x = after_attention(x, mixed, gains[3:4, :], w_proj, w_up, w_down)
    final = norm(x, gains[4:5, :]).astype(BF16)
    for j in range(out.shape[0]):
        out[j] = final


def decode_kernel(tokens, weight, out):
    count, own, width = tokens.shape
    for c in range(2):
        w = weight[c]
        for j in range(count):
            out[c, j * own : (j + 1) * own, :] = dot_nn(tokens[j], w).astype(BF16)


def on_core(kernel, outs, scratch=(), flops=0, moved=0):
    vmem = pl.BlockSpec(memory_space=pltpu.VMEM)

    def call(*operands):
        return pl.pallas_call(
            kernel,
            out_shape=outs,
            in_specs=[vmem] * len(operands),
            out_specs=jax.tree.map(lambda _: vmem, outs),
            scratch_shapes=list(scratch),
            compiler_params=pltpu.CompilerParams(vmem_limit_bytes=40 * 2**20),
            cost_estimate=pl.CostEstimate(flops=flops, bytes_accessed=moved, transcendentals=0),
        )(*operands)

    return call


def shifted(value, axes, size, steps):
    return lax.ppermute(value, axes, [(i, (i + steps) % size) for i in range(size)])


ZL_BACK = (0, 2, -2, 4, 1, 3, -1, 5)


def eastward():
    pairs = []
    for zh in range(2):
        for x in range(4):
            for zl in range(8):
                to = (zh, x, zl + 1) if zl < 7 else (1 - zh, (x + 1) % 4, 0)
                pairs.append(((zh * 4 + x) * 8 + zl, (to[0] * 4 + to[1]) * 8 + to[2]))
    return pairs


def weight_pieces(qkv, proj, up, down):
    core = lax.axis_index("core")
    qkv, up = jnp.swapaxes(qkv, 1, 2), jnp.swapaxes(up, 1, 2)
    attn = jnp.concatenate([qkv, proj], axis=1)
    lanes = [lax.dynamic_slice_in_dim(a, core * 16, 16, 1) for a in (attn, up, down)]
    piece = jnp.concatenate(lanes, axis=1)
    return piece.reshape(1, -1, piece.shape[2])


def body(
    patches,
    embed_weight,
    channel_embed,
    agg_query,
    norm_gains,
    qkv_weight,
    proj_weight,
    up_weight,
    down_weight,
    decode_weight,
):
    chans, rows, cols, width_p = patches.shape
    width = embed_weight.shape[2]
    tokens = rows * cols
    parts = lax.axis_size("y") * lax.axis_size("core")
    own = tokens // parts

    piece = weight_pieces(qkv_weight, proj_weight, up_weight, down_weight)
    pieces = jnp.concatenate(
        [piece] + [shifted(piece, RING, 16, k) for k in (2, -2, 4)], axis=0
    )
    pieces = jnp.concatenate([pieces, shifted(pieces, RING, 16, 1)], axis=0)
    mine = jnp.concatenate([pieces] + [shifted(pieces, "x", 4, k) for k in (1, 2, 3)], axis=0)
    other = shifted(mine, "core", 2, 1)

    sums = on_core(
        embed_kernel,
        jax.ShapeDtypeStruct((parts, own + EXTRA, width), BF16),
        flops=2 * chans * tokens * width_p * width,
        moved=2 * 2**20,
    )(
        patches.reshape(chans, tokens, width_p),
        embed_weight,
        channel_embed,
        agg_query.reshape(1, width),
    )
    got = lax.all_to_all(sums, GROUP, 0, 0, tiled=True)
    sent, average, stats = on_core(
        combine_kernel,
        (
            jax.ShapeDtypeStruct((own + EXTRA, width), BF16),
            jax.ShapeDtypeStruct((own, width), F32),
            jax.ShapeDtypeStruct((8, own), F32),
        ),
        moved=2**20,
    )(got)
    partner = shifted(sent, "zh", 2, 1)

    scratch = [pltpu.VMEM((3 * width, width), F32), pltpu.VMEM((width, width), F32)]
    half = jax.ShapeDtypeStruct((own // 2, width), BF16)
    block_flops = 2 * own * width * width * 12
    state, west, east = on_core(
        block0_kernel,
        (jax.ShapeDtypeStruct((own, width), F32), half, half),
        scratch,
        flops=block_flops,
        moved=4 * 2**20,
    )(average, stats, partner, norm_gains, mine, other)
    pairs = eastward()
    from_west = lax.ppermute(east, ("zh", "x", "zl"), pairs)
    from_east = lax.ppermute(west, ("zh", "x", "zl"), [(b, a) for a, b in pairs])
    final = on_core(
        block1_kernel,
        jax.ShapeDtypeStruct((parts, own, width), BF16),
        scratch,
        flops=block_flops,
        moved=4 * 2**20,
    )(state, from_west, from_east, norm_gains, mine, other)
    everyone = lax.all_to_all(final, GROUP, 0, 0, tiled=True)
    decoded = on_core(
        decode_kernel,
        jax.ShapeDtypeStruct((chans, tokens, width_p), BF16),
        flops=2 * chans * tokens * width_p * width,
        moved=2 * 2**20,
    )(everyone, decode_weight)
    return decoded.reshape(chans, rows, cols, width_p)


def solution(mesh):
    fine = Mesh(mesh.devices.reshape(2, 4, 2, 4, 8), ("zh", "y", "core", "x", "zl"))
    chan, lon = ("zh", "y", "core"), ("x", "zl")
    placed = (
        P(chan, None, lon, None),
        P(chan, None, None),
        P(chan, None),
        P(),
        P(),
        P(None, None, lon),
        P(None, lon, None),
        P(None, None, lon),
        P(None, lon, None),
        P(chan, None, None),
    )
    return jax.shard_map(
        body, mesh=fine, in_specs=placed, out_specs=P(chan, None, lon, None), check_vma=False
    )
```

time: 430 us -> 126 us (0.29)
  blocking collectives: 243 us -> 29.9 us
  waiting for transfers between devices: 114 us -> 29.8 us
  starting transfers between devices: 25.3 us -> 56 us
  matrix products: 20.7 us -> 0 us
  between operations: 13.7 us -> 0.28 us
  Pallas kernels: 0 us -> 8.14 us
  other arithmetic: 6.91 us -> 0.79 us
  local copies, waits for them, and re-layouts: 6.39 us -> 0.94 us
    all_gather x2 -> x0, blocking collectives: 214 us -> none  [gather_packed(): lines, at, gathered = (lax.all_gather(ravelled, axis), 0, [])]
    all_gather x2 -> x0, waiting for transfers between devices: 87.6 us -> none  [rows_first(): filled = lax.all_gather(both, axis, axis=0, tiled=True)]
    ppermute x2 -> x11, starting transfers between devices: 5.9 us -> 56 us  [the longest x9 48.2 us: shifted(): lax.ppermute(value, axes, [(i, (i + steps) % size) for i in range(size)])]
    dot_general x14 -> x0, matrix products: 20.1 us -> none  [the longest x1 10.7 us: body(): jnp.einsum('ct,cte->te', shares, embedded, precision=lax.Precision.HIGHEST)]
    all_to_all x1 -> x0, starting transfers between devices: 19.2 us -> none  [from_everyone(): lax.all_to_all(jnp.broadcast_to(array[None], (size, *array.shape)), axis,...]
    ppermute x2 -> x11, waiting for transfers between devices: 12.4 us -> 29.8 us  [the longest x9 23.8 us: shifted(): lax.ppermute(value, axes, [(i, (i + steps) % size) for i in range(size)])]
    all_to_all x1 -> x0, waiting for transfers between devices: 13.7 us -> none  [from_everyone(): lax.all_to_all(jnp.broadcast_to(array[None], (size, *array.shape)), axis,...]
    pallas_call x0 -> x5, Pallas kernels: none -> 8.14 us  [call(): pl.pallas_call(kernel, out_shape=outs, in_specs=[vmem] * len(operands), o...]
  transfers between devices with their start and end apart: 6 -> 11, of which waited for: 4 -> 6; matrix products, arithmetic and copies ran while one was open for 3% -> 0% of each run, Pallas kernels for 0% -> 1%
where the time goes in v1:
time: 126 us
  starting transfers between devices  56 us (44%)
  blocking collectives  29.9 us (24%)
  waiting for transfers between devices  29.8 us (24%)
  Pallas kernels  8.14 us (6%)
    ppermute x9, starting transfers between devices, shifted(): lax.ppermute(value, axes, [(i, (i + steps) % size) for i in range(size)])  48.2 us
    ppermute x9, waiting for transfers between devices, shifted(): lax.ppermute(value, axes, [(i, (i + steps) % size) for i in range(size)])  23.8 us
    all_to_all x1, blocking collectives, body(): everyone = lax.all_to_all(final, GROUP, 0, 0, tiled=True)  15.2 us
    all_to_all x1, blocking collectives, body(): got = lax.all_to_all(sums, GROUP, 0, 0, tiled=True)  14.7 us
    pallas_call x5, Pallas kernels, call(): pl.pallas_call(kernel, out_shape=outs, in_specs=[vmem] * len(operands), o...  8.14 us
    ppermute x1, waiting for transfers between devices, body(): from_west = lax.ppermute(east, ('zh', 'x', 'zl'), pairs)  6.04 us
    ppermute x1, starting transfers between devices, body(): lax.ppermute(west, ('zh', 'x', 'zl'), [(b, a) for a, b in pairs])  5.84 us
  transfers between devices with their start and end apart: 11, of which 6 were waited for; matrix products, arithmetic and copies ran while one was open for 0% of the time, Pallas kernels for 1%

profile of v1, /device:TPU:1, one launch (start us, length us, event | category | flops | bytes accessed | tf_op | source)
XLA Modules:
  0.0 125.9 jit_solution(8470949794154049941)
XLA Ops:
  0.0 0.8 copy-done
  0.8 0.8 fusion
  1.5 5.7 %collective-permute-start.1 = (bf16[1,96,256]{2,1,0:T(8,128)(2,1)S(1)}, bf16[1,96,256]{2,1,0:T(8,128)(2,1)S(1)}, u32[]{:S(2)}, u32[]{:S(2)}) collective-permute-start(bf16[1,96,256]{2,1,0:T(8,128)(2,1)S(1)} %bitcast.12), channel_id=1, source_target_pairs={{0,2},{1,3},{2,4},{3,5},{4,6},{5,7},{6,256},{7,257},{256,258},{257... | collective-permute-start | bytes 147464 | tf_op jit(solution)/shard_map/ppermute | solution.py:262
  7.3 8.6 %collective-permute-start.2 = (bf16[1,96,256]{2,1,0:T(8,128)(2,1)S(1)}, bf16[1,96,256]{2,1,0:T(8,128)(2,1)S(1)}, u32[]{:S(2)}, u32[]{:S(2)}) collective-permute-start(bf16[1,96,256]{2,1,0:T(8,128)(2,1)S(1)} %bitcast.13), channel_id=1, source_target_pairs={{0,262},{1,263},{2,0},{3,1},{4,2},{5,3},{6,4},{7,5},{256,6},{257,7... | collective-permute-start | bytes 147464 | tf_op jit(solution)/shard_map/ppermute | solution.py:262
  15.9 2.7 %collective-permute-start.3 = (bf16[1,96,256]{2,1,0:T(8,128)(2,1)S(1)}, bf16[1,96,256]{2,1,0:T(8,128)(2,1)S(1)}, u32[]{:S(2)}, u32[]{:S(2)}) collective-permute-start(bf16[1,96,256]{2,1,0:T(8,128)(2,1)S(1)} %bitcast.14), channel_id=1, source_target_pairs={{0,4},{1,5},{2,6},{3,7},{4,256},{5,257},{6,258},{7,259},{256,260},... | collective-permute-start | bytes 147464 | tf_op jit(solution)/shard_map/ppermute | solution.py:262
  18.6 0.0 collective-permute-done.1
  18.6 6.1 %collective-permute-done.3 = bf16[1,96,256]{2,1,0:T(8,128)(2,1)S(1)} collective-permute-done((bf16[1,96,256]{2,1,0:T(8,128)(2,1)S(1)}, bf16[1,96,256]{2,1,0:T(8,128)(2,1)S(1)}, u32[]{:S(2)}, u32[]{:S(2)}) %collective-permute-start.3) | collective-permute-done | bytes 49184 | tf_op jit(solution)/shard_map/ppermute | solution.py:262
  24.7 2.6 %collective-permute-start.4 = (bf16[4,96,256]{2,1,0:T(8,128)(2,1)S(1)}, bf16[4,96,256]{2,1,0:T(8,128)(2,1)S(1)}, u32[]{:S(2)}, u32[]{:S(2)}) collective-permute-start(bf16[4,96,256]{2,1,0:T(8,128)(2,1)S(1)} %pad_maximum_fusion), channel_id=1, source_target_pairs={{0,1},{1,2},{2,3},{3,4},{4,5},{5,6},{6,7},{7,256},{256,257},{257,2... | collective-permute-start | bytes 589832 | tf_op jit(solution)/shard_map/ppermute | solution.py:262
  27.3 0.0 copy-start.1
  27.3 0.0 copy-start.2
  27.4 0.0 copy-start.5
  27.4 0.0 copy-start.6
  27.4 4.9 %collective-permute-done.4 = bf16[4,96,256]{2,1,0:T(8,128)(2,1)S(1)} collective-permute-done((bf16[4,96,256]{2,1,0:T(8,128)(2,1)S(1)}, bf16[4,96,256]{2,1,0:T(8,128)(2,1)S(1)}, u32[]{:S(2)}, u32[]{:S(2)}) %collective-permute-start.4) | collective-permute-done | bytes 196640 | tf_op jit(solution)/shard_map/ppermute | solution.py:262
  32.4 3.1 %collective-permute-start.5 = (bf16[8,96,256]{2,1,0:T(8,128)(2,1)S(1)}, bf16[8,96,256]{2,1,0:T(8,128)(2,1)S(1)}, u32[]{:S(2)}, u32[]{:S(2)}) collective-permute-start(bf16[8,96,256]{2,1,0:T(8,128)(2,1)S(1)} %get-tuple-element.17), channel_id=1, source_target_pairs={{0,8},{8,16},{16,24},{24,0},{1,9},{9,17},{17,25},{25,1},{2,10},{10... | collective-permute-start | bytes 1179656 | tf_op jit(solution)/shard_map/ppermute | solution.py:262
  35.5 4.4 %collective-permute-start.6 = (bf16[8,96,256]{2,1,0:T(8,128)(2,1)S(1)}, bf16[8,96,256]{2,1,0:T(8,128)(2,1)S(1)}, u32[]{:S(2)}, u32[]{:S(2)}) collective-permute-start(bf16[8,96,256]{2,1,0:T(8,128)(2,1)S(1)} %get-tuple-element.17), channel_id=1, source_target_pairs={{0,16},{8,24},{16,0},{24,8},{1,17},{9,25},{17,1},{25,9},{2,18},{10... | collective-permute-start | bytes 1179656 | tf_op jit(solution)/shard_map/ppermute | solution.py:262
  39.9 3.1 %collective-permute-start.7 = (bf16[8,96,256]{2,1,0:T(8,128)(2,1)S(1)}, bf16[8,96,256]{2,1,0:T(8,128)(2,1)S(1)}, u32[]{:S(2)}, u32[]{:S(2)}) collective-permute-start(bf16[8,96,256]{2,1,0:T(8,128)(2,1)S(1)} %get-tuple-element.17), channel_id=1, source_target_pairs={{0,24},{8,0},{16,8},{24,16},{1,25},{9,1},{17,9},{25,17},{2,26},{10... | collective-permute-start | bytes 1179656 | tf_op jit(solution)/shard_map/ppermute | solution.py:262
  43.0 7.9 %collective-permute-done.6 = bf16[8,96,256]{2,1,0:T(8,128)(2,1)S(1)} collective-permute-done((bf16[8,96,256]{2,1,0:T(8,128)(2,1)S(1)}, bf16[8,96,256]{2,1,0:T(8,128)(2,1)S(1)}, u32[]{:S(2)}, u32[]{:S(2)}) %collective-permute-start.6) | collective-permute-done | bytes 393248 | tf_op jit(solution)/shard_map/ppermute | solution.py:262
  50.9 2.5 %collective-permute-done.7 = bf16[8,96,256]{2,1,0:T(8,128)(2,1)S(1)} collective-permute-done((bf16[8,96,256]{2,1,0:T(8,128)(2,1)S(1)}, bf16[8,96,256]{2,1,0:T(8,128)(2,1)S(1)}, u32[]{:S(2)}, u32[]{:S(2)}) %collective-permute-start.7) | collective-permute-done | bytes 393248 | tf_op jit(solution)/shard_map/ppermute | solution.py:262
  53.4 0.0 copy-start.4
  53.5 6.4 %collective-permute-start.8 = (bf16[32,96,256]{2,1,0:T(8,128)(2,1)S(1)}, bf16[32,96,256]{2,1,0:T(8,128)(2,1)S(1)}, u32[]{:S(2)}, u32[]{:S(2)}) collective-permute-start(bf16[32,96,256]{2,1,0:T(8,128)(2,1)S(1)} %constant_dynamic-update-slice_fusion.5.mine), channel_id=1, source_target_pairs={{0,32},{32,0},{1,33},{33,1},{2,34},{34,2},{3,35},{35,3},{4,36},{36... | collective-permute-start | bytes 4718600 | tf_op jit(solution)/shard_map/ppermute | solution.py:262
  59.9 0.9 shard_map.100
  60.8 14.7 %all_to_all.10.got = bf16[8,144,256]{2,1,0:T(8,128)(2,1)S(1)} all-to-all(bf16[8,144,256]{2,1,0:T(8,128)(2,1)S(1)} %shard_map.100), channel_id=1, replica_groups=mesh['zh'=2,'y'=4,'core'=2,'x'=4,'zl'=8] {'y','core'}, dimensions={0} | all-to-all | bytes 1179648 | tf_op jit(solution)/shard_map/all_to_all | solution.py:324
  75.5 0.4 shard_map.101
  75.9 11.7 %collective-permute-start = (bf16[144,256]{1,0:T(8,128)(2,1)S(1)}, bf16[144,256]{1,0:T(8,128)(2,1)S(1)}, u32[]{:S(2)}, u32[]{:S(2)}) collective-permute-start(bf16[144,256]{1,0:T(8,128)(2,1)S(1)} %get-tuple-element.13), channel_id=1, source_target_pairs={{0,256},{256,0},{1,257},{257,1},{2,258},{258,2},{3,259},{259,3},{4... | collective-permute-start | bytes 221192 | tf_op jit(solution)/shard_map/ppermute | solution.py:262
  87.6 2.3 %collective-permute-done.got = bf16[144,256]{1,0:T(8,128)(2,1)S(1)} collective-permute-done((bf16[144,256]{1,0:T(8,128)(2,1)S(1)}, bf16[144,256]{1,0:T(8,128)(2,1)S(1)}, u32[]{:S(2)}, u32[]{:S(2)}) %collective-permute-start) | collective-permute-done | bytes 73760 | tf_op jit(solution)/shard_map/ppermute | solution.py:262
  89.9 2.4 %shard_map.102 = (f32[128,256]{1,0:T(8,128)S(1)}, bf16[64,256]{1,0:T(8,128)(2,1)S(1)}, bf16[64,256]{1,0:T(8,128)(2,1)S(1)}) custom-call(f32[128,256]{1,0:T(8,128)S(1)} %get-tuple-element.11.own, f32[8,128]{1,0:T(8,128)S(1)} %get-tuple-element.12.own_rows, bf16[144,256]{1,0:T(8,128)(2,1)S(1)} %collective-permute-done.got, f32[5,256]{1,0:T(8,128)S(1)} %copy-done.4, ...), custom_call_target="tpu_custom_call" | custom-call | flops 201326592 | bytes 4194304 | tf_op jit(solution)/shard_map/pallas_call | solution.py:248
  92.4 5.8 %collective-permute-start.10 = (bf16[64,256]{1,0:T(8,128)(2,1)S(1)}, bf16[64,256]{1,0:T(8,128)(2,1)S(1)}, u32[]{:S(2)}, u32[]{:S(2)}) collective-permute-start(bf16[64,256]{1,0:T(8,128)(2,1)S(1)} %get-tuple-element.16), channel_id=1, source_target_pairs={{1,0},{2,1},{3,2},{4,3},{5,4},{6,5},{7,6},{264,7},{9,8},{10,9},{11... | collective-permute-start | bytes 98312 | tf_op jit(solution)/shard_map/ppermute | solution.py:348
  98.2 1.9 %collective-permute-start.9 = (bf16[64,256]{1,0:T(8,128)(2,1)S(1)}, bf16[64,256]{1,0:T(8,128)(2,1)S(1)}, u32[]{:S(2)}, u32[]{:S(2)}) collective-permute-start(bf16[64,256]{1,0:T(8,128)(2,1)S(1)} %get-tuple-element.15), channel_id=1, source_target_pairs={{0,1},{1,2},{2,3},{3,4},{4,5},{5,6},{6,7},{7,264},{8,9},{9,10},{10... | collective-permute-start | bytes 98312 | tf_op jit(solution)/shard_map/ppermute | solution.py:347
  100.2 6.0 %collective-permute-done.9.from_west = bf16[64,256]{1,0:T(8,128)(2,1)S(1)} collective-permute-done((bf16[64,256]{1,0:T(8,128)(2,1)S(1)}, bf16[64,256]{1,0:T(8,128)(2,1)S(1)}, u32[]{:S(2)}, u32[]{:S(2)}) %collective-permute-start.9) | collective-permute-done | bytes 32800 | tf_op jit(solution)/shard_map/ppermute | solution.py:347
  106.2 3.2 %shard_map.103 = bf16[8,128,256]{2,1,0:T(8,128)(2,1)S(1)} custom-call(f32[128,256]{1,0:T(8,128)S(1)} %get-tuple-element.14.state, bf16[64,256]{1,0:T(8,128)(2,1)S(1)} %collective-permute-done.9.from_west, bf16[64,256]{1,0:T(8,128)(2,1)S(1)} %collective-permute-done.10.from_east, f32[5,256]{1,0:T(8,128)S(1)} %copy-done.4, ...), custom_call_target="tpu_custom_call" | custom-call | flops 201326592 | bytes 4194304 | tf_op jit(solution)/shard_map/pallas_call | solution.py:248
  109.5 15.2 %all_to_all.11.tokens = bf16[8,128,256]{2,1,0:T(8,128)(2,1)S(1)} all-to-all(bf16[8,128,256]{2,1,0:T(8,128)(2,1)S(1)} %shard_map.103), channel_id=1, replica_groups=mesh['zh'=2,'y'=4,'core'=2,'x'=4,'zl'=8] {'y','core'}, dimensions={0} | all-to-all | bytes 1048576 | tf_op jit(solution)/shard_map/all_to_all | solution.py:356
  124.6 1.2 shard_map.104
  (23 shorter events, 0.2 us)
Async XLA Ops:
  0.0 0.8 copy-start
  1.5 17.1 %collective-permute-start.1 = (bf16[1,96,256]{2,1,0:T(8,128)(2,1)S(1)}, bf16[1,96,256]{2,1,0:T(8,128)(2,1)S(1)}, u32[]{:S(2)}, u32[]{:S(2)}) collective-permute-start(bf16[1,96,256]{2,1,0:T(8,128)(2,1)S(1)} %bitcast.12), channel_id=1, source_target_pairs={{0,2},{1,3},{2,4},{3,5},{4,6},{5,7},{6,256},{7,257},{256,258},{257... | collective-permute-start | bytes 147464 | tf_op jit(solution)/shard_map/ppermute | solution.py:262
  7.3 11.4 %collective-permute-start.2 = (bf16[1,96,256]{2,1,0:T(8,128)(2,1)S(1)}, bf16[1,96,256]{2,1,0:T(8,128)(2,1)S(1)}, u32[]{:S(2)}, u32[]{:S(2)}) collective-permute-start(bf16[1,96,256]{2,1,0:T(8,128)(2,1)S(1)} %bitcast.13), channel_id=1, source_target_pairs={{0,262},{1,263},{2,0},{3,1},{4,2},{5,3},{6,4},{7,5},{256,6},{257,7... | collective-permute-start | bytes 147464 | tf_op jit(solution)/shard_map/ppermute | solution.py:262
  15.9 8.8 %collective-permute-start.3 = (bf16[1,96,256]{2,1,0:T(8,128)(2,1)S(1)}, bf16[1,96,256]{2,1,0:T(8,128)(2,1)S(1)}, u32[]{:S(2)}, u32[]{:S(2)}) collective-permute-start(bf16[1,96,256]{2,1,0:T(8,128)(2,1)S(1)} %bitcast.14), channel_id=1, source_target_pairs={{0,4},{1,5},{2,6},{3,7},{4,256},{5,257},{6,258},{7,259},{256,260},... | collective-permute-start | bytes 147464 | tf_op jit(solution)/shard_map/ppermute | solution.py:262
  24.7 7.6 %collective-permute-start.4 = (bf16[4,96,256]{2,1,0:T(8,128)(2,1)S(1)}, bf16[4,96,256]{2,1,0:T(8,128)(2,1)S(1)}, u32[]{:S(2)}, u32[]{:S(2)}) collective-permute-start(bf16[4,96,256]{2,1,0:T(8,128)(2,1)S(1)} %pad_maximum_fusion), channel_id=1, source_target_pairs={{0,1},{1,2},{2,3},{3,4},{4,5},{5,6},{6,7},{7,256},{256,257},{257,2... | collective-permute-start | bytes 589832 | tf_op jit(solution)/shard_map/ppermute | solution.py:262
  27.3 32.6 %copy-start.1 = (bf16[2,128,8,128]{3,2,1,0:T(8,128)(2,1)S(1)}, bf16[2,128,8,128]{3,2,1,0:T(8,128)(2,1)}, u32[]{:S(2)}) copy-start(bf16[2,128,8,128]{3,2,1,0:T(8,128)(2,1)} %param.10) | copy-start | bytes 1572868
  27.3 32.6 %copy-start.2 = (bf16[2,128,256]{2,1,0:T(8,128)(2,1)S(1)}, bf16[2,128,256]{2,1,0:T(8,128)(2,1)}, u32[]{:S(2)}) copy-start(bf16[2,128,256]{2,1,0:T(8,128)(2,1)} %weight.2) | copy-start | bytes 393220
  27.4 32.5 %copy-start.5 = (bf16[2,256]{1,0:T(2,128)(2,1)S(1)}, bf16[2,256]{1,0:T(2,128)(2,1)}, u32[]{:S(2)}) copy-start(bf16[2,256]{1,0:T(2,128)(2,1)} %chan.1) | copy-start | bytes 3076
  27.4 32.5 %copy-start.6 = (f32[256]{0:T(256)S(1)}, f32[256]{0:T(256)}, u32[]{:S(2)}) copy-start(f32[256]{0:T(256)} %param.13) | copy-start | bytes 3076
  32.4 10.6 %collective-permute-start.5 = (bf16[8,96,256]{2,1,0:T(8,128)(2,1)S(1)}, bf16[8,96,256]{2,1,0:T(8,128)(2,1)S(1)}, u32[]{:S(2)}, u32[]{:S(2)}) collective-permute-start(bf16[8,96,256]{2,1,0:T(8,128)(2,1)S(1)} %get-tuple-element.17), channel_id=1, source_target_pairs={{0,8},{8,16},{16,24},{24,0},{1,9},{9,17},{17,25},{25,1},{2,10},{10... | collective-permute-start | bytes 1179656 | tf_op jit(solution)/shard_map/ppermute | solution.py:262
  35.5 15.4 %collective-permute-start.6 = (bf16[8,96,256]{2,1,0:T(8,128)(2,1)S(1)}, bf16[8,96,256]{2,1,0:T(8,128)(2,1)S(1)}, u32[]{:S(2)}, u32[]{:S(2)}) collective-permute-start(bf16[8,96,256]{2,1,0:T(8,128)(2,1)S(1)} %get-tuple-element.17), channel_id=1, source_target_pairs={{0,16},{8,24},{16,0},{24,8},{1,17},{9,25},{17,1},{25,9},{2,18},{10... | collective-permute-start | bytes 1179656 | tf_op jit(solution)/shard_map/ppermute | solution.py:262
  39.9 13.5 %collective-permute-start.7 = (bf16[8,96,256]{2,1,0:T(8,128)(2,1)S(1)}, bf16[8,96,256]{2,1,0:T(8,128)(2,1)S(1)}, u32[]{:S(2)}, u32[]{:S(2)}) collective-permute-start(bf16[8,96,256]{2,1,0:T(8,128)(2,1)S(1)} %get-tuple-element.17), channel_id=1, source_target_pairs={{0,24},{8,0},{16,8},{24,16},{1,25},{9,1},{17,9},{25,17},{2,26},{10... | collective-permute-start | bytes 1179656 | tf_op jit(solution)/shard_map/ppermute | solution.py:262
  53.4 36.5 %copy-start.4 = (f32[5,256]{1,0:T(8,128)S(1)}, f32[5,256]{1,0:T(8,128)}, u32[]{:S(2)}) copy-start(f32[5,256]{1,0:T(8,128)} %gains.3) | copy-start | bytes 15364
  53.5 36.5 %collective-permute-start.8 = (bf16[32,96,256]{2,1,0:T(8,128)(2,1)S(1)}, bf16[32,96,256]{2,1,0:T(8,128)(2,1)S(1)}, u32[]{:S(2)}, u32[]{:S(2)}) collective-permute-start(bf16[32,96,256]{2,1,0:T(8,128)(2,1)S(1)} %constant_dynamic-update-slice_fusion.5.mine), channel_id=1, source_target_pairs={{0,32},{32,0},{1,33},{33,1},{2,34},{34,2},{3,35},{35,3},{4,36},{36... | collective-permute-start | bytes 4718600 | tf_op jit(solution)/shard_map/ppermute | solution.py:262
  75.9 14.0 %collective-permute-start = (bf16[144,256]{1,0:T(8,128)(2,1)S(1)}, bf16[144,256]{1,0:T(8,128)(2,1)S(1)}, u32[]{:S(2)}, u32[]{:S(2)}) collective-permute-start(bf16[144,256]{1,0:T(8,128)(2,1)S(1)} %get-tuple-element.13), channel_id=1, source_target_pairs={{0,256},{256,0},{1,257},{257,1},{2,258},{258,2},{3,259},{259,3},{4... | collective-permute-start | bytes 221192 | tf_op jit(solution)/shard_map/ppermute | solution.py:262
  92.4 7.8 %collective-permute-start.10 = (bf16[64,256]{1,0:T(8,128)(2,1)S(1)}, bf16[64,256]{1,0:T(8,128)(2,1)S(1)}, u32[]{:S(2)}, u32[]{:S(2)}) collective-permute-start(bf16[64,256]{1,0:T(8,128)(2,1)S(1)} %get-tuple-element.16), channel_id=1, source_target_pairs={{1,0},{2,1},{3,2},{4,3},{5,4},{6,5},{7,6},{264,7},{9,8},{10,9},{11... | collective-permute-start | bytes 98312 | tf_op jit(solution)/shard_map/ppermute | solution.py:348
  98.2 8.0 %collective-permute-start.9 = (bf16[64,256]{1,0:T(8,128)(2,1)S(1)}, bf16[64,256]{1,0:T(8,128)(2,1)S(1)}, u32[]{:S(2)}, u32[]{:S(2)}) collective-permute-start(bf16[64,256]{1,0:T(8,128)(2,1)S(1)} %get-tuple-element.15), channel_id=1, source_target_pairs={{0,1},{1,2},{2,3},{3,4},{4,5},{5,6},{6,7},{7,264},{8,9},{9,10},{10... | collective-permute-start | bytes 98312 | tf_op jit(solution)/shard_map/ppermute | solution.py:347
  106.2 18.4 %copy-start.3 = (bf16[2,256,128]{2,1,0:T(8,128)(2,1)S(1)}, bf16[2,256,128]{2,1,0:T(8,128)(2,1)}, u32[]{:S(2)}) copy-start(bf16[2,256,128]{2,1,0:T(8,128)(2,1)} %weight.3) | copy-start | bytes 393220

commit v2 on v1

--- a/solution.py
+++ b/solution.py
@@ -13,7 +13,6 @@
 F32 = jnp.float32
 BF16 = jnp.bfloat16
 GROUP = ("y", "core")
-RING = ("zh", "zl")
 EXTRA = 16
 
 
@@ -45,9 +44,10 @@
     return full.T
 
 
-def embed_kernel(patches, weight, chan, query, out):
+def embed_kernel(patches, weight, chan, query, *outs):
     tokens = patches.shape[1]
-    own = tokens // out.shape[0]
+    owners = 2 * outs[0].shape[0]
+    own = tokens // owners
     q = query[...]
     parts = in_rows(thirds(q), 16).astype(BF16)
     scale = q.shape[1] ** (-0.5)
@@ -65,15 +65,16 @@
     extra = in_rows(thirds(top) + thirds(total), EXTRA).astype(BF16)
     chan0 = chan[0:1, :].astype(F32)
     chan1 = chan[1:2, :].astype(F32)
-    for j in range(out.shape[0]):
+    for j in range(owners):
         lo, hi = j * own, (j + 1) * own
         e0 = dot_nn(patches[0, lo:hi, :], weight[0]) + chan0
         e1 = dot_nn(patches[1, lo:hi, :], weight[1]) + chan1
         w = jnp.broadcast_to(share[:, lo:hi], (own, own)).T
         w = jnp.concatenate([w, w], axis=1)
-        out[j, :own, :] = (e1 + w * (e0 - e1)).astype(BF16)
-        out[j, own:, :own] = extra[:, lo:hi]
-        out[j, own:, own:] = jnp.zeros((EXTRA, out.shape[2] - own), BF16)
+        out = outs[j % 2]
+        out[j // 2, :own, :] = (e1 + w * (e0 - e1)).astype(BF16)
+        out[j // 2, own:, :own] = extra[:, lo:hi]
+        out[j // 2, own:, own:] = jnp.zeros((EXTRA, out.shape[2] - own), BF16)
 
 
 def top_and_total(block):
@@ -93,17 +94,33 @@
     return out, top, total
 
 
-def combine_kernel(got, sent, own, own_rows):
-    count = got.shape[0]
-    n = own.shape[0]
-    stats = [top_and_total(got[d, n:, :n]) for d in range(count)]
-    averages = [got[d, :n, :].astype(F32) for d in range(count)]
-    state, top, total = merged(averages, [s[0] for s in stats], [s[1] for s in stats])
+def put_message(out, state, top, total):
+    n = state.shape[0]
+    out[:n, :] = state.astype(BF16)
+    out[n:, :n] = in_rows(thirds(top) + thirds(total), EXTRA).astype(BF16)
+    out[n:, n:] = jnp.zeros((EXTRA, out.shape[1] - n), BF16)
+
+
+def merge_messages(messages):
+    n = messages[0].shape[0] - EXTRA
+    stats = [top_and_total(m[n:, :n]) for m in messages]
+    averages = [m[:n, :].astype(F32) for m in messages]
+    return merged(averages, [s[0] for s in stats], [s[1] for s in stats])
+
+
+def pair_kernel(first, second, got, *outs):
+    core, y = lax.axis_index("core"), lax.axis_index("y")
+    for k, out in enumerate(outs):
+        to = (y + k) & 3
+        mine = jnp.where(core == 0, first[to].astype(F32), second[to].astype(F32))
+        put_message(out, *merge_messages([mine, got[to]]))
+
+
+def combine_kernel(mine, one, two, three, sent, own, own_rows):
+    state, top, total = merge_messages([m[...] for m in (mine, one, two, three)])
     own[...] = state
     own_rows[...] = in_rows([top, total], 8)
-    sent[:n, :] = state.astype(BF16)
-    sent[n:, :n] = in_rows(thirds(top) + thirds(total), EXTRA).astype(BF16)
-    sent[n:, n:] = jnp.zeros((EXTRA, sent.shape[1] - n), BF16)
+    put_message(sent, state, top, total)
 
 
 def norm(v, gain):
@@ -114,21 +131,15 @@
 
 
 def attention_weights(layer, mine, other, qkv_rows, proj_rows):
+    lo = 48 * layer
     first_core = lax.axis_index("core") == 0
-    x_at, zl_at = lax.axis_index("x"), lax.axis_index("zl")
-    lo = 48 * layer
-    for xs in range(4):
-        for slot, back in enumerate(ZL_BACK):
-            lon = ((x_at + (4 - xs)) & 3) * 8 + ((zl_at + (16 - back)) & 7)
-            piece = xs * 8 + slot
-            a = mine[piece, lo : lo + 16, :].astype(F32)
-            b = other[piece, lo : lo + 16, :].astype(F32)
-            head = jnp.where(first_core, a, b)
-            tail = jnp.where(first_core, b, a)
-            at = pl.multiple_of(lon * 24, 8)
-            qkv_rows[pl.ds(at, 16), :] = head
-            qkv_rows[pl.ds(at + 16, 8), :] = tail[:8]
-            proj_rows[pl.ds(pl.multiple_of(lon * 8, 8), 8), :] = tail[8:]
+    for lon in range(mine.shape[0]):
+        a = mine[lon, lo : lo + 16, :].astype(F32)
+        b = other[lon, lo : lo + 16, :].astype(F32)
+        tail = jnp.where(first_core, b, a)
+        qkv_rows[lon * 24 : lon * 24 + 16, :] = jnp.where(first_core, a, b)
+        qkv_rows[lon * 24 + 16 : lon * 24 + 24, :] = tail[:8]
+        proj_rows[lon * 8 : lon * 8 + 8, :] = tail[8:]
     return qkv_rows[...].astype(BF16), proj_rows[...].astype(BF16)
 
 
@@ -241,28 +252,70 @@
             out[c, j * own : (j + 1) * own, :] = dot_nn(tokens[j], w).astype(BF16)
 
 
-def on_core(kernel, outs, scratch=(), flops=0, moved=0):
-    vmem = pl.BlockSpec(memory_space=pltpu.VMEM)
+def spread_kernel(count, times, *refs):
+    parts, outs = refs[:count], refs[-len(times) :]
+    height = outs[0].shape[-2]
+    at = 0
+    for part in parts:
+        n = part.shape[0]
+        for layer, (out, repeat) in enumerate(zip(outs, times)):
+            rows = part[:, layer * height : (layer + 1) * height, :]
+            for k in range(repeat):
+                out[k, at : at + n] = rows
+        at += n
+
+
+def spread(parts, times, after=()):
+    pieces, height, width = parts[0].shape
+    total = sum(p.shape[0] for p in parts)
+    vmem, anywhere = pl.BlockSpec(memory_space=pltpu.VMEM), pl.BlockSpec(memory_space=pl.ANY)
+    return pl.pallas_call(
+        functools.partial(spread_kernel, len(parts), times),
+        out_shape=[
+            jax.ShapeDtypeStruct((n, total, height // len(times), width), BF16) for n in times
+        ],
+        in_specs=[vmem] * len(parts) + [anywhere] * len(after),
+        out_specs=[vmem] * len(times),
+        compiler_params=pltpu.CompilerParams(vmem_limit_bytes=16 * 2**20),
+        cost_estimate=pl.CostEstimate(
+            flops=0, bytes_accessed=2 * (1 + sum(times)) * total * height * width, transcendentals=0
+        ),
+    )(*parts, *after)
+
+
+def held_until(value, after):
+    anywhere = pl.BlockSpec(memory_space=pl.ANY)
+    return pl.pallas_call(
+        lambda *refs: None,
+        out_shape=jax.ShapeDtypeStruct(value.shape, value.dtype),
+        in_specs=[anywhere] * (1 + len(after)),
+        out_specs=anywhere,
+        input_output_aliases={0: 0},
+    )(value, *after)
+
+
+def on_core(kernel, outs, scratch=(), flops=0, moved=0, after=()):
+    vmem, anywhere = pl.BlockSpec(memory_space=pltpu.VMEM), pl.BlockSpec(memory_space=pl.ANY)
+
+    def ordered(*refs):
+        kernel(*refs[len(after) :])
 
     def call(*operands):
         return pl.pallas_call(
-            kernel,
+            ordered,
             out_shape=outs,
-            in_specs=[vmem] * len(operands),
+            in_specs=[anywhere] * len(after) + [vmem] * len(operands),
             out_specs=jax.tree.map(lambda _: vmem, outs),
             scratch_shapes=list(scratch),
             compiler_params=pltpu.CompilerParams(vmem_limit_bytes=40 * 2**20),
             cost_estimate=pl.CostEstimate(flops=flops, bytes_accessed=moved, transcendentals=0),
-        )(*operands)
+        )(*after, *operands)
 
     return call
 
 
 def shifted(value, axes, size, steps):
     return lax.ppermute(value, axes, [(i, (i + steps) % size) for i in range(size)])
-
-
-ZL_BACK = (0, 2, -2, 4, 1, 3, -1, 5)
 
 
 def eastward():
@@ -303,16 +356,14 @@
     own = tokens // parts
 
     piece = weight_pieces(qkv_weight, proj_weight, up_weight, down_weight)
-    pieces = jnp.concatenate(
-        [piece] + [shifted(piece, RING, 16, k) for k in (2, -2, 4)], axis=0
-    )
-    pieces = jnp.concatenate([pieces, shifted(pieces, RING, 16, 1)], axis=0)
-    mine = jnp.concatenate([pieces] + [shifted(pieces, "x", 4, k) for k in (1, 2, 3)], axis=0)
-    other = shifted(mine, "core", 2, 1)
-
-    sums = on_core(
+    (near,) = spread([piece], (8,))
+    near = lax.all_to_all(near.reshape(8, -1, width), "zl", 0, 0, tiled=True)
+
+    message = jax.ShapeDtypeStruct((own + EXTRA, width), BF16)
+    messages = jax.ShapeDtypeStruct((4, own + EXTRA, width), BF16)
+    first, second = on_core(
         embed_kernel,
-        jax.ShapeDtypeStruct((parts, own + EXTRA, width), BF16),
+        (messages, messages),
         flops=2 * chans * tokens * width_p * width,
         moved=2 * 2**20,
     )(
@@ -321,17 +372,24 @@
         channel_embed,
         agg_query.reshape(1, width),
     )
-    got = lax.all_to_all(sums, GROUP, 0, 0, tiled=True)
+    leaving = jnp.where(lax.axis_index("core") == 0, second, first)
+    got = shifted(leaving, "core", 2, 1)
+    paired = on_core(pair_kernel, (message,) * 4, moved=2**20)(first, second, got)
+    along = [shifted(paired[k], "y", 4, k) for k in (1, 2, 3)]
     sent, average, stats = on_core(
         combine_kernel,
         (
-            jax.ShapeDtypeStruct((own + EXTRA, width), BF16),
+            message,
             jax.ShapeDtypeStruct((own, width), F32),
             jax.ShapeDtypeStruct((8, own), F32),
         ),
         moved=2**20,
-    )(got)
+    )(paired[0], *along)
+    (copies,) = spread([near], (4,), after=(sent,))
+    mine = lax.all_to_all(copies, "x", 0, 0, tiled=True).reshape(32, -1, width)
     partner = shifted(sent, "zh", 2, 1)
+    mine = held_until(mine, (partner,))
+    other = shifted(mine, "core", 2, 1)
 
     scratch = [pltpu.VMEM((3 * width, width), F32), pltpu.VMEM((width, width), F32)]
     half = jax.ShapeDtypeStruct((own // 2, width), BF16)

time: 126 us -> 106 us (0.84)
  blocking collectives: 29.9 us -> 14.3 us
  waiting for transfers between devices: 29.8 us -> 17.4 us
  local copies, waits for them, and re-layouts: 0.94 us -> 6.5 us
  Pallas kernels: 8.14 us -> 10.5 us
    ppermute x9 -> x6, starting transfers between devices: 48.2 us -> 27.7 us  [shifted(): lax.ppermute(value, axes, [(i, (i + steps) % size) for i in range(size)])]
    all_to_all x0 -> x2, starting transfers between devices: none -> 17.1 us  [the longest x1 13.1 us: body(): near = lax.all_to_all(near.reshape(8, -1, width), 'zl', 0, 0, tiled=True)]
    all_to_all x1 -> x0, blocking collectives: 14.7 us -> none  [body(): got = lax.all_to_all(sums, GROUP, 0, 0, tiled=True)]
    ppermute x9 -> x6, waiting for transfers between devices: 23.8 us -> 12.8 us  [shifted(): lax.ppermute(value, axes, [(i, (i + steps) % size) for i in range(size)])]
    ppermute x1, waiting for transfers between devices: 6.04 us -> 0.01 us  [body(): from_west = lax.ppermute(east, ('zh', 'x', 'zl'), pairs)]
    unnamed x20 -> x22, local copies, waits for them, and re-layouts: 0.88 us -> 6.49 us
    all_to_all x0 -> x2, waiting for transfers between devices: none -> 3.57 us  [the longest x1 3.57 us: body(): mine = lax.all_to_all(copies, 'x', 0, 0, tiled=True).reshape(32, -1, width)]
    pallas_call x5 -> x9, Pallas kernels: 8.14 us -> 10.5 us  [the longest x6 8.48 us: call(): pl.pallas_call(ordered, out_shape=outs, in_specs=[anywhere] * len(after)...]
  transfers between devices with their start and end apart: 11 -> 10, of which waited for: 6 -> 6; matrix products, arithmetic and copies ran while one was open for 0% -> 0% of each run, Pallas kernels for 1% -> 2%
where the time goes in v2:
time: 106 us; the launch traced here: 105 us
  starting transfers between devices  55.5 us (52%)
  waiting for transfers between devices  17.4 us (16%)
  blocking collectives  14.3 us (13%)
  Pallas kernels  10.5 us (10%)
  local copies, waits for them, and re-layouts  6.5 us (6%)
    ppermute x6, starting transfers between devices, shifted(): lax.ppermute(value, axes, [(i, (i + steps) % size) for i in range(size)])  27.7 us
    all_to_all x1, blocking collectives, body(): everyone = lax.all_to_all(final, GROUP, 0, 0, tiled=True)  14.3 us
    all_to_all x1, starting transfers between devices, body(): near = lax.all_to_all(near.reshape(8, -1, width), 'zl', 0, 0, tiled=True)  13.1 us
    ppermute x6, waiting for transfers between devices, shifted(): lax.ppermute(value, axes, [(i, (i + steps) % size) for i in range(size)])  12.8 us
    pallas_call x6, Pallas kernels, call(): pl.pallas_call(ordered, out_shape=outs, in_specs=[anywhere] * len(after)...  8.48 us
    ppermute x1, starting transfers between devices, body(): lax.ppermute(west, ('zh', 'x', 'zl'), [(b, a) for a, b in pairs])  7.08 us
    unnamed x22, local copies, waits for them, and re-layouts  6.49 us
    all_to_all x1, starting transfers between devices, body(): mine = lax.all_to_all(copies, 'x', 0, 0, tiled=True).reshape(32, -1, width)  4.01 us
  transfers between devices with their start and end apart: 10, of which 6 were waited for; matrix products, arithmetic and copies ran while one was open for 0% of the time, Pallas kernels for 2%

profile of v2, /device:TPU:1, one launch (start us, length us, event | category | flops | bytes accessed | tf_op | source)
XLA Modules:
  0.0 105.1 jit_solution(7849091398616042941)
XLA Ops:
  0.0 0.8 copy-done
  0.8 0.8 fusion
  1.5 0.8 shard_map.103
  2.3 13.1 %all-to-all-start = ((bf16[8,96,256]{2,1,0:T(8,128)(2,1)}), bf16[8,96,256]{2,1,0:T(8,128)(2,1)S(1)}, u32[]{:S(2)}, u32[]{:S(2)}) async-start(bf16[8,96,256]{2,1,0:T(8,128)(2,1)} %bitcast.5), calls=%async_computation | async-start | bytes 786432 | tf_op jit(solution)/shard_map/all_to_all | solution.py:360
  15.4 0.9 copy-done.6
  16.3 0.7 copy-done.9
  17.0 0.7 copy-done.10
  17.7 0.8 shard_map.100
  18.6 2.9 %collective-permute-start = (bf16[4,144,256]{2,1,0:T(8,128)(2,1)S(1)}, bf16[4,144,256]{2,1,0:T(8,128)(2,1)S(1)}, u32[]{:S(2)}, u32[]{:S(2)}) collective-permute-start(bf16[4,144,256]{2,1,0:T(8,128)(2,1)S(1)} %broadcast_select_fusion), channel_id=1, source_target_pairs={{0,32},{32,0},{1,33},{33,1},{2,34},{34,2},{3,35},{35,3},{4,36},{36... | collective-permute-start | bytes 884744 | tf_op jit(solution)/shard_map/ppermute | solution.py:318
  21.4 1.2 %collective-permute-done.refs_2_ = bf16[4,144,256]{2,1,0:T(8,128)(2,1)S(1)} collective-permute-done((bf16[4,144,256]{2,1,0:T(8,128)(2,1)S(1)}, bf16[4,144,256]{2,1,0:T(8,128)(2,1)S(1)}, u32[]{:S(2)}, u32[]{:S(2)}) %collective-permute-start) | collective-permute-done | bytes 294944 | tf_op jit(solution)/shard_map/ppermute | solution.py:318
  22.6 0.5 shard_map.101
  23.1 3.2 %collective-permute-start.1 = (bf16[144,256]{1,0:T(8,128)(2,1)S(1)}, bf16[144,256]{1,0:T(8,128)(2,1)S(1)}, u32[]{:S(2)}, u32[]{:S(2)}) collective-permute-start(bf16[144,256]{1,0:T(8,128)(2,1)S(1)} %get-tuple-element.20), channel_id=1, source_target_pairs={{0,64},{64,128},{128,192},{192,0},{1,65},{65,129},{129,193},{193,1... | collective-permute-start | bytes 221192 | tf_op jit(solution)/shard_map/ppermute | solution.py:318
  26.3 4.5 %collective-permute-start.2 = (bf16[144,256]{1,0:T(8,128)(2,1)S(1)}, bf16[144,256]{1,0:T(8,128)(2,1)S(1)}, u32[]{:S(2)}, u32[]{:S(2)}) collective-permute-start(bf16[144,256]{1,0:T(8,128)(2,1)S(1)} %get-tuple-element.21), channel_id=1, source_target_pairs={{0,128},{64,192},{128,0},{192,64},{1,129},{65,193},{129,1},{193,65... | collective-permute-start | bytes 221192 | tf_op jit(solution)/shard_map/ppermute | solution.py:318
  30.8 3.0 %collective-permute-start.3 = (bf16[144,256]{1,0:T(8,128)(2,1)S(1)}, bf16[144,256]{1,0:T(8,128)(2,1)S(1)}, u32[]{:S(2)}, u32[]{:S(2)}) collective-permute-start(bf16[144,256]{1,0:T(8,128)(2,1)S(1)} %get-tuple-element.22), channel_id=1, source_target_pairs={{0,192},{64,0},{128,64},{192,128},{1,193},{65,1},{129,65},{193,129... | collective-permute-start | bytes 221192 | tf_op jit(solution)/shard_map/ppermute | solution.py:318
  33.8 2.4 %collective-permute-done.3.refs_3_ = bf16[144,256]{1,0:T(8,128)(2,1)S(1)} collective-permute-done((bf16[144,256]{1,0:T(8,128)(2,1)S(1)}, bf16[144,256]{1,0:T(8,128)(2,1)S(1)}, u32[]{:S(2)}, u32[]{:S(2)}) %collective-permute-start.3) | collective-permute-done | bytes 73760 | tf_op jit(solution)/shard_map/ppermute | solution.py:318
  36.5 1.3 %shard_map.104 = bf16[4,8,96,256]{3,2,1,0:T(8,128)(2,1)} custom-call(bf16[8,96,256]{2,1,0:T(8,128)(2,1)S(1)} %all-to-all-done.refs_0_, bf16[144,256]{1,0:T(8,128)(2,1)S(1)} %get-tuple-element.25.refs_1_), custom_call_target="tpu_custom_call" | custom-call | bytes 1966080 | tf_op jit(solution)/shard_map/pallas_call | solution.py:272
  37.8 4.0 %all-to-all-start.1 = ((bf16[4,8,96,256]{3,2,1,0:T(8,128)(2,1)}), bf16[4,8,96,256]{3,2,1,0:T(8,128)(2,1)S(1)}, u32[]{:S(2)}, u32[]{:S(2)}) async-start(bf16[4,8,96,256]{3,2,1,0:T(8,128)(2,1)} %shard_map.104), calls=%async_computation.1 | async-start | bytes 3145728 | tf_op jit(solution)/shard_map/all_to_all | solution.py:389
  41.8 7.9 %collective-permute-start.4 = (bf16[144,256]{1,0:T(8,128)(2,1)S(1)}, bf16[144,256]{1,0:T(8,128)(2,1)S(1)}, u32[]{:S(2)}, u32[]{:S(2)}) collective-permute-start(bf16[144,256]{1,0:T(8,128)(2,1)S(1)} %get-tuple-element.25.refs_1_), channel_id=1, source_target_pairs={{0,256},{256,0},{1,257},{257,1},{2,258},{258,2},{3,259},{259,3},{4... | collective-permute-start | bytes 221192 | tf_op jit(solution)/shard_map/ppermute | solution.py:318
  49.8 6.0 %collective-permute-done.4.refs_1_.refs_2_ = bf16[144,256]{1,0:T(8,128)(2,1)S(1)} collective-permute-done((bf16[144,256]{1,0:T(8,128)(2,1)S(1)}, bf16[144,256]{1,0:T(8,128)(2,1)S(1)}, u32[]{:S(2)}, u32[]{:S(2)}) %collective-permute-start.4) | collective-permute-done | bytes 73760 | tf_op jit(solution)/shard_map/ppermute | solution.py:318
  55.8 3.6 %all-to-all-done.1 = bf16[4,8,96,256]{3,2,1,0:T(8,128)(2,1)S(1)} async-done(((bf16[4,8,96,256]{3,2,1,0:T(8,128)(2,1)}), bf16[4,8,96,256]{3,2,1,0:T(8,128)(2,1)S(1)}, u32[]{:S(2)}, u32[]{:S(2)}) %all-to-all-start.1) | async-done | bytes 1572896 | tf_op jit(solution)/shard_map/all_to_all | solution.py:389
  59.4 1.2 %copy-done.1 = bf16[4,8,96,256]{3,2,1,0:T(8,128)(2,1)} copy-done((bf16[4,8,96,256]{3,2,1,0:T(8,128)(2,1)}, bf16[4,8,96,256]{3,2,1,0:T(8,128)(2,1)S(1)}, u32[]{:S(2)}) %copy-start.1) | copy-done | bytes 1572888
  60.5 6.2 %collective-permute-start.5 = (bf16[32,96,256]{2,1,0:T(8,128)(2,1)}, bf16[32,96,256]{2,1,0:T(8,128)(2,1)S(1)}, u32[]{:S(2)}, u32[]{:S(2)}) collective-permute-start(bf16[32,96,256]{2,1,0:T(8,128)(2,1)} %shard_map.105.refs_4_), channel_id=1, source_target_pairs={{0,32},{32,0},{1,33},{33,1},{2,34},{34,2},{3,35},{35,3},{4,36},{36... | collective-permute-start | bytes 4718600 | tf_op jit(solution)/shard_map/ppermute | solution.py:318
  66.7 3.2 %collective-permute-done.5.refs_5_ = bf16[32,96,256]{2,1,0:T(8,128)(2,1)S(1)} collective-permute-done((bf16[32,96,256]{2,1,0:T(8,128)(2,1)}, bf16[32,96,256]{2,1,0:T(8,128)(2,1)S(1)}, u32[]{:S(2)}, u32[]{:S(2)}) %collective-permute-start.5) | collective-permute-done | bytes 1572896 | tf_op jit(solution)/shard_map/ppermute | solution.py:318
  69.9 1.4 %copy-done.2 = bf16[32,96,256]{2,1,0:T(8,128)(2,1)S(1)} copy-done((bf16[32,96,256]{2,1,0:T(8,128)(2,1)S(1)}, bf16[32,96,256]{2,1,0:T(8,128)(2,1)}, u32[]{:S(2)}) %copy-start.2) | copy-done | bytes 1572888
  71.3 0.9 copy-done.5
  72.2 2.4 %shard_map.106 = (f32[128,256]{1,0:T(8,128)S(1)}, bf16[64,256]{1,0:T(8,128)(2,1)S(1)}, bf16[64,256]{1,0:T(8,128)(2,1)S(1)}) custom-call(f32[128,256]{1,0:T(8,128)S(1)} %get-tuple-element.23.refs_0_, f32[8,128]{1,0:T(8,128)S(1)} %get-tuple-element.24.refs_1_, bf16[144,256]{1,0:T(8,128)(2,1)S(1)} %copy-done.5, f32[5,256]{1,0:T(8,128)S(1)} %copy-done.8, ...), custom_call_target="tpu_custom_call" | custom-call | flops 201326592 | bytes 4194304 | tf_op jit(solution)/shard_map/pallas_call | solution.py:304
  74.7 3.6 %collective-permute-start.6 = (bf16[64,256]{1,0:T(8,128)(2,1)S(1)}, bf16[64,256]{1,0:T(8,128)(2,1)S(1)}, u32[]{:S(2)}, u32[]{:S(2)}) collective-permute-start(bf16[64,256]{1,0:T(8,128)(2,1)S(1)} %get-tuple-element.27), channel_id=1, source_target_pairs={{0,1},{1,2},{2,3},{3,4},{4,5},{5,6},{6,7},{7,264},{8,9},{9,10},{10... | collective-permute-start | bytes 98312 | tf_op jit(solution)/shard_map/ppermute | solution.py:405
  78.3 7.1 %collective-permute-start.7 = (bf16[64,256]{1,0:T(8,128)(2,1)S(1)}, bf16[64,256]{1,0:T(8,128)(2,1)S(1)}, u32[]{:S(2)}, u32[]{:S(2)}) collective-permute-start(bf16[64,256]{1,0:T(8,128)(2,1)S(1)} %get-tuple-element.28), channel_id=1, source_target_pairs={{1,0},{2,1},{3,2},{4,3},{5,4},{6,5},{7,6},{264,7},{9,8},{10,9},{11... | collective-permute-start | bytes 98312 | tf_op jit(solution)/shard_map/ppermute | solution.py:406
  85.4 1.0 collective-permute-done.7.refs_2_
  86.4 3.2 %shard_map.107 = bf16[8,128,256]{2,1,0:T(8,128)(2,1)S(1)} custom-call(f32[128,256]{1,0:T(8,128)S(1)} %get-tuple-element.26.refs_0_, bf16[64,256]{1,0:T(8,128)(2,1)S(1)} %collective-permute-done.6.refs_1_, bf16[64,256]{1,0:T(8,128)(2,1)S(1)} %collective-permute-done.7.refs_2_, f32[5,256]{1,0:T(8,128)S(1)} %copy-done.8, bf16[32,96,256]{2,1,0:T(8,128)(2,1)S(1)} %copy-done.2, ...), custom_call_target="tpu_custom_call" | custom-call | flops 201326592 | bytes 4194304 | tf_op jit(solution)/shard_map/pallas_call | solution.py:304
  89.7 14.3 %all_to_all.15.refs_0_ = bf16[8,128,256]{2,1,0:T(8,128)(2,1)S(1)} all-to-all(bf16[8,128,256]{2,1,0:T(8,128)(2,1)S(1)} %shard_map.107), channel_id=1, replica_groups=mesh['zh'=2,'y'=4,'core'=2,'x'=4,'zl'=8] {'y','core'}, dimensions={0} | all-to-all | bytes 1048576 | tf_op jit(solution)/shard_map/all_to_all | solution.py:414
  103.9 1.2 %shard_map.108 = bf16[2,1024,128]{2,1,0:T(8,128)(2,1)} custom-call(bf16[8,128,256]{2,1,0:T(8,128)(2,1)S(1)} %all_to_all.15.refs_0_, bf16[2,256,128]{2,1,0:T(8,128)(2,1)S(1)} %copy-done.7), custom_call_target="tpu_custom_call" | custom-call | flops 134217728 | bytes 2097152 | tf_op jit(solution)/shard_map/pallas_call | solution.py:304
  (24 shorter events, 0.4 us)
Async XLA Ops:
  0.0 0.8 copy-start
  0.0 15.4 %copy-start.3 = (bf16[2,128,8,128]{3,2,1,0:T(8,128)(2,1)S(1)}, bf16[2,128,8,128]{3,2,1,0:T(8,128)(2,1)}, u32[]{:S(2)}) copy-start(bf16[2,128,8,128]{3,2,1,0:T(8,128)(2,1)} %param.10) | copy-start | bytes 1572868
  2.3 34.2 %all-to-all-start = ((bf16[8,96,256]{2,1,0:T(8,128)(2,1)}), bf16[8,96,256]{2,1,0:T(8,128)(2,1)S(1)}, u32[]{:S(2)}, u32[]{:S(2)}) async-start(bf16[8,96,256]{2,1,0:T(8,128)(2,1)} %bitcast.5), calls=%async_computation | async-start | bytes 786432 | tf_op jit(solution)/shard_map/all_to_all | solution.py:360
  15.4 0.9 copy-start.6
  16.3 0.7 copy-start.9
  17.0 0.7 copy-start.10
  18.6 4.1 %collective-permute-start = (bf16[4,144,256]{2,1,0:T(8,128)(2,1)S(1)}, bf16[4,144,256]{2,1,0:T(8,128)(2,1)S(1)}, u32[]{:S(2)}, u32[]{:S(2)}) collective-permute-start(bf16[4,144,256]{2,1,0:T(8,128)(2,1)S(1)} %broadcast_select_fusion), channel_id=1, source_target_pairs={{0,32},{32,0},{1,33},{33,1},{2,34},{34,2},{3,35},{35,3},{4,36},{36... | collective-permute-start | bytes 884744 | tf_op jit(solution)/shard_map/ppermute | solution.py:318
  23.1 10.7 %collective-permute-start.1 = (bf16[144,256]{1,0:T(8,128)(2,1)S(1)}, bf16[144,256]{1,0:T(8,128)(2,1)S(1)}, u32[]{:S(2)}, u32[]{:S(2)}) collective-permute-start(bf16[144,256]{1,0:T(8,128)(2,1)S(1)} %get-tuple-element.20), channel_id=1, source_target_pairs={{0,64},{64,128},{128,192},{192,0},{1,65},{65,129},{129,193},{193,1... | collective-permute-start | bytes 221192 | tf_op jit(solution)/shard_map/ppermute | solution.py:318
  26.3 7.5 %collective-permute-start.2 = (bf16[144,256]{1,0:T(8,128)(2,1)S(1)}, bf16[144,256]{1,0:T(8,128)(2,1)S(1)}, u32[]{:S(2)}, u32[]{:S(2)}) collective-permute-start(bf16[144,256]{1,0:T(8,128)(2,1)S(1)} %get-tuple-element.21), channel_id=1, source_target_pairs={{0,128},{64,192},{128,0},{192,64},{1,129},{65,193},{129,1},{193,65... | collective-permute-start | bytes 221192 | tf_op jit(solution)/shard_map/ppermute | solution.py:318
  30.8 5.4 %collective-permute-start.3 = (bf16[144,256]{1,0:T(8,128)(2,1)S(1)}, bf16[144,256]{1,0:T(8,128)(2,1)S(1)}, u32[]{:S(2)}, u32[]{:S(2)}) collective-permute-start(bf16[144,256]{1,0:T(8,128)(2,1)S(1)} %get-tuple-element.22), channel_id=1, source_target_pairs={{0,192},{64,0},{128,64},{192,128},{1,193},{65,1},{129,65},{193,129... | collective-permute-start | bytes 221192 | tf_op jit(solution)/shard_map/ppermute | solution.py:318
  37.8 21.6 %all-to-all-start.1 = ((bf16[4,8,96,256]{3,2,1,0:T(8,128)(2,1)}), bf16[4,8,96,256]{3,2,1,0:T(8,128)(2,1)S(1)}, u32[]{:S(2)}, u32[]{:S(2)}) async-start(bf16[4,8,96,256]{3,2,1,0:T(8,128)(2,1)} %shard_map.104), calls=%async_computation.1 | async-start | bytes 3145728 | tf_op jit(solution)/shard_map/all_to_all | solution.py:389
  41.8 14.0 %collective-permute-start.4 = (bf16[144,256]{1,0:T(8,128)(2,1)S(1)}, bf16[144,256]{1,0:T(8,128)(2,1)S(1)}, u32[]{:S(2)}, u32[]{:S(2)}) collective-permute-start(bf16[144,256]{1,0:T(8,128)(2,1)S(1)} %get-tuple-element.25.refs_1_), channel_id=1, source_target_pairs={{0,256},{256,0},{1,257},{257,1},{2,258},{258,2},{3,259},{259,3},{4... | collective-permute-start | bytes 221192 | tf_op jit(solution)/shard_map/ppermute | solution.py:318
  55.8 3.6 %copy-start.4 = (bf16[144,256]{1,0:T(8,128)(2,1)}, bf16[144,256]{1,0:T(8,128)(2,1)S(1)}, u32[]{:S(2)}) copy-start(bf16[144,256]{1,0:T(8,128)(2,1)S(1)} %collective-permute-done.4.refs_1_.refs_2_) | copy-start | bytes 221188
  59.4 1.2 %copy-start.1 = (bf16[4,8,96,256]{3,2,1,0:T(8,128)(2,1)}, bf16[4,8,96,256]{3,2,1,0:T(8,128)(2,1)S(1)}, u32[]{:S(2)}) copy-start(bf16[4,8,96,256]{3,2,1,0:T(8,128)(2,1)S(1)} %all-to-all-done.1) | copy-start | bytes 4718596
  60.5 9.4 %copy-start.8 = (f32[5,256]{1,0:T(8,128)S(1)}, f32[5,256]{1,0:T(8,128)}, u32[]{:S(2)}) copy-start(f32[5,256]{1,0:T(8,128)} %refs_3_.3) | copy-start | bytes 15364
  60.5 9.4 %collective-permute-start.5 = (bf16[32,96,256]{2,1,0:T(8,128)(2,1)}, bf16[32,96,256]{2,1,0:T(8,128)(2,1)S(1)}, u32[]{:S(2)}, u32[]{:S(2)}) collective-permute-start(bf16[32,96,256]{2,1,0:T(8,128)(2,1)} %shard_map.105.refs_4_), channel_id=1, source_target_pairs={{0,32},{32,0},{1,33},{33,1},{2,34},{34,2},{3,35},{35,3},{4,36},{36... | collective-permute-start | bytes 4718600 | tf_op jit(solution)/shard_map/ppermute | solution.py:318
  69.9 1.4 %copy-start.2 = (bf16[32,96,256]{2,1,0:T(8,128)(2,1)S(1)}, bf16[32,96,256]{2,1,0:T(8,128)(2,1)}, u32[]{:S(2)}) copy-start(bf16[32,96,256]{2,1,0:T(8,128)(2,1)} %shard_map.105.refs_4_) | copy-start | bytes 4718596
  71.3 0.9 copy-start.5
  74.7 10.7 %collective-permute-start.6 = (bf16[64,256]{1,0:T(8,128)(2,1)S(1)}, bf16[64,256]{1,0:T(8,128)(2,1)S(1)}, u32[]{:S(2)}, u32[]{:S(2)}) collective-permute-start(bf16[64,256]{1,0:T(8,128)(2,1)S(1)} %get-tuple-element.27), channel_id=1, source_target_pairs={{0,1},{1,2},{2,3},{3,4},{4,5},{5,6},{6,7},{7,264},{8,9},{9,10},{10... | collective-permute-start | bytes 98312 | tf_op jit(solution)/shard_map/ppermute | solution.py:405
  78.3 8.1 %collective-permute-start.7 = (bf16[64,256]{1,0:T(8,128)(2,1)S(1)}, bf16[64,256]{1,0:T(8,128)(2,1)S(1)}, u32[]{:S(2)}, u32[]{:S(2)}) collective-permute-start(bf16[64,256]{1,0:T(8,128)(2,1)S(1)} %get-tuple-element.28), channel_id=1, source_target_pairs={{1,0},{2,1},{3,2},{4,3},{5,4},{6,5},{7,6},{264,7},{9,8},{10,9},{11... | collective-permute-start | bytes 98312 | tf_op jit(solution)/shard_map/ppermute | solution.py:406
  86.4 17.5 %copy-start.7 = (bf16[2,256,128]{2,1,0:T(8,128)(2,1)S(1)}, bf16[2,256,128]{2,1,0:T(8,128)(2,1)}, u32[]{:S(2)}) copy-start(bf16[2,256,128]{2,1,0:T(8,128)(2,1)} %refs_1_.3) | copy-start | bytes 393220

commit v3 on v2

--- a/solution.py
+++ b/solution.py
@@ -44,37 +44,39 @@
     return full.T
 
 
-def embed_kernel(patches, weight, chan, query, *outs):
-    tokens = patches.shape[1]
-    owners = 2 * outs[0].shape[0]
-    own = tokens // owners
-    q = query[...]
+def embed_kernel(table, patches, stay, leave, shares, extras):
+    depth = patches.shape[2]
+    weight = [table[c * depth : (c + 1) * depth, :].astype(BF16) for c in range(2)]
+    chan = table[2 * depth : 2 * depth + 8, :]
+    owners = 2 * stay.shape[0]
+    own = patches.shape[1] // owners
+    q = chan[2:3, :]
     parts = in_rows(thirds(q), 16).astype(BF16)
     scale = q.shape[1] ** (-0.5)
     scores = []
     for c in range(2):
         proj = jnp.sum(dot_nt(parts, weight[c]), axis=0, keepdims=True)
-        bias = jnp.sum(chan[c : c + 1, :].astype(F32) * q, axis=1, keepdims=True)
+        bias = jnp.sum(chan[c : c + 1, :] * q, axis=1, keepdims=True)
         split = in_rows(thirds(proj), 16).astype(BF16)
         terms = dot_nt(split, patches[c])
         scores.append((jnp.sum(terms, axis=0, keepdims=True) + bias) * scale)
     top = jnp.maximum(scores[0], scores[1])
     first = jnp.exp(scores[0] - top)
     total = first + jnp.exp(scores[1] - top)
-    share = first / total
-    extra = in_rows(thirds(top) + thirds(total), EXTRA).astype(BF16)
-    chan0 = chan[0:1, :].astype(F32)
-    chan1 = chan[1:2, :].astype(F32)
-    for j in range(owners):
-        lo, hi = j * own, (j + 1) * own
-        e0 = dot_nn(patches[0, lo:hi, :], weight[0]) + chan0
-        e1 = dot_nn(patches[1, lo:hi, :], weight[1]) + chan1
-        w = jnp.broadcast_to(share[:, lo:hi], (own, own)).T
-        w = jnp.concatenate([w, w], axis=1)
-        out = outs[j % 2]
-        out[j // 2, :own, :] = (e1 + w * (e0 - e1)).astype(BF16)
-        out[j // 2, own:, :own] = extra[:, lo:hi]
-        out[j // 2, own:, own:] = jnp.zeros((EXTRA, out.shape[2] - own), BF16)
+    shares[...] = in_rows((first / total,), 8)
+    extras[...] = in_rows(thirds(top) + thirds(total), EXTRA)
+    chan0, chan1 = chan[0:1, :], chan[1:2, :]
+    core = lax.axis_index("core")
+    for side, out in enumerate((stay, leave)):
+        for y in range(out.shape[0]):
+            at = pl.multiple_of((2 * y + (core ^ side)) * own, own)
+            e0 = dot_nn(patches[0, pl.ds(at, own), :], weight[0]) + chan0
+            e1 = dot_nn(patches[1, pl.ds(at, own), :], weight[1]) + chan1
+            w = jnp.broadcast_to(shares[0:1, pl.ds(at, own)], (own, own)).T
+            w = jnp.concatenate([w, w], axis=1)
+            out[y, :own, :] = (e1 + w * (e0 - e1)).astype(BF16)
+            out[y, own:, :own] = extras[:, pl.ds(at, own)].astype(BF16)
+            out[y, own:, own:] = jnp.zeros((EXTRA, out.shape[2] - own), BF16)
 
 
 def top_and_total(block):
@@ -108,12 +110,11 @@
     return merged(averages, [s[0] for s in stats], [s[1] for s in stats])
 
 
-def pair_kernel(first, second, got, *outs):
-    core, y = lax.axis_index("core"), lax.axis_index("y")
+def pair_kernel(stay, got, *outs):
+    y = lax.axis_index("y")
     for k, out in enumerate(outs):
         to = (y + k) & 3
-        mine = jnp.where(core == 0, first[to].astype(F32), second[to].astype(F32))
-        put_message(out, *merge_messages([mine, got[to]]))
+        put_message(out, *merge_messages([stay[to], got[to]]))
 
 
 def combine_kernel(mine, one, two, three, sent, own, own_rows):
@@ -245,11 +246,13 @@
 
 
 def decode_kernel(tokens, weight, out):
-    count, own, width = tokens.shape
+    cores, chips, own, width = tokens.shape
     for c in range(2):
         w = weight[c]
-        for j in range(count):
-            out[c, j * own : (j + 1) * own, :] = dot_nn(tokens[j], w).astype(BF16)
+        for y in range(chips):
+            for core in range(cores):
+                at = (y * cores + core) * own
+                out[c, at : at + own, :] = dot_nn(tokens[core, y], w).astype(BF16)
 
 
 def spread_kernel(count, times, *refs):
@@ -268,13 +271,13 @@
 def spread(parts, times, after=()):
     pieces, height, width = parts[0].shape
     total = sum(p.shape[0] for p in parts)
-    vmem, anywhere = pl.BlockSpec(memory_space=pltpu.VMEM), pl.BlockSpec(memory_space=pl.ANY)
+    vmem = pl.BlockSpec(memory_space=pltpu.VMEM)
     return pl.pallas_call(
         functools.partial(spread_kernel, len(parts), times),
         out_shape=[
             jax.ShapeDtypeStruct((n, total, height // len(times), width), BF16) for n in times
         ],
-        in_specs=[vmem] * len(parts) + [anywhere] * len(after),
+        in_specs=[vmem] * (len(parts) + len(after)),
         out_specs=[vmem] * len(times),
         compiler_params=pltpu.CompilerParams(vmem_limit_bytes=16 * 2**20),
         cost_estimate=pl.CostEstimate(
@@ -283,33 +286,30 @@
     )(*parts, *after)
 
 
+def copy_kernel(value, *refs):
+    for k in range(value.shape[0]):
+        refs[-1][k] = value[k]
+
+
 def held_until(value, after):
-    anywhere = pl.BlockSpec(memory_space=pl.ANY)
-    return pl.pallas_call(
-        lambda *refs: None,
-        out_shape=jax.ShapeDtypeStruct(value.shape, value.dtype),
-        in_specs=[anywhere] * (1 + len(after)),
-        out_specs=anywhere,
-        input_output_aliases={0: 0},
-    )(value, *after)
-
-
-def on_core(kernel, outs, scratch=(), flops=0, moved=0, after=()):
+    return on_core(copy_kernel, jax.ShapeDtypeStruct(value.shape, value.dtype), moved=2**20)(
+        value, *after
+    )
+
+
+def on_core(kernel, outs, scratch=(), flops=0, moved=0, far=()):
     vmem, anywhere = pl.BlockSpec(memory_space=pltpu.VMEM), pl.BlockSpec(memory_space=pl.ANY)
-
-    def ordered(*refs):
-        kernel(*refs[len(after) :])
 
     def call(*operands):
         return pl.pallas_call(
-            ordered,
+            kernel,
             out_shape=outs,
-            in_specs=[anywhere] * len(after) + [vmem] * len(operands),
+            in_specs=[anywhere] * len(far) + [vmem] * len(operands),
             out_specs=jax.tree.map(lambda _: vmem, outs),
             scratch_shapes=list(scratch),
             compiler_params=pltpu.CompilerParams(vmem_limit_bytes=40 * 2**20),
             cost_estimate=pl.CostEstimate(flops=flops, bytes_accessed=moved, transcendentals=0),
-        )(*after, *operands)
+        )(*far, *operands)
 
     return call
 
@@ -359,22 +359,29 @@
     (near,) = spread([piece], (8,))
     near = lax.all_to_all(near.reshape(8, -1, width), "zl", 0, 0, tiled=True)
 
+    table = jnp.concatenate(
+        [
+            embed_weight.reshape(-1, width).astype(F32),
+            channel_embed.astype(F32),
+            agg_query.reshape(1, width),
+            jnp.zeros((8 - chans - 1, width), F32),
+        ],
+        axis=0,
+    )
     message = jax.ShapeDtypeStruct((own + EXTRA, width), BF16)
     messages = jax.ShapeDtypeStruct((4, own + EXTRA, width), BF16)
-    first, second = on_core(
+    stay, leave = on_core(
         embed_kernel,
         (messages, messages),
+        [
+            pltpu.VMEM((8, tokens), F32),
+            pltpu.VMEM((EXTRA, tokens), F32),
+        ],
         flops=2 * chans * tokens * width_p * width,
         moved=2 * 2**20,
-    )(
-        patches.reshape(chans, tokens, width_p),
-        embed_weight,
-        channel_embed,
-        agg_query.reshape(1, width),
-    )
-    leaving = jnp.where(lax.axis_index("core") == 0, second, first)
-    got = shifted(leaving, "core", 2, 1)
-    paired = on_core(pair_kernel, (message,) * 4, moved=2**20)(first, second, got)
+    )(table, patches.reshape(chans, tokens, width_p))
+    got = shifted(leave, "core", 2, 1)
+    paired = on_core(pair_kernel, (message,) * 4, moved=2**20)(stay, got)
     along = [shifted(paired[k], "y", 4, k) for k in (1, 2, 3)]
     sent, average, stats = on_core(
         combine_kernel,
@@ -383,13 +390,12 @@
             jax.ShapeDtypeStruct((own, width), F32),
             jax.ShapeDtypeStruct((8, own), F32),
         ),
-        moved=2**20,
+        flops=6 * 10**10,
     )(paired[0], *along)
-    (copies,) = spread([near], (4,), after=(sent,))
+    (copies,) = spread([near], (4,), after=(paired[0],))
     mine = lax.all_to_all(copies, "x", 0, 0, tiled=True).reshape(32, -1, width)
     partner = shifted(sent, "zh", 2, 1)
-    mine = held_until(mine, (partner,))
-    other = shifted(mine, "core", 2, 1)
+    other = shifted(held_until(mine, (partner,)), "core", 2, 1)
 
     scratch = [pltpu.VMEM((3 * width, width), F32), pltpu.VMEM((width, width), F32)]
     half = jax.ShapeDtypeStruct((own // 2, width), BF16)
@@ -406,12 +412,12 @@
     from_east = lax.ppermute(west, ("zh", "x", "zl"), [(b, a) for a, b in pairs])
     final = on_core(
         block1_kernel,
-        jax.ShapeDtypeStruct((parts, own, width), BF16),
+        jax.ShapeDtypeStruct((4, own, width), BF16),
         scratch,
         flops=block_flops,
         moved=4 * 2**20,
     )(state, from_west, from_east, norm_gains, mine, other)
-    everyone = lax.all_to_all(final, GROUP, 0, 0, tiled=True)
+    everyone = lax.all_gather(lax.all_to_all(final, "y", 0, 0, tiled=True), "core")
     decoded = on_core(
         decode_kernel,
         jax.ShapeDtypeStruct((chans, tokens, width_p), BF16),

time: 106 us -> 99.3 us (0.937)
  waiting for transfers between devices: 17.4 us -> 11.2 us
  local copies, waits for them, and re-layouts: 6.5 us -> 0.84 us
  starting transfers between devices: 55.5 us -> 61 us
  blocking collectives: 14.3 us -> 12.4 us
  other arithmetic: 0.8 us -> 2.47 us
    ppermute x6, starting transfers between devices: 27.7 us -> 35.3 us  [shifted(): lax.ppermute(value, axes, [(i, (i + steps) % size) for i in range(size)])]
    all_to_all x1, blocking collectives: 14.3 us -> 7.92 us  [body(): lax.all_to_all(final, 'y', 0, 0, tiled=True)]
    unnamed x22 -> x10, local copies, waits for them, and re-layouts: 6.49 us -> 0.76 us
    all_gather x0 -> x1, blocking collectives: none -> 4.45 us  [body(): lax.all_gather(lax.all_to_all(final, 'y', 0, 0, tiled=True), 'core')]
    all_to_all x1, waiting for transfers between devices: 3.57 us -> 0.01 us  [body(): mine = lax.all_to_all(copies, 'x', 0, 0, tiled=True).reshape(32, -1, width)]
    ppermute x6, waiting for transfers between devices: 12.8 us -> 10.2 us  [shifted(): lax.ppermute(value, axes, [(i, (i + steps) % size) for i in range(size)])]
    ppermute x1, starting transfers between devices: 3.64 us -> 1.92 us  [body(): from_west = lax.ppermute(east, ('zh', 'x', 'zl'), pairs)]
    convert_element_type x0 -> x2, other arithmetic: none -> 1.6 us  [the longest x1 0.92 us: body(): embed_weight.reshape(-1, width).astype(F32)]
  transfers between devices with their start and end apart: 10 -> 10, of which waited for: 6 -> 4; matrix products, arithmetic and copies ran while one was open for 0% -> 2% of each run, Pallas kernels for 2% -> 3%
where the time goes in v3:
time: 99.3 us; the launch traced here: 98.6 us
  starting transfers between devices  61 us (61%)
  blocking collectives  12.4 us (12%)
  waiting for transfers between devices  11.2 us (11%)
  Pallas kernels  10.6 us (11%)
  other arithmetic  2.47 us (2%)
    ppermute x6, starting transfers between devices, shifted(): lax.ppermute(value, axes, [(i, (i + steps) % size) for i in range(size)])  35.3 us
    all_to_all x1, starting transfers between devices, body(): near = lax.all_to_all(near.reshape(8, -1, width), 'zl', 0, 0, tiled=True)  13.1 us
    ppermute x6, waiting for transfers between devices, shifted(): lax.ppermute(value, axes, [(i, (i + steps) % size) for i in range(size)])  10.2 us
    pallas_call x7, Pallas kernels, call(): pl.pallas_call(kernel, out_shape=outs, in_specs=[anywhere] * len(far) + [...  8.58 us
    all_to_all x1, blocking collectives, body(): lax.all_to_all(final, 'y', 0, 0, tiled=True)  7.92 us
    ppermute x1, starting transfers between devices, body(): lax.ppermute(west, ('zh', 'x', 'zl'), [(b, a) for a, b in pairs])  6.68 us
    all_gather x1, blocking collectives, body(): lax.all_gather(lax.all_to_all(final, 'y', 0, 0, tiled=True), 'core')  4.45 us
    all_to_all x1, starting transfers between devices, body(): mine = lax.all_to_all(copies, 'x', 0, 0, tiled=True).reshape(32, -1, width)  4.02 us
  transfers between devices with their start and end apart: 10, of which 4 were waited for; matrix products, arithmetic and copies ran while one was open for 2% of the time, Pallas kernels for 3%

profile of v3, /device:TPU:1, one launch (start us, length us, event | category | flops | bytes accessed | tf_op | source)
XLA Modules:
  0.0 98.6 jit_solution(5891707428129670826)
XLA Ops:
  0.0 0.7 copy-done
  0.8 0.8 fusion
  1.5 0.8 shard_map.103
  2.3 13.1 %all-to-all-start = ((bf16[8,96,256]{2,1,0:T(8,128)(2,1)}), bf16[8,96,256]{2,1,0:T(8,128)(2,1)S(1)}, u32[]{:S(2)}, u32[]{:S(2)}) async-start(bf16[8,96,256]{2,1,0:T(8,128)(2,1)} %bitcast.6), calls=%async_computation | async-start | bytes 786432 | tf_op jit(solution)/shard_map/all_to_all | solution.py:360
  15.4 0.7 convert_element_type.11
  16.1 0.1 pad.8.clone
  16.1 0.9 bitcast_convert_fusion
  17.1 0.1 maximum_maximum_fusion.table
  17.2 0.9 shard_map.100
  18.1 2.9 %collective-permute-start = (bf16[4,144,256]{2,1,0:T(8,128)(2,1)S(1)}, bf16[4,144,256]{2,1,0:T(8,128)(2,1)S(1)}, u32[]{:S(2)}, u32[]{:S(2)}) collective-permute-start(bf16[4,144,256]{2,1,0:T(8,128)(2,1)S(1)} %get-tuple-element.18), channel_id=1, source_target_pairs={{0,32},{32,0},{1,33},{33,1},{2,34},{34,2},{3,35},{35,3},{4,36},{36... | collective-permute-start | bytes 884744 | tf_op jit(solution)/shard_map/ppermute | solution.py:318
  20.9 1.2 %collective-permute-done.got = bf16[4,144,256]{2,1,0:T(8,128)(2,1)S(1)} collective-permute-done((bf16[4,144,256]{2,1,0:T(8,128)(2,1)S(1)}, bf16[4,144,256]{2,1,0:T(8,128)(2,1)S(1)}, u32[]{:S(2)}, u32[]{:S(2)}) %collective-permute-start) | collective-permute-done | bytes 294944 | tf_op jit(solution)/shard_map/ppermute | solution.py:318
  22.1 0.5 shard_map.101
  22.6 3.2 %collective-permute-start.1 = (bf16[144,256]{1,0:T(8,128)(2,1)S(1)}, bf16[144,256]{1,0:T(8,128)(2,1)S(1)}, u32[]{:S(2)}, u32[]{:S(2)}) collective-permute-start(bf16[144,256]{1,0:T(8,128)(2,1)S(1)} %get-tuple-element.20), channel_id=1, source_target_pairs={{0,64},{64,128},{128,192},{192,0},{1,65},{65,129},{129,193},{193,1... | collective-permute-start | bytes 221192 | tf_op jit(solution)/shard_map/ppermute | solution.py:318
  25.8 4.5 %collective-permute-start.2 = (bf16[144,256]{1,0:T(8,128)(2,1)S(1)}, bf16[144,256]{1,0:T(8,128)(2,1)S(1)}, u32[]{:S(2)}, u32[]{:S(2)}) collective-permute-start(bf16[144,256]{1,0:T(8,128)(2,1)S(1)} %get-tuple-element.21), channel_id=1, source_target_pairs={{0,128},{64,192},{128,0},{192,64},{1,129},{65,193},{129,1},{193,65... | collective-permute-start | bytes 221192 | tf_op jit(solution)/shard_map/ppermute | solution.py:318
  30.3 3.0 %collective-permute-start.3 = (bf16[144,256]{1,0:T(8,128)(2,1)S(1)}, bf16[144,256]{1,0:T(8,128)(2,1)S(1)}, u32[]{:S(2)}, u32[]{:S(2)}) collective-permute-start(bf16[144,256]{1,0:T(8,128)(2,1)S(1)} %get-tuple-element.22), channel_id=1, source_target_pairs={{0,192},{64,0},{128,64},{192,128},{1,193},{65,1},{129,65},{193,129... | collective-permute-start | bytes 221192 | tf_op jit(solution)/shard_map/ppermute | solution.py:318
  33.3 0.0 all-to-all-done.refs_0_
  33.3 1.3 %shard_map.104 = bf16[4,8,96,256]{3,2,1,0:T(8,128)(2,1)} custom-call(bf16[8,96,256]{2,1,0:T(8,128)(2,1)S(1)} %all-to-all-done.refs_0_, bf16[144,256]{1,0:T(8,128)(2,1)S(1)} %get-tuple-element.19.mine.refs_1_), custom_call_target="tpu_custom_call" | custom-call | bytes 1966080 | tf_op jit(solution)/shard_map/pallas_call | solution.py:275
  34.6 4.0 %all-to-all-start.1 = ((bf16[4,8,96,256]{3,2,1,0:T(8,128)(2,1)}), bf16[4,8,96,256]{3,2,1,0:T(8,128)(2,1)S(1)}, u32[]{:S(2)}, u32[]{:S(2)}) async-start(bf16[4,8,96,256]{3,2,1,0:T(8,128)(2,1)} %shard_map.104), calls=%async_computation.1 | async-start | bytes 3145728 | tf_op jit(solution)/shard_map/all_to_all | solution.py:396
  38.6 0.3 shard_map.102
  38.9 7.9 %collective-permute-start.4 = (bf16[144,256]{1,0:T(8,128)(2,1)S(1)}, bf16[144,256]{1,0:T(8,128)(2,1)S(1)}, u32[]{:S(2)}, u32[]{:S(2)}) collective-permute-start(bf16[144,256]{1,0:T(8,128)(2,1)S(1)} %get-tuple-element.25), channel_id=1, source_target_pairs={{0,256},{256,0},{1,257},{257,1},{2,258},{258,2},{3,259},{259,3},{4... | collective-permute-start | bytes 221192 | tf_op jit(solution)/shard_map/ppermute | solution.py:318
  46.9 5.9 %collective-permute-done.4.refs_0_.got = bf16[144,256]{1,0:T(8,128)(2,1)S(1)} collective-permute-done((bf16[144,256]{1,0:T(8,128)(2,1)S(1)}, bf16[144,256]{1,0:T(8,128)(2,1)S(1)}, u32[]{:S(2)}, u32[]{:S(2)}) %collective-permute-start.4) | collective-permute-done | bytes 73760 | tf_op jit(solution)/shard_map/ppermute | solution.py:318
  52.8 0.1 shard_map.105
  52.9 13.8 %collective-permute-start.5 = (bf16[32,96,256]{2,1,0:T(8,128)(2,1)S(1)}, bf16[32,96,256]{2,1,0:T(8,128)(2,1)S(1)}, u32[]{:S(2)}, u32[]{:S(2)}) collective-permute-start(bf16[32,96,256]{2,1,0:T(8,128)(2,1)S(1)} %shard_map.105), channel_id=1, source_target_pairs={{0,32},{32,0},{1,33},{33,1},{2,34},{34,2},{3,35},{35,3},{4,36},{36... | collective-permute-start | bytes 4718600 | tf_op jit(solution)/shard_map/ppermute | solution.py:318
  66.7 3.0 %collective-permute-done.5.other = bf16[32,96,256]{2,1,0:T(8,128)(2,1)S(1)} collective-permute-done((bf16[32,96,256]{2,1,0:T(8,128)(2,1)S(1)}, bf16[32,96,256]{2,1,0:T(8,128)(2,1)S(1)}, u32[]{:S(2)}, u32[]{:S(2)}) %collective-permute-start.5) | collective-permute-done | bytes 1572896 | tf_op jit(solution)/shard_map/ppermute | solution.py:318
  69.7 2.4 %shard_map.106 = (f32[128,256]{1,0:T(8,128)S(1)}, bf16[64,256]{1,0:T(8,128)(2,1)S(1)}, bf16[64,256]{1,0:T(8,128)(2,1)S(1)}) custom-call(f32[128,256]{1,0:T(8,128)S(1)} %get-tuple-element.23.own, f32[8,128]{1,0:T(8,128)S(1)} %get-tuple-element.24.own_rows, bf16[144,256]{1,0:T(8,128)(2,1)S(1)} %collective-permute-done.4.refs_0_.got, f32[5,256]{1,0:T(8,128)S(1)} %copy-done.3, ...), custom_call_target="tpu_custom_call" | custom-call | flops 201326592 | bytes 4194304 | tf_op jit(solution)/shard_map/pallas_call | solution.py:304
  72.2 1.9 %collective-permute-start.6 = (bf16[64,256]{1,0:T(8,128)(2,1)S(1)}, bf16[64,256]{1,0:T(8,128)(2,1)S(1)}, u32[]{:S(2)}, u32[]{:S(2)}) collective-permute-start(bf16[64,256]{1,0:T(8,128)(2,1)S(1)} %get-tuple-element.27), channel_id=1, source_target_pairs={{0,1},{1,2},{2,3},{3,4},{4,5},{5,6},{6,7},{7,264},{8,9},{9,10},{10... | collective-permute-start | bytes 98312 | tf_op jit(solution)/shard_map/ppermute | solution.py:411
  74.1 6.7 %collective-permute-start.7 = (bf16[64,256]{1,0:T(8,128)(2,1)S(1)}, bf16[64,256]{1,0:T(8,128)(2,1)S(1)}, u32[]{:S(2)}, u32[]{:S(2)}) collective-permute-start(bf16[64,256]{1,0:T(8,128)(2,1)S(1)} %get-tuple-element.28), channel_id=1, source_target_pairs={{1,0},{2,1},{3,2},{4,3},{5,4},{6,5},{7,6},{264,7},{9,8},{10,9},{11... | collective-permute-start | bytes 98312 | tf_op jit(solution)/shard_map/ppermute | solution.py:412
  80.8 1.0 %collective-permute-done.7.from_east = bf16[64,256]{1,0:T(8,128)(2,1)S(1)} collective-permute-done((bf16[64,256]{1,0:T(8,128)(2,1)S(1)}, bf16[64,256]{1,0:T(8,128)(2,1)S(1)}, u32[]{:S(2)}, u32[]{:S(2)}) %collective-permute-start.7) | collective-permute-done | bytes 32800 | tf_op jit(solution)/shard_map/ppermute | solution.py:412
  81.8 3.2 %shard_map.107 = bf16[4,128,256]{2,1,0:T(8,128)(2,1)S(1)} custom-call(f32[128,256]{1,0:T(8,128)S(1)} %get-tuple-element.26.state, bf16[64,256]{1,0:T(8,128)(2,1)S(1)} %collective-permute-done.6.from_west, bf16[64,256]{1,0:T(8,128)(2,1)S(1)} %collective-permute-done.7.from_east, f32[5,256]{1,0:T(8,128)S(1)} %copy-done.3, bf16[32,96,256]{2,1,0:T(8,128)(2,1)S(1)} %bitcast.15, ...), custom_call_target="tpu_custom_call" | custom-call | flops 201326592 | bytes 4194304 | tf_op jit(solution)/shard_map/pallas_call | solution.py:304
  85.0 7.9 %all_to_all.15 = bf16[4,128,256]{2,1,0:T(8,128)(2,1)S(1)} all-to-all(bf16[4,128,256]{2,1,0:T(8,128)(2,1)S(1)} %shard_map.107), channel_id=1, replica_groups=mesh['zh'=2,'y'=4,'core'=2,'x'=4,'zl'=8] {'y'}, dimensions={0} | all-to-all | bytes 524288 | tf_op jit(solution)/shard_map/all_to_all | solution.py:420
  93.0 4.5 %all-gather = bf16[8,128,256]{2,1,0:T(8,128)(2,1)S(1)} all-gather(bf16[4,128,256]{2,1,0:T(8,128)(2,1)S(1)} %all_to_all.15), channel_id=2, replica_groups=mesh['zh'=2,'y'=4,'core'=2,'x'=4,'zl'=8] {'core'}, dimensions={0}, use_global_device_ids=true | all-gather | bytes 786432 | tf_op jit(solution)/shard_map/all_gather | solution.py:420
  97.4 1.2 %shard_map.108 = bf16[2,1024,128]{2,1,0:T(8,128)(2,1)} custom-call(bf16[2,4,128,256]{3,2,1,0:T(8,128)(2,1)S(1)} %bitcast.16, bf16[2,256,128]{2,1,0:T(8,128)(2,1)S(1)} %copy-done.2), custom_call_target="tpu_custom_call" | custom-call | flops 134217728 | bytes 2097152 | tf_op jit(solution)/shard_map/pallas_call | solution.py:304
  (17 shorter events, 0.0 us)
Async XLA Ops:
  0.0 0.8 copy-start
  0.0 17.1 %copy-start.4 = (f32[256]{0:T(256)S(1)}, f32[256]{0:T(256)}, u32[]{:S(2)}) copy-start(f32[256]{0:T(256)} %param.13) | copy-start | bytes 3076
  0.0 17.2 %copy-start.1 = (bf16[2,128,8,128]{3,2,1,0:T(8,128)(2,1)S(1)}, bf16[2,128,8,128]{3,2,1,0:T(8,128)(2,1)}, u32[]{:S(2)}) copy-start(bf16[2,128,8,128]{3,2,1,0:T(8,128)(2,1)} %param.10) | copy-start | bytes 1572868
  2.3 31.0 %all-to-all-start = ((bf16[8,96,256]{2,1,0:T(8,128)(2,1)}), bf16[8,96,256]{2,1,0:T(8,128)(2,1)S(1)}, u32[]{:S(2)}, u32[]{:S(2)}) async-start(bf16[8,96,256]{2,1,0:T(8,128)(2,1)} %bitcast.6), calls=%async_computation | async-start | bytes 786432 | tf_op jit(solution)/shard_map/all_to_all | solution.py:360
  18.1 4.1 %collective-permute-start = (bf16[4,144,256]{2,1,0:T(8,128)(2,1)S(1)}, bf16[4,144,256]{2,1,0:T(8,128)(2,1)S(1)}, u32[]{:S(2)}, u32[]{:S(2)}) collective-permute-start(bf16[4,144,256]{2,1,0:T(8,128)(2,1)S(1)} %get-tuple-element.18), channel_id=1, source_target_pairs={{0,32},{32,0},{1,33},{33,1},{2,34},{34,2},{3,35},{35,3},{4,36},{36... | collective-permute-start | bytes 884744 | tf_op jit(solution)/shard_map/ppermute | solution.py:318
  22.6 16.0 %collective-permute-start.1 = (bf16[144,256]{1,0:T(8,128)(2,1)S(1)}, bf16[144,256]{1,0:T(8,128)(2,1)S(1)}, u32[]{:S(2)}, u32[]{:S(2)}) collective-permute-start(bf16[144,256]{1,0:T(8,128)(2,1)S(1)} %get-tuple-element.20), channel_id=1, source_target_pairs={{0,64},{64,128},{128,192},{192,0},{1,65},{65,129},{129,193},{193,1... | collective-permute-start | bytes 221192 | tf_op jit(solution)/shard_map/ppermute | solution.py:318
  25.8 12.8 %collective-permute-start.2 = (bf16[144,256]{1,0:T(8,128)(2,1)S(1)}, bf16[144,256]{1,0:T(8,128)(2,1)S(1)}, u32[]{:S(2)}, u32[]{:S(2)}) collective-permute-start(bf16[144,256]{1,0:T(8,128)(2,1)S(1)} %get-tuple-element.21), channel_id=1, source_target_pairs={{0,128},{64,192},{128,0},{192,64},{1,129},{65,193},{129,1},{193,65... | collective-permute-start | bytes 221192 | tf_op jit(solution)/shard_map/ppermute | solution.py:318
  30.3 8.3 %collective-permute-start.3 = (bf16[144,256]{1,0:T(8,128)(2,1)S(1)}, bf16[144,256]{1,0:T(8,128)(2,1)S(1)}, u32[]{:S(2)}, u32[]{:S(2)}) collective-permute-start(bf16[144,256]{1,0:T(8,128)(2,1)S(1)} %get-tuple-element.22), channel_id=1, source_target_pairs={{0,192},{64,0},{128,64},{192,128},{1,193},{65,1},{129,65},{193,129... | collective-permute-start | bytes 221192 | tf_op jit(solution)/shard_map/ppermute | solution.py:318
  34.6 18.2 %all-to-all-start.1 = ((bf16[4,8,96,256]{3,2,1,0:T(8,128)(2,1)}), bf16[4,8,96,256]{3,2,1,0:T(8,128)(2,1)S(1)}, u32[]{:S(2)}, u32[]{:S(2)}) async-start(bf16[4,8,96,256]{3,2,1,0:T(8,128)(2,1)} %shard_map.104), calls=%async_computation.1 | async-start | bytes 3145728 | tf_op jit(solution)/shard_map/all_to_all | solution.py:396
  38.9 13.9 %collective-permute-start.4 = (bf16[144,256]{1,0:T(8,128)(2,1)S(1)}, bf16[144,256]{1,0:T(8,128)(2,1)S(1)}, u32[]{:S(2)}, u32[]{:S(2)}) collective-permute-start(bf16[144,256]{1,0:T(8,128)(2,1)S(1)} %get-tuple-element.25), channel_id=1, source_target_pairs={{0,256},{256,0},{1,257},{257,1},{2,258},{258,2},{3,259},{259,3},{4... | collective-permute-start | bytes 221192 | tf_op jit(solution)/shard_map/ppermute | solution.py:318
  52.8 16.9 %copy-start.3 = (f32[5,256]{1,0:T(8,128)S(1)}, f32[5,256]{1,0:T(8,128)}, u32[]{:S(2)}) copy-start(f32[5,256]{1,0:T(8,128)} %gains.3) | copy-start | bytes 15364
  52.9 16.8 %collective-permute-start.5 = (bf16[32,96,256]{2,1,0:T(8,128)(2,1)S(1)}, bf16[32,96,256]{2,1,0:T(8,128)(2,1)S(1)}, u32[]{:S(2)}, u32[]{:S(2)}) collective-permute-start(bf16[32,96,256]{2,1,0:T(8,128)(2,1)S(1)} %shard_map.105), channel_id=1, source_target_pairs={{0,32},{32,0},{1,33},{33,1},{2,34},{34,2},{3,35},{35,3},{4,36},{36... | collective-permute-start | bytes 4718600 | tf_op jit(solution)/shard_map/ppermute | solution.py:318
  72.2 8.6 %collective-permute-start.6 = (bf16[64,256]{1,0:T(8,128)(2,1)S(1)}, bf16[64,256]{1,0:T(8,128)(2,1)S(1)}, u32[]{:S(2)}, u32[]{:S(2)}) collective-permute-start(bf16[64,256]{1,0:T(8,128)(2,1)S(1)} %get-tuple-element.27), channel_id=1, source_target_pairs={{0,1},{1,2},{2,3},{3,4},{4,5},{5,6},{6,7},{7,264},{8,9},{9,10},{10... | collective-permute-start | bytes 98312 | tf_op jit(solution)/shard_map/ppermute | solution.py:411
  74.1 7.7 %collective-permute-start.7 = (bf16[64,256]{1,0:T(8,128)(2,1)S(1)}, bf16[64,256]{1,0:T(8,128)(2,1)S(1)}, u32[]{:S(2)}, u32[]{:S(2)}) collective-permute-start(bf16[64,256]{1,0:T(8,128)(2,1)S(1)} %get-tuple-element.28), channel_id=1, source_target_pairs={{1,0},{2,1},{3,2},{4,3},{5,4},{6,5},{7,6},{264,7},{9,8},{10,9},{11... | collective-permute-start | bytes 98312 | tf_op jit(solution)/shard_map/ppermute | solution.py:412
  81.8 15.6 %copy-start.2 = (bf16[2,256,128]{2,1,0:T(8,128)(2,1)S(1)}, bf16[2,256,128]{2,1,0:T(8,128)(2,1)}, u32[]{:S(2)}) copy-start(bf16[2,256,128]{2,1,0:T(8,128)(2,1)} %weight.1) | copy-start | bytes 393220

commit v4 on v3

--- a/solution.py
+++ b/solution.py
@@ -131,12 +131,11 @@
     return centred * lax.rsqrt(spread + EPS) * gain
 
 
-def attention_weights(layer, mine, other, qkv_rows, proj_rows):
-    lo = 48 * layer
+def attention_weights(mine, other, qkv_rows, proj_rows):
     first_core = lax.axis_index("core") == 0
     for lon in range(mine.shape[0]):
-        a = mine[lon, lo : lo + 16, :].astype(F32)
-        b = other[lon, lo : lo + 16, :].astype(F32)
+        a = mine[lon, :16, :].astype(F32)
+        b = other[lon, :16, :].astype(F32)
         tail = jnp.where(first_core, b, a)
         qkv_rows[lon * 24 : lon * 24 + 16, :] = jnp.where(first_core, a, b)
         qkv_rows[lon * 24 + 16 : lon * 24 + 24, :] = tail[:8]
@@ -144,8 +143,7 @@
     return qkv_rows[...].astype(BF16), proj_rows[...].astype(BF16)
 
 
-def mlp_weights(layer, mine, other):
-    lo = 48 * layer
+def mlp_weights(mine, other):
     width = mine.shape[2]
 
     def rows(at):
@@ -153,7 +151,7 @@
             [w[:, at : at + 16, :].reshape(-1, width) for w in (mine, other)], axis=0
         )
 
-    return rows(lo + 16), rows(lo + 32)
+    return rows(16), rows(32)
 
 
 def attend(q, keys, values, allowed):
@@ -197,15 +195,20 @@
     return dot_nn(jnp.where(pick, 1.0, 0.0).astype(BF16), x).astype(BF16)
 
 
-def block0_kernel(own, own_rows, got, gains, mine, other, state, west, east, qkv_rows, proj_rows):
-    n, width = own.shape
+def whole_kernel(own, own_rows, got, state):
+    n = own.shape[0]
     got_top, got_total = top_and_total(got[n:, :n])
     rows = own_rows[...]
-    x, _, _ = merged(
+    state[...], _, _ = merged(
         [own[...], got[:n, :].astype(F32)], [rows[0:1], got_top], [rows[1:2], got_total]
     )
-    w_qkv, w_proj = attention_weights(0, mine, other, qkv_rows, proj_rows)
-    w_up, w_down = mlp_weights(0, mine, other)
+
+
+def block0_kernel(start, gains, mine, other, state, near, far, qkv_rows, proj_rows):
+    n, width = start.shape
+    x = start[...]
+    w_qkv, w_proj = attention_weights(mine, other, qkv_rows, proj_rows)
+    w_up, w_down = mlp_weights(mine, other)
     a = norm(x, gains[0:1, :]).astype(BF16)
     qkv = dot_nt(a, w_qkv).astype(BF16).astype(F32)
     allowed = token_at((n, n), 0)[0] == token_at((n, n), 1)[0]
@@ -215,21 +218,26 @@
     x = after_attention(x, mixed, gains[1:2, :], w_proj, w_up, w_down)
     state[...] = x
     short = x.astype(BF16)
-    west[...] = half_tokens(short, 0)
-    east[...] = half_tokens(short, 1)
-
-
-def block1_kernel(state, from_west, from_east, gains, mine, other, out, qkv_rows, proj_rows):
+    odd = lax.axis_index("zl") & 1
+    near[...] = half_tokens(short, 1 - odd)
+    far[...] = half_tokens(short, odd)
+
+
+def sides_kernel(from_near, from_far, gains, out):
+    odd = (lax.axis_index("zl") & 1) == 1
+    near, far = from_near[...].astype(F32), from_far[...].astype(F32)
+    sides = jnp.concatenate([jnp.where(odd, near, far), jnp.where(odd, far, near)], axis=0)
+    out[...] = norm(sides, gains[2:3, :]).astype(BF16)
+
+
+def block1_kernel(state, sides, gains, mine, other, out, qkv_rows, proj_rows):
     n, width = state.shape
     x = state[...]
-    w_qkv, w_proj = attention_weights(1, mine, other, qkv_rows, proj_rows)
-    w_up, w_down = mlp_weights(1, mine, other)
-    sides = jnp.concatenate([from_west[...].astype(F32), from_east[...].astype(F32)], axis=0)
-    gain = gains[2:3, :]
-    a = norm(x, gain).astype(BF16)
-    b = norm(sides, gain).astype(BF16)
+    w_qkv, w_proj = attention_weights(mine, other, qkv_rows, proj_rows)
+    w_up, w_down = mlp_weights(mine, other)
+    a = norm(x, gains[2:3, :]).astype(BF16)
     qkv = dot_nt(a, w_qkv).astype(BF16).astype(F32)
-    side_kv = dot_nt(b, w_qkv[width:, :]).astype(BF16).astype(F32)
+    side_kv = dot_nt(sides[...], w_qkv[width:, :]).astype(BF16).astype(F32)
     keys = jnp.concatenate([qkv[:, width : 2 * width], side_kv[:, :width]], axis=0)
     values = jnp.concatenate([qkv[:, 2 * width :], side_kv[:, width:]], axis=0)
     q_block, q_half, _ = token_at((n, 2 * n), 0)
@@ -318,14 +326,19 @@
     return lax.ppermute(value, axes, [(i, (i + steps) % size) for i in range(size)])
 
 
-def eastward():
-    pairs = []
+def swaps():
+    def at(zh, x, zl):
+        return (zh * 4 + x) * 8 + zl
+
+    near, far = [], []
     for zh in range(2):
         for x in range(4):
-            for zl in range(8):
-                to = (zh, x, zl + 1) if zl < 7 else (1 - zh, (x + 1) % 4, 0)
-                pairs.append(((zh * 4 + x) * 8 + zl, (to[0] * 4 + to[1]) * 8 + to[2]))
-    return pairs
+            near += [(at(zh, x, zl), at(zh, x, zl ^ 1)) for zl in range(8)]
+            far += [(at(zh, x, zl), at(zh, x, zl + 1)) for zl in (1, 3, 5)]
+            far += [(at(zh, x, zl), at(zh, x, zl - 1)) for zl in (2, 4, 6)]
+            far.append((at(zh, x, 7), at(1 - zh, (x + 1) % 4, 0)))
+            far.append((at(zh, x, 0), at(1 - zh, (x + 3) % 4, 7)))
+    return near, far
 
 
 def weight_pieces(qkv, proj, up, down):
@@ -392,31 +405,39 @@
         ),
         flops=6 * 10**10,
     )(paired[0], *along)
-    (copies,) = spread([near], (4,), after=(paired[0],))
-    mine = lax.all_to_all(copies, "x", 0, 0, tiled=True).reshape(32, -1, width)
+    copies0, copies1 = spread([near], (4, 4), after=(paired[0],))
+    mine0 = lax.all_to_all(copies0, "x", 0, 0, tiled=True).reshape(32, -1, width)
+    mine1 = lax.all_to_all(copies1, "x", 0, 0, tiled=True).reshape(32, -1, width)
     partner = shifted(sent, "zh", 2, 1)
-    other = shifted(held_until(mine, (partner,)), "core", 2, 1)
+    other0 = shifted(mine0, "core", 2, 1)
+    start = on_core(
+        whole_kernel, jax.ShapeDtypeStruct((own, width), F32), flops=6 * 10**10
+    )(average, stats, partner)
 
     scratch = [pltpu.VMEM((3 * width, width), F32), pltpu.VMEM((width, width), F32)]
     half = jax.ShapeDtypeStruct((own // 2, width), BF16)
     block_flops = 2 * own * width * width * 12
-    state, west, east = on_core(
+    state, to_near, to_far = on_core(
         block0_kernel,
         (jax.ShapeDtypeStruct((own, width), F32), half, half),
         scratch,
         flops=block_flops,
         moved=4 * 2**20,
-    )(average, stats, partner, norm_gains, mine, other)
-    pairs = eastward()
-    from_west = lax.ppermute(east, ("zh", "x", "zl"), pairs)
-    from_east = lax.ppermute(west, ("zh", "x", "zl"), [(b, a) for a, b in pairs])
+    )(start, norm_gains, mine0, other0)
+    near_pairs, far_pairs = swaps()
+    from_near = lax.ppermute(to_near, ("zh", "x", "zl"), near_pairs)
+    from_far = lax.ppermute(to_far, ("zh", "x", "zl"), far_pairs)
+    other1 = shifted(held_until(mine1, (to_far,)), "core", 2, 1)
+    sides = on_core(
+        sides_kernel, jax.ShapeDtypeStruct((own, width), BF16), flops=6 * 10**10
+    )(from_near, from_far, norm_gains)
     final = on_core(
         block1_kernel,
         jax.ShapeDtypeStruct((4, own, width), BF16),
         scratch,
         flops=block_flops,
         moved=4 * 2**20,
-    )(state, from_west, from_east, norm_gains, mine, other)
+    )(state, sides, norm_gains, mine1, other1)
     everyone = lax.all_gather(lax.all_to_all(final, "y", 0, 0, tiled=True), "core")
     decoded = on_core(
         decode_kernel,

time: 99.3 us -> 98.1 us (0.988)
  waiting for transfers between devices: 11.2 us -> 4.86 us
  starting transfers between devices: 61 us -> 64.9 us
  other arithmetic: 2.47 us -> 0.86 us
  local copies, waits for them, and re-layouts: 0.84 us -> 2.34 us
    ppermute x6 -> x7, waiting for transfers between devices: 10.2 us -> 4.5 us  [shifted(): lax.ppermute(value, axes, [(i, (i + steps) % size) for i in range(size)])]
    all_to_all x1 -> x2, starting transfers between devices: 4.02 us -> 8.19 us  [the longest x1 4.17 us: body(): lax.all_to_all(copies1, 'x', 0, 0, tiled=True).reshape(32, -1, width)]
    all_to_all x1, blocking collectives: 7.92 us -> 9.51 us  [body(): lax.all_to_all(final, 'y', 0, 0, tiled=True)]
    unnamed x10 -> x18, local copies, waits for them, and re-layouts: 0.76 us -> 2.26 us
    ppermute x6 -> x7, starting transfers between devices: 35.3 us -> 34 us  [shifted(): lax.ppermute(value, axes, [(i, (i + steps) % size) for i in range(size)])]
    pallas_call x7 -> x9, Pallas kernels: 8.58 us -> 8.73 us  [call(): pl.pallas_call(kernel, out_shape=outs, in_specs=[anywhere] * len(far) + [...]
  transfers between devices with their start and end apart: 10 -> 12, of which waited for: 4 -> 5; matrix products, arithmetic and copies ran while one was open for 2% -> 0% of each run, Pallas kernels for 3% -> 6%
where the time goes in v4:
time: 98.1 us; the launch traced here: 97.2 us
  starting transfers between devices  64.9 us (66%)
  blocking collectives  13.2 us (13%)
  Pallas kernels  10.7 us (11%)
  waiting for transfers between devices  4.86 us (5%)
  local copies, waits for them, and re-layouts  2.34 us (2%)
    ppermute x7, starting transfers between devices, shifted(): lax.ppermute(value, axes, [(i, (i + steps) % size) for i in range(size)])  34 us
    all_to_all x1, starting transfers between devices, body(): near = lax.all_to_all(near.reshape(8, -1, width), 'zl', 0, 0, tiled=True)  13.2 us
    all_to_all x1, blocking collectives, body(): lax.all_to_all(final, 'y', 0, 0, tiled=True)  9.51 us
    pallas_call x9, Pallas kernels, call(): pl.pallas_call(kernel, out_shape=outs, in_specs=[anywhere] * len(far) + [...  8.73 us
    ppermute x1, starting transfers between devices, body(): from_far = lax.ppermute(to_far, ('zh', 'x', 'zl'), far_pairs)  6.51 us
    ppermute x7, waiting for transfers between devices, shifted(): lax.ppermute(value, axes, [(i, (i + steps) % size) for i in range(size)])  4.5 us
    all_to_all x1, starting transfers between devices, body(): lax.all_to_all(copies1, 'x', 0, 0, tiled=True).reshape(32, -1, width)  4.17 us
    all_to_all x1, starting transfers between devices, body(): lax.all_to_all(copies0, 'x', 0, 0, tiled=True).reshape(32, -1, width)  4.01 us
  transfers between devices with their start and end apart: 12, of which 5 were waited for; matrix products, arithmetic and copies ran while one was open for 0% of the time, Pallas kernels for 6%

profile of v4, /device:TPU:1, one launch (start us, length us, event | category | flops | bytes accessed | tf_op | source)
XLA Modules:
  0.0 97.2 jit_solution(4903481679686465370)
XLA Ops:
  0.0 0.8 copy-done
  0.8 0.7 copy-done.6
  1.5 0.7 fusion
  2.2 0.8 shard_map.104
  3.0 13.2 %all-to-all-start = ((bf16[8,96,256]{2,1,0:T(8,128)(2,1)}), bf16[8,96,256]{2,1,0:T(8,128)(2,1)S(1)}, u32[]{:S(2)}, u32[]{:S(2)}) async-start(bf16[8,96,256]{2,1,0:T(8,128)(2,1)} %bitcast.6), calls=%async_computation | async-start | bytes 786432 | tf_op jit(solution)/shard_map/all_to_all | solution.py:373
  16.5 0.8 copy-done.1
  17.2 0.9 shard_map.100
  18.1 2.9 %collective-permute-start = (bf16[4,144,256]{2,1,0:T(8,128)(2,1)S(1)}, bf16[4,144,256]{2,1,0:T(8,128)(2,1)S(1)}, u32[]{:S(2)}, u32[]{:S(2)}) collective-permute-start(bf16[4,144,256]{2,1,0:T(8,128)(2,1)S(1)} %get-tuple-element.20), channel_id=1, source_target_pairs={{0,32},{32,0},{1,33},{33,1},{2,34},{34,2},{3,35},{35,3},{4,36},{36... | collective-permute-start | bytes 884744 | tf_op jit(solution)/shard_map/ppermute | solution.py:326
  21.0 1.2 %collective-permute-done.got = bf16[4,144,256]{2,1,0:T(8,128)(2,1)S(1)} collective-permute-done((bf16[4,144,256]{2,1,0:T(8,128)(2,1)S(1)}, bf16[4,144,256]{2,1,0:T(8,128)(2,1)S(1)}, u32[]{:S(2)}, u32[]{:S(2)}) %collective-permute-start) | collective-permute-done | bytes 294944 | tf_op jit(solution)/shard_map/ppermute | solution.py:326
  22.2 0.5 shard_map.101
  22.6 3.2 %collective-permute-start.1 = (bf16[144,256]{1,0:T(8,128)(2,1)S(1)}, bf16[144,256]{1,0:T(8,128)(2,1)S(1)}, u32[]{:S(2)}, u32[]{:S(2)}) collective-permute-start(bf16[144,256]{1,0:T(8,128)(2,1)S(1)} %get-tuple-element.22), channel_id=1, source_target_pairs={{0,64},{64,128},{128,192},{192,0},{1,65},{65,129},{129,193},{193,1... | collective-permute-start | bytes 221192 | tf_op jit(solution)/shard_map/ppermute | solution.py:326
  25.8 4.5 %collective-permute-start.2 = (bf16[144,256]{1,0:T(8,128)(2,1)S(1)}, bf16[144,256]{1,0:T(8,128)(2,1)S(1)}, u32[]{:S(2)}, u32[]{:S(2)}) collective-permute-start(bf16[144,256]{1,0:T(8,128)(2,1)S(1)} %get-tuple-element.23), channel_id=1, source_target_pairs={{0,128},{64,192},{128,0},{192,64},{1,129},{65,193},{129,1},{193,65... | collective-permute-start | bytes 221192 | tf_op jit(solution)/shard_map/ppermute | solution.py:326
  30.4 3.0 %collective-permute-start.3 = (bf16[144,256]{1,0:T(8,128)(2,1)S(1)}, bf16[144,256]{1,0:T(8,128)(2,1)S(1)}, u32[]{:S(2)}, u32[]{:S(2)}) collective-permute-start(bf16[144,256]{1,0:T(8,128)(2,1)S(1)} %get-tuple-element.24), channel_id=1, source_target_pairs={{0,192},{64,0},{128,64},{192,128},{1,193},{65,1},{129,65},{193,129... | collective-permute-start | bytes 221192 | tf_op jit(solution)/shard_map/ppermute | solution.py:326
  33.4 0.3 all-to-all-done.refs_0_
  33.6 1.2 %shard_map.105 = (bf16[4,8,48,256]{3,2,1,0:T(8,128)(2,1)}, bf16[4,8,48,256]{3,2,1,0:T(8,128)(2,1)}) custom-call(bf16[8,96,256]{2,1,0:T(8,128)(2,1)S(1)} %all-to-all-done.refs_0_, bf16[144,256]{1,0:T(8,128)(2,1)S(1)} %get-tuple-element.21.mine.refs_1_), custom_call_target="tpu_custom_call" | custom-call | bytes 3538944 | tf_op jit(solution)/shard_map/pallas_call | solution.py:283
  34.9 4.0 %all-to-all-start.1 = ((bf16[4,8,48,256]{3,2,1,0:T(8,128)(2,1)}), bf16[4,8,48,256]{3,2,1,0:T(8,128)(2,1)S(1)}, u32[]{:S(2)}, u32[]{:S(2)}) async-start(bf16[4,8,48,256]{3,2,1,0:T(8,128)(2,1)} %get-tuple-element.28), calls=%async_computation.1 | async-start | bytes 1572864 | tf_op jit(solution)/shard_map/all_to_all | solution.py:409
  38.9 0.3 shard_map.102
  39.2 7.9 %collective-permute-start.4 = (bf16[144,256]{1,0:T(8,128)(2,1)S(1)}, bf16[144,256]{1,0:T(8,128)(2,1)S(1)}, u32[]{:S(2)}, u32[]{:S(2)}) collective-permute-start(bf16[144,256]{1,0:T(8,128)(2,1)S(1)} %get-tuple-element.27), channel_id=1, source_target_pairs={{0,256},{256,0},{1,257},{257,1},{2,258},{258,2},{3,259},{259,3},{4... | collective-permute-start | bytes 221192 | tf_op jit(solution)/shard_map/ppermute | solution.py:326
  47.2 4.2 %all-to-all-start.2 = ((bf16[4,8,48,256]{3,2,1,0:T(8,128)(2,1)}), bf16[4,8,48,256]{3,2,1,0:T(8,128)(2,1)S(1)}, u32[]{:S(2)}, u32[]{:S(2)}) async-start(bf16[4,8,48,256]{3,2,1,0:T(8,128)(2,1)} %get-tuple-element.32), calls=%async_computation.2 | async-start | bytes 1572864 | tf_op jit(solution)/shard_map/all_to_all | solution.py:410
  51.4 9.6 %collective-permute-start.5 = (bf16[32,48,256]{2,1,0:T(8,128)(2,1)S(1)}, bf16[32,48,256]{2,1,0:T(8,128)(2,1)S(1)}, u32[]{:S(2)}, u32[]{:S(2)}) collective-permute-start(bf16[32,48,256]{2,1,0:T(8,128)(2,1)S(1)} %bitcast.16), channel_id=1, source_target_pairs={{0,32},{32,0},{1,33},{33,1},{2,34},{34,2},{3,35},{35,3},{4,36},{36... | collective-permute-start | bytes 2359304 | tf_op jit(solution)/shard_map/ppermute | solution.py:326
  61.1 0.2 shard_map.103.start
  61.3 1.6 %collective-permute-done.5.other = bf16[32,48,256]{2,1,0:T(8,128)(2,1)S(1)} collective-permute-done((bf16[32,48,256]{2,1,0:T(8,128)(2,1)S(1)}, bf16[32,48,256]{2,1,0:T(8,128)(2,1)S(1)}, u32[]{:S(2)}, u32[]{:S(2)}) %collective-permute-start.5) | collective-permute-done | bytes 786464 | tf_op jit(solution)/shard_map/ppermute | solution.py:326
  62.9 2.2 %shard_map.106 = (f32[128,256]{1,0:T(8,128)S(1)}, bf16[64,256]{1,0:T(8,128)(2,1)S(1)}, bf16[64,256]{1,0:T(8,128)(2,1)S(1)}) custom-call(f32[128,256]{1,0:T(8,128)S(1)} %shard_map.103.start, f32[5,256]{1,0:T(8,128)S(1)} %copy-done.3, bf16[32,48,256]{2,1,0:T(8,128)(2,1)S(1)} %bitcast.17, bf16[32,48,256]{2,1,0:T(8,128)(2,1)S(1)} %collective-permute-done.5.other), custom_call_target="tpu_custom_call" | custom-call | flops 201326592 | bytes 4194304 | tf_op jit(solution)/shard_map/pallas_call | solution.py:312
  65.2 3.0 %collective-permute-start.6 = (bf16[64,256]{1,0:T(8,128)(2,1)S(1)}, bf16[64,256]{1,0:T(8,128)(2,1)S(1)}, u32[]{:S(2)}, u32[]{:S(2)}) collective-permute-start(bf16[64,256]{1,0:T(8,128)(2,1)S(1)} %get-tuple-element.30), channel_id=1, source_target_pairs={{0,1},{1,0},{2,3},{3,2},{4,5},{5,4},{6,7},{7,6},{8,9},{9,8},{10,11... | collective-permute-start | bytes 98312 | tf_op jit(solution)/shard_map/ppermute | solution.py:428
  68.2 6.5 %collective-permute-start.7 = (bf16[64,256]{1,0:T(8,128)(2,1)S(1)}, bf16[64,256]{1,0:T(8,128)(2,1)S(1)}, u32[]{:S(2)}, u32[]{:S(2)}) collective-permute-start(bf16[64,256]{1,0:T(8,128)(2,1)S(1)} %get-tuple-element.31.refs_0_), channel_id=1, source_target_pairs={{1,2},{3,4},{5,6},{2,1},{4,3},{6,5},{7,264},{0,287},{9,10},{11,12}... | collective-permute-start | bytes 98312 | tf_op jit(solution)/shard_map/ppermute | solution.py:429
  74.8 2.8 %collective-permute-start.8 = (bf16[32,48,256]{2,1,0:T(8,128)(2,1)S(1)}, bf16[32,48,256]{2,1,0:T(8,128)(2,1)S(1)}, u32[]{:S(2)}, u32[]{:S(2)}) collective-permute-start(bf16[32,48,256]{2,1,0:T(8,128)(2,1)S(1)} %shard_map.108), channel_id=1, source_target_pairs={{0,32},{32,0},{1,33},{33,1},{2,34},{34,2},{3,35},{35,3},{4,36},{36... | collective-permute-start | bytes 2359304 | tf_op jit(solution)/shard_map/ppermute | solution.py:326
  77.7 0.2 shard_map.107.sides
  77.9 1.7 %collective-permute-done.8.other = bf16[32,48,256]{2,1,0:T(8,128)(2,1)S(1)} collective-permute-done((bf16[32,48,256]{2,1,0:T(8,128)(2,1)S(1)}, bf16[32,48,256]{2,1,0:T(8,128)(2,1)S(1)}, u32[]{:S(2)}, u32[]{:S(2)}) %collective-permute-start.8) | collective-permute-done | bytes 786464 | tf_op jit(solution)/shard_map/ppermute | solution.py:326
  79.5 3.2 %shard_map.109 = bf16[4,128,256]{2,1,0:T(8,128)(2,1)S(1)} custom-call(f32[128,256]{1,0:T(8,128)S(1)} %get-tuple-element.29.state, bf16[128,256]{1,0:T(8,128)(2,1)S(1)} %shard_map.107.sides, f32[5,256]{1,0:T(8,128)S(1)} %copy-done.3, bf16[32,48,256]{2,1,0:T(8,128)(2,1)S(1)} %bitcast.15, bf16[32,48,256]{2,1,0:T(8,128)(2,1)S(1)} %collective-permute-done.8.other), custom_call_target="tpu_custom_call" | custom-call | flops 201326592 | bytes 4194304 | tf_op jit(solution)/shard_map/pallas_call | solution.py:312
  82.7 9.5 %all_to_all.20 = bf16[4,128,256]{2,1,0:T(8,128)(2,1)S(1)} all-to-all(bf16[4,128,256]{2,1,0:T(8,128)(2,1)S(1)} %shard_map.109), channel_id=1, replica_groups=mesh['zh'=2,'y'=4,'core'=2,'x'=4,'zl'=8] {'y'}, dimensions={0} | all-to-all | bytes 524288 | tf_op jit(solution)/shard_map/all_to_all | solution.py:441
  92.3 3.7 %all-gather = bf16[8,128,256]{2,1,0:T(8,128)(2,1)S(1)} all-gather(bf16[4,128,256]{2,1,0:T(8,128)(2,1)S(1)} %all_to_all.20), channel_id=2, replica_groups=mesh['zh'=2,'y'=4,'core'=2,'x'=4,'zl'=8] {'core'}, dimensions={0}, use_global_device_ids=true | all-gather | bytes 786432 | tf_op jit(solution)/shard_map/all_gather | solution.py:441
  96.0 1.2 %shard_map.110 = bf16[2,1024,128]{2,1,0:T(8,128)(2,1)} custom-call(bf16[2,4,128,256]{3,2,1,0:T(8,128)(2,1)S(1)} %bitcast.18, bf16[2,256,128]{2,1,0:T(8,128)(2,1)S(1)} %copy-done.2), custom_call_target="tpu_custom_call" | custom-call | flops 134217728 | bytes 2097152 | tf_op jit(solution)/shard_map/pallas_call | solution.py:312
  (31 shorter events, 0.4 us)
Async XLA Ops:
  0.0 0.8 copy-start
  0.0 0.8 copy-start.5
  0.8 0.7 copy-start.6
  3.0 13.2 %copy-start.8 = (bf16[2,256]{1,0:T(2,128)(2,1)S(1)}, bf16[2,256]{1,0:T(2,128)(2,1)}, u32[]{:S(2)}) copy-start(bf16[2,256]{1,0:T(2,128)(2,1)} %param.12) | copy-start | bytes 3076
  3.0 13.3 %copy-start.4 = (bf16[2,128,256]{2,1,0:T(8,128)(2,1)S(1)}, bf16[2,128,256]{2,1,0:T(8,128)(2,1)}, u32[]{:S(2)}) copy-start(bf16[2,128,256]{2,1,0:T(8,128)(2,1)} %param.11) | copy-start | bytes 393220
  3.0 13.4 %copy-start.7 = (f32[256]{0:T(256)S(1)}, f32[256]{0:T(256)}, u32[]{:S(2)}) copy-start(f32[256]{0:T(256)} %param.13) | copy-start | bytes 3076
  3.0 30.6 %all-to-all-start = ((bf16[8,96,256]{2,1,0:T(8,128)(2,1)}), bf16[8,96,256]{2,1,0:T(8,128)(2,1)S(1)}, u32[]{:S(2)}, u32[]{:S(2)}) async-start(bf16[8,96,256]{2,1,0:T(8,128)(2,1)} %bitcast.6), calls=%async_computation | async-start | bytes 786432 | tf_op jit(solution)/shard_map/all_to_all | solution.py:373
  16.2 1.0 %copy-start.1 = (bf16[2,128,8,128]{3,2,1,0:T(8,128)(2,1)S(1)}, bf16[2,128,8,128]{3,2,1,0:T(8,128)(2,1)}, u32[]{:S(2)}) copy-start(bf16[2,128,8,128]{3,2,1,0:T(8,128)(2,1)} %param.10) | copy-start | bytes 1572868
  18.1 4.0 %collective-permute-start = (bf16[4,144,256]{2,1,0:T(8,128)(2,1)S(1)}, bf16[4,144,256]{2,1,0:T(8,128)(2,1)S(1)}, u32[]{:S(2)}, u32[]{:S(2)}) collective-permute-start(bf16[4,144,256]{2,1,0:T(8,128)(2,1)S(1)} %get-tuple-element.20), channel_id=1, source_target_pairs={{0,32},{32,0},{1,33},{33,1},{2,34},{34,2},{3,35},{35,3},{4,36},{36... | collective-permute-start | bytes 884744 | tf_op jit(solution)/shard_map/ppermute | solution.py:326
  22.6 16.3 %collective-permute-start.1 = (bf16[144,256]{1,0:T(8,128)(2,1)S(1)}, bf16[144,256]{1,0:T(8,128)(2,1)S(1)}, u32[]{:S(2)}, u32[]{:S(2)}) collective-permute-start(bf16[144,256]{1,0:T(8,128)(2,1)S(1)} %get-tuple-element.22), channel_id=1, source_target_pairs={{0,64},{64,128},{128,192},{192,0},{1,65},{65,129},{129,193},{193,1... | collective-permute-start | bytes 221192 | tf_op jit(solution)/shard_map/ppermute | solution.py:326
  25.8 13.1 %collective-permute-start.2 = (bf16[144,256]{1,0:T(8,128)(2,1)S(1)}, bf16[144,256]{1,0:T(8,128)(2,1)S(1)}, u32[]{:S(2)}, u32[]{:S(2)}) collective-permute-start(bf16[144,256]{1,0:T(8,128)(2,1)S(1)} %get-tuple-element.23), channel_id=1, source_target_pairs={{0,128},{64,192},{128,0},{192,64},{1,129},{65,193},{129,1},{193,65... | collective-permute-start | bytes 221192 | tf_op jit(solution)/shard_map/ppermute | solution.py:326
  30.4 8.5 %collective-permute-start.3 = (bf16[144,256]{1,0:T(8,128)(2,1)S(1)}, bf16[144,256]{1,0:T(8,128)(2,1)S(1)}, u32[]{:S(2)}, u32[]{:S(2)}) collective-permute-start(bf16[144,256]{1,0:T(8,128)(2,1)S(1)} %get-tuple-element.24), channel_id=1, source_target_pairs={{0,192},{64,0},{128,64},{192,128},{1,193},{65,1},{129,65},{193,129... | collective-permute-start | bytes 221192 | tf_op jit(solution)/shard_map/ppermute | solution.py:326
  34.9 12.4 %all-to-all-start.1 = ((bf16[4,8,48,256]{3,2,1,0:T(8,128)(2,1)}), bf16[4,8,48,256]{3,2,1,0:T(8,128)(2,1)S(1)}, u32[]{:S(2)}, u32[]{:S(2)}) async-start(bf16[4,8,48,256]{3,2,1,0:T(8,128)(2,1)} %get-tuple-element.28), calls=%async_computation.1 | async-start | bytes 1572864 | tf_op jit(solution)/shard_map/all_to_all | solution.py:409
  39.2 21.9 %collective-permute-start.4 = (bf16[144,256]{1,0:T(8,128)(2,1)S(1)}, bf16[144,256]{1,0:T(8,128)(2,1)S(1)}, u32[]{:S(2)}, u32[]{:S(2)}) collective-permute-start(bf16[144,256]{1,0:T(8,128)(2,1)S(1)} %get-tuple-element.27), channel_id=1, source_target_pairs={{0,256},{256,0},{1,257},{257,1},{2,258},{258,2},{3,259},{259,3},{4... | collective-permute-start | bytes 221192 | tf_op jit(solution)/shard_map/ppermute | solution.py:326
  47.2 27.5 %all-to-all-start.2 = ((bf16[4,8,48,256]{3,2,1,0:T(8,128)(2,1)}), bf16[4,8,48,256]{3,2,1,0:T(8,128)(2,1)S(1)}, u32[]{:S(2)}, u32[]{:S(2)}) async-start(bf16[4,8,48,256]{3,2,1,0:T(8,128)(2,1)} %get-tuple-element.32), calls=%async_computation.2 | async-start | bytes 1572864 | tf_op jit(solution)/shard_map/all_to_all | solution.py:410
  51.4 11.5 %collective-permute-start.5 = (bf16[32,48,256]{2,1,0:T(8,128)(2,1)S(1)}, bf16[32,48,256]{2,1,0:T(8,128)(2,1)S(1)}, u32[]{:S(2)}, u32[]{:S(2)}) collective-permute-start(bf16[32,48,256]{2,1,0:T(8,128)(2,1)S(1)} %bitcast.16), channel_id=1, source_target_pairs={{0,32},{32,0},{1,33},{33,1},{2,34},{34,2},{3,35},{35,3},{4,36},{36... | collective-permute-start | bytes 2359304 | tf_op jit(solution)/shard_map/ppermute | solution.py:326
  61.1 1.9 %copy-start.3 = (f32[5,256]{1,0:T(8,128)S(1)}, f32[5,256]{1,0:T(8,128)}, u32[]{:S(2)}) copy-start(f32[5,256]{1,0:T(8,128)} %gains.5) | copy-start | bytes 15364
  65.2 12.5 %collective-permute-start.6 = (bf16[64,256]{1,0:T(8,128)(2,1)S(1)}, bf16[64,256]{1,0:T(8,128)(2,1)S(1)}, u32[]{:S(2)}, u32[]{:S(2)}) collective-permute-start(bf16[64,256]{1,0:T(8,128)(2,1)S(1)} %get-tuple-element.30), channel_id=1, source_target_pairs={{0,1},{1,0},{2,3},{3,2},{4,5},{5,4},{6,7},{7,6},{8,9},{9,8},{10,11... | collective-permute-start | bytes 98312 | tf_op jit(solution)/shard_map/ppermute | solution.py:428
  68.2 9.4 %collective-permute-start.7 = (bf16[64,256]{1,0:T(8,128)(2,1)S(1)}, bf16[64,256]{1,0:T(8,128)(2,1)S(1)}, u32[]{:S(2)}, u32[]{:S(2)}) collective-permute-start(bf16[64,256]{1,0:T(8,128)(2,1)S(1)} %get-tuple-element.31.refs_0_), channel_id=1, source_target_pairs={{1,2},{3,4},{5,6},{2,1},{4,3},{6,5},{7,264},{0,287},{9,10},{11,12}... | collective-permute-start | bytes 98312 | tf_op jit(solution)/shard_map/ppermute | solution.py:429
  74.8 4.7 %collective-permute-start.8 = (bf16[32,48,256]{2,1,0:T(8,128)(2,1)S(1)}, bf16[32,48,256]{2,1,0:T(8,128)(2,1)S(1)}, u32[]{:S(2)}, u32[]{:S(2)}) collective-permute-start(bf16[32,48,256]{2,1,0:T(8,128)(2,1)S(1)} %shard_map.108), channel_id=1, source_target_pairs={{0,32},{32,0},{1,33},{33,1},{2,34},{34,2},{3,35},{35,3},{4,36},{36... | collective-permute-start | bytes 2359304 | tf_op jit(solution)/shard_map/ppermute | solution.py:326
  92.3 3.7 %copy-start.2 = (bf16[2,256,128]{2,1,0:T(8,128)(2,1)S(1)}, bf16[2,256,128]{2,1,0:T(8,128)(2,1)}, u32[]{:S(2)}) copy-start(bf16[2,256,128]{2,1,0:T(8,128)(2,1)} %weight.1) | copy-start | bytes 393220

commit v5 on v4

--- a/solution.py
+++ b/solution.py
@@ -204,7 +204,7 @@
     )
 
 
-def block0_kernel(start, gains, mine, other, state, near, far, qkv_rows, proj_rows):
+def block0_kernel(start, gains, mine, other, state, far, near, qkv_rows, proj_rows):
     n, width = start.shape
     x = start[...]
     w_qkv, w_proj = attention_weights(mine, other, qkv_rows, proj_rows)
@@ -223,7 +223,7 @@
     far[...] = half_tokens(short, odd)
 
 
-def sides_kernel(from_near, from_far, gains, out):
+def sides_kernel(from_far, from_near, gains, out):
     odd = (lax.axis_index("zl") & 1) == 1
     near, far = from_near[...].astype(F32), from_far[...].astype(F32)
     sides = jnp.concatenate([jnp.where(odd, near, far), jnp.where(odd, far, near)], axis=0)
@@ -276,7 +276,7 @@
         at += n
 
 
-def spread(parts, times, after=()):
+def spread(parts, times, after=(), flops=0):
     pieces, height, width = parts[0].shape
     total = sum(p.shape[0] for p in parts)
     vmem = pl.BlockSpec(memory_space=pltpu.VMEM)
@@ -289,7 +289,7 @@
         out_specs=[vmem] * len(times),
         compiler_params=pltpu.CompilerParams(vmem_limit_bytes=16 * 2**20),
         cost_estimate=pl.CostEstimate(
-            flops=0, bytes_accessed=2 * (1 + sum(times)) * total * height * width, transcendentals=0
+            flops=flops, bytes_accessed=2 * (1 + sum(times)) * total * height * width, transcendentals=0
         ),
     )(*parts, *after)
 
@@ -405,8 +405,9 @@
         ),
         flops=6 * 10**10,
     )(paired[0], *along)
-    copies0, copies1 = spread([near], (4, 4), after=(paired[0],))
+    copies0, near1 = spread([near], (4, 1), after=(paired[0],))
     mine0 = lax.all_to_all(copies0, "x", 0, 0, tiled=True).reshape(32, -1, width)
+    (copies1,) = spread([near1[0]], (4,), after=(mine0,), flops=0)
     mine1 = lax.all_to_all(copies1, "x", 0, 0, tiled=True).reshape(32, -1, width)
     partner = shifted(sent, "zh", 2, 1)
     other0 = shifted(mine0, "core", 2, 1)
@@ -417,7 +418,7 @@
     scratch = [pltpu.VMEM((3 * width, width), F32), pltpu.VMEM((width, width), F32)]
     half = jax.ShapeDtypeStruct((own // 2, width), BF16)
     block_flops = 2 * own * width * width * 12
-    state, to_near, to_far = on_core(
+    state, to_far, to_near = on_core(
         block0_kernel,
         (jax.ShapeDtypeStruct((own, width), F32), half, half),
         scratch,
@@ -425,12 +426,12 @@
         moved=4 * 2**20,
     )(start, norm_gains, mine0, other0)
     near_pairs, far_pairs = swaps()
+    from_far = lax.ppermute(to_far, ("zh", "x", "zl"), far_pairs)
     from_near = lax.ppermute(to_near, ("zh", "x", "zl"), near_pairs)
-    from_far = lax.ppermute(to_far, ("zh", "x", "zl"), far_pairs)
-    other1 = shifted(held_until(mine1, (to_far,)), "core", 2, 1)
+    other1 = shifted(held_until(mine1, (to_near,)), "core", 2, 1)
     sides = on_core(
         sides_kernel, jax.ShapeDtypeStruct((own, width), BF16), flops=6 * 10**10
-    )(from_near, from_far, norm_gains)
+    )(from_far, from_near, norm_gains)
     final = on_core(
         block1_kernel,
         jax.ShapeDtypeStruct((4, own, width), BF16),

time: 98.1 us -> 97.9 us (level)
  waiting for transfers between devices: 4.86 us -> 3.23 us
    ppermute x7, waiting for transfers between devices: 4.5 us -> 2.87 us  [shifted(): lax.ppermute(value, axes, [(i, (i + steps) % size) for i in range(size)])]
    ppermute x1, starting transfers between devices: 3.03 us -> 1.92 us  [body(): from_near = lax.ppermute(to_near, ('zh', 'x', 'zl'), near_pairs)]
    pallas_call x2 -> x3, Pallas kernels: 2.01 us -> 2.67 us  [spread(): pl.pallas_call(functools.partial(spread_kernel, len(parts), times), out_s...]
  transfers between devices with their start and end apart: 12 -> 12, of which waited for: 5 -> 4; matrix products, arithmetic and copies ran while one was open for 0% -> 0% of each run, Pallas kernels for 6% -> 6%
where the time goes in v5:
time: 97.9 us; the launch traced here: 97 us
  starting transfers between devices  64.8 us (66%)
  blocking collectives  13.7 us (14%)
  Pallas kernels  11.4 us (12%)
  waiting for transfers between devices  3.23 us (3%)
  local copies, waits for them, and re-layouts  2.78 us (3%)
    ppermute x7, starting transfers between devices, shifted(): lax.ppermute(value, axes, [(i, (i + steps) % size) for i in range(size)])  34.7 us
    all_to_all x1, starting transfers between devices, body(): near = lax.all_to_all(near.reshape(8, -1, width), 'zl', 0, 0, tiled=True)  13.2 us
    all_to_all x1, blocking collectives, body(): lax.all_to_all(final, 'y', 0, 0, tiled=True)  10 us
    pallas_call x9, Pallas kernels, call(): pl.pallas_call(kernel, out_shape=outs, in_specs=[anywhere] * len(far) + [...  8.72 us
    ppermute x1, starting transfers between devices, body(): from_far = lax.ppermute(to_far, ('zh', 'x', 'zl'), far_pairs)  7.36 us
    all_to_all x1, starting transfers between devices, body(): lax.all_to_all(copies0, 'x', 0, 0, tiled=True).reshape(32, -1, width)  4.01 us
    all_gather x1, blocking collectives, body(): lax.all_gather(lax.all_to_all(final, 'y', 0, 0, tiled=True), 'core')  3.74 us
    all_to_all x1, starting transfers between devices, body(): lax.all_to_all(copies1, 'x', 0, 0, tiled=True).reshape(32, -1, width)  3.58 us
  transfers between devices with their start and end apart: 12, of which 4 were waited for; matrix products, arithmetic and copies ran while one was open for 0% of the time, Pallas kernels for 6%

profile of v5, /device:TPU:1, one launch (start us, length us, event | category | flops | bytes accessed | tf_op | source)
XLA Modules:
  0.0 97.0 jit_solution(7963000466437788348)
XLA Ops:
  0.0 0.8 copy-done
  0.8 0.7 copy-done.6
  1.5 0.7 fusion
  2.2 0.8 shard_map.104
  3.0 13.2 %all-to-all-start = ((bf16[8,96,256]{2,1,0:T(8,128)(2,1)}), bf16[8,96,256]{2,1,0:T(8,128)(2,1)S(1)}, u32[]{:S(2)}, u32[]{:S(2)}) async-start(bf16[8,96,256]{2,1,0:T(8,128)(2,1)} %bitcast.6), calls=%async_computation | async-start | bytes 786432 | tf_op jit(solution)/shard_map/all_to_all | solution.py:373
  16.5 0.8 copy-done.1
  17.2 0.9 shard_map.100
  18.1 2.9 %collective-permute-start = (bf16[4,144,256]{2,1,0:T(8,128)(2,1)S(1)}, bf16[4,144,256]{2,1,0:T(8,128)(2,1)S(1)}, u32[]{:S(2)}, u32[]{:S(2)}) collective-permute-start(bf16[4,144,256]{2,1,0:T(8,128)(2,1)S(1)} %get-tuple-element.20), channel_id=1, source_target_pairs={{0,32},{32,0},{1,33},{33,1},{2,34},{34,2},{3,35},{35,3},{4,36},{36... | collective-permute-start | bytes 884744 | tf_op jit(solution)/shard_map/ppermute | solution.py:326
  21.0 1.2 %collective-permute-done.got = bf16[4,144,256]{2,1,0:T(8,128)(2,1)S(1)} collective-permute-done((bf16[4,144,256]{2,1,0:T(8,128)(2,1)S(1)}, bf16[4,144,256]{2,1,0:T(8,128)(2,1)S(1)}, u32[]{:S(2)}, u32[]{:S(2)}) %collective-permute-start) | collective-permute-done | bytes 294944 | tf_op jit(solution)/shard_map/ppermute | solution.py:326
  22.2 0.5 shard_map.101
  22.6 3.2 %collective-permute-start.1 = (bf16[144,256]{1,0:T(8,128)(2,1)S(1)}, bf16[144,256]{1,0:T(8,128)(2,1)S(1)}, u32[]{:S(2)}, u32[]{:S(2)}) collective-permute-start(bf16[144,256]{1,0:T(8,128)(2,1)S(1)} %get-tuple-element.22), channel_id=1, source_target_pairs={{0,64},{64,128},{128,192},{192,0},{1,65},{65,129},{129,193},{193,1... | collective-permute-start | bytes 221192 | tf_op jit(solution)/shard_map/ppermute | solution.py:326
  25.8 4.5 %collective-permute-start.2 = (bf16[144,256]{1,0:T(8,128)(2,1)S(1)}, bf16[144,256]{1,0:T(8,128)(2,1)S(1)}, u32[]{:S(2)}, u32[]{:S(2)}) collective-permute-start(bf16[144,256]{1,0:T(8,128)(2,1)S(1)} %get-tuple-element.23), channel_id=1, source_target_pairs={{0,128},{64,192},{128,0},{192,64},{1,129},{65,193},{129,1},{193,65... | collective-permute-start | bytes 221192 | tf_op jit(solution)/shard_map/ppermute | solution.py:326
  30.4 3.0 %collective-permute-start.3 = (bf16[144,256]{1,0:T(8,128)(2,1)S(1)}, bf16[144,256]{1,0:T(8,128)(2,1)S(1)}, u32[]{:S(2)}, u32[]{:S(2)}) collective-permute-start(bf16[144,256]{1,0:T(8,128)(2,1)S(1)} %get-tuple-element.24), channel_id=1, source_target_pairs={{0,192},{64,0},{128,64},{192,128},{1,193},{65,1},{129,65},{193,129... | collective-permute-start | bytes 221192 | tf_op jit(solution)/shard_map/ppermute | solution.py:326
  33.4 0.3 all-to-all-done.refs_0_
  33.6 1.0 shard_map.105
  34.6 4.0 %all-to-all-start.1 = ((bf16[4,8,48,256]{3,2,1,0:T(8,128)(2,1)}), bf16[4,8,48,256]{3,2,1,0:T(8,128)(2,1)S(1)}, u32[]{:S(2)}, u32[]{:S(2)}) async-start(bf16[4,8,48,256]{3,2,1,0:T(8,128)(2,1)} %get-tuple-element.28), calls=%async_computation.1 | async-start | bytes 1572864 | tf_op jit(solution)/shard_map/all_to_all | solution.py:409
  38.6 0.3 shard_map.102
  38.9 7.9 %collective-permute-start.4 = (bf16[144,256]{1,0:T(8,128)(2,1)S(1)}, bf16[144,256]{1,0:T(8,128)(2,1)S(1)}, u32[]{:S(2)}, u32[]{:S(2)}) collective-permute-start(bf16[144,256]{1,0:T(8,128)(2,1)S(1)} %get-tuple-element.27), channel_id=1, source_target_pairs={{0,256},{256,0},{1,257},{257,1},{2,258},{258,2},{3,259},{259,3},{4... | collective-permute-start | bytes 221192 | tf_op jit(solution)/shard_map/ppermute | solution.py:326
  46.9 10.0 %collective-permute-start.5 = (bf16[32,48,256]{2,1,0:T(8,128)(2,1)S(1)}, bf16[32,48,256]{2,1,0:T(8,128)(2,1)S(1)}, u32[]{:S(2)}, u32[]{:S(2)}) collective-permute-start(bf16[32,48,256]{2,1,0:T(8,128)(2,1)S(1)} %bitcast.15), channel_id=1, source_target_pairs={{0,32},{32,0},{1,33},{33,1},{2,34},{34,2},{3,35},{35,3},{4,36},{36... | collective-permute-start | bytes 2359304 | tf_op jit(solution)/shard_map/ppermute | solution.py:326
  56.9 0.9 shard_map.108
  57.8 3.6 %all-to-all-start.2 = ((bf16[4,8,48,256]{3,2,1,0:T(8,128)(2,1)}), bf16[4,8,48,256]{3,2,1,0:T(8,128)(2,1)S(1)}, u32[]{:S(2)}, u32[]{:S(2)}) async-start(bf16[4,8,48,256]{3,2,1,0:T(8,128)(2,1)} %shard_map.108), calls=%async_computation.2 | async-start | bytes 1572864 | tf_op jit(solution)/shard_map/all_to_all | solution.py:411
  61.4 0.2 shard_map.103.start
  61.7 0.4 copy-done.3
  62.1 2.2 %shard_map.106 = (f32[128,256]{1,0:T(8,128)S(1)}, bf16[64,256]{1,0:T(8,128)(2,1)S(1)}, bf16[64,256]{1,0:T(8,128)(2,1)S(1)}) custom-call(f32[128,256]{1,0:T(8,128)S(1)} %shard_map.103.start, f32[5,256]{1,0:T(8,128)S(1)} %copy-done.3, bf16[32,48,256]{2,1,0:T(8,128)(2,1)S(1)} %bitcast.17, bf16[32,48,256]{2,1,0:T(8,128)(2,1)S(1)} %collective-permute-done.5.other), custom_call_target="tpu_custom_call" | custom-call | flops 201326592 | bytes 4194304 | tf_op jit(solution)/shard_map/pallas_call | solution.py:312
  64.4 7.4 %collective-permute-start.6 = (bf16[64,256]{1,0:T(8,128)(2,1)S(1)}, bf16[64,256]{1,0:T(8,128)(2,1)S(1)}, u32[]{:S(2)}, u32[]{:S(2)}) collective-permute-start(bf16[64,256]{1,0:T(8,128)(2,1)S(1)} %get-tuple-element.30), channel_id=1, source_target_pairs={{1,2},{3,4},{5,6},{2,1},{4,3},{6,5},{7,264},{0,287},{9,10},{11,12}... | collective-permute-start | bytes 98312 | tf_op jit(solution)/shard_map/ppermute | solution.py:429
  71.7 1.9 %collective-permute-start.7 = (bf16[64,256]{1,0:T(8,128)(2,1)S(1)}, bf16[64,256]{1,0:T(8,128)(2,1)S(1)}, u32[]{:S(2)}, u32[]{:S(2)}) collective-permute-start(bf16[64,256]{1,0:T(8,128)(2,1)S(1)} %get-tuple-element.31.refs_0_), channel_id=1, source_target_pairs={{0,1},{1,0},{2,3},{3,2},{4,5},{5,4},{6,7},{7,6},{8,9},{9,8},{10,11... | collective-permute-start | bytes 98312 | tf_op jit(solution)/shard_map/ppermute | solution.py:430
  73.7 3.3 %collective-permute-start.8 = (bf16[32,48,256]{2,1,0:T(8,128)(2,1)S(1)}, bf16[32,48,256]{2,1,0:T(8,128)(2,1)S(1)}, u32[]{:S(2)}, u32[]{:S(2)}) collective-permute-start(bf16[32,48,256]{2,1,0:T(8,128)(2,1)S(1)} %shard_map.109), channel_id=1, source_target_pairs={{0,32},{32,0},{1,33},{33,1},{2,34},{34,2},{3,35},{35,3},{4,36},{36... | collective-permute-start | bytes 2359304 | tf_op jit(solution)/shard_map/ppermute | solution.py:326
  77.2 1.7 %collective-permute-done.8.other = bf16[32,48,256]{2,1,0:T(8,128)(2,1)S(1)} collective-permute-done((bf16[32,48,256]{2,1,0:T(8,128)(2,1)S(1)}, bf16[32,48,256]{2,1,0:T(8,128)(2,1)S(1)}, u32[]{:S(2)}, u32[]{:S(2)}) %collective-permute-start.8) | collective-permute-done | bytes 786464 | tf_op jit(solution)/shard_map/ppermute | solution.py:326
  78.9 3.2 %shard_map.110 = bf16[4,128,256]{2,1,0:T(8,128)(2,1)S(1)} custom-call(f32[128,256]{1,0:T(8,128)S(1)} %get-tuple-element.29.state, bf16[128,256]{1,0:T(8,128)(2,1)S(1)} %shard_map.107.sides, f32[5,256]{1,0:T(8,128)S(1)} %copy-done.3, bf16[32,48,256]{2,1,0:T(8,128)(2,1)S(1)} %bitcast.19, bf16[32,48,256]{2,1,0:T(8,128)(2,1)S(1)} %collective-permute-done.8.other), custom_call_target="tpu_custom_call" | custom-call | flops 201326592 | bytes 4194304 | tf_op jit(solution)/shard_map/pallas_call | solution.py:312
  82.1 10.0 %all_to_all.20 = bf16[4,128,256]{2,1,0:T(8,128)(2,1)S(1)} all-to-all(bf16[4,128,256]{2,1,0:T(8,128)(2,1)S(1)} %shard_map.110), channel_id=1, replica_groups=mesh['zh'=2,'y'=4,'core'=2,'x'=4,'zl'=8] {'y'}, dimensions={0} | all-to-all | bytes 524288 | tf_op jit(solution)/shard_map/all_to_all | solution.py:442
  92.1 3.7 %all-gather = bf16[8,128,256]{2,1,0:T(8,128)(2,1)S(1)} all-gather(bf16[4,128,256]{2,1,0:T(8,128)(2,1)S(1)} %all_to_all.20), channel_id=2, replica_groups=mesh['zh'=2,'y'=4,'core'=2,'x'=4,'zl'=8] {'core'}, dimensions={0}, use_global_device_ids=true | all-gather | bytes 786432 | tf_op jit(solution)/shard_map/all_gather | solution.py:442
  95.8 1.2 %shard_map.111 = bf16[2,1024,128]{2,1,0:T(8,128)(2,1)} custom-call(bf16[2,4,128,256]{3,2,1,0:T(8,128)(2,1)S(1)} %bitcast.20, bf16[2,256,128]{2,1,0:T(8,128)(2,1)S(1)} %copy-done.2), custom_call_target="tpu_custom_call" | custom-call | flops 134217728 | bytes 2097152 | tf_op jit(solution)/shard_map/pallas_call | solution.py:312
  (32 shorter events, 0.6 us)
Async XLA Ops:
  0.0 0.8 copy-start
  0.0 0.8 copy-start.5
  0.8 0.7 copy-start.6
  3.0 13.2 %copy-start.8 = (bf16[2,256]{1,0:T(2,128)(2,1)S(1)}, bf16[2,256]{1,0:T(2,128)(2,1)}, u32[]{:S(2)}) copy-start(bf16[2,256]{1,0:T(2,128)(2,1)} %param.12) | copy-start | bytes 3076
  3.0 13.3 %copy-start.4 = (bf16[2,128,256]{2,1,0:T(8,128)(2,1)S(1)}, bf16[2,128,256]{2,1,0:T(8,128)(2,1)}, u32[]{:S(2)}) copy-start(bf16[2,128,256]{2,1,0:T(8,128)(2,1)} %param.11) | copy-start | bytes 393220
  3.0 13.4 %copy-start.7 = (f32[256]{0:T(256)S(1)}, f32[256]{0:T(256)}, u32[]{:S(2)}) copy-start(f32[256]{0:T(256)} %param.13) | copy-start | bytes 3076
  3.0 30.6 %all-to-all-start = ((bf16[8,96,256]{2,1,0:T(8,128)(2,1)}), bf16[8,96,256]{2,1,0:T(8,128)(2,1)S(1)}, u32[]{:S(2)}, u32[]{:S(2)}) async-start(bf16[8,96,256]{2,1,0:T(8,128)(2,1)} %bitcast.6), calls=%async_computation | async-start | bytes 786432 | tf_op jit(solution)/shard_map/all_to_all | solution.py:373
  16.2 1.0 %copy-start.1 = (bf16[2,128,8,128]{3,2,1,0:T(8,128)(2,1)S(1)}, bf16[2,128,8,128]{3,2,1,0:T(8,128)(2,1)}, u32[]{:S(2)}) copy-start(bf16[2,128,8,128]{3,2,1,0:T(8,128)(2,1)} %param.10) | copy-start | bytes 1572868
  18.1 4.0 %collective-permute-start = (bf16[4,144,256]{2,1,0:T(8,128)(2,1)S(1)}, bf16[4,144,256]{2,1,0:T(8,128)(2,1)S(1)}, u32[]{:S(2)}, u32[]{:S(2)}) collective-permute-start(bf16[4,144,256]{2,1,0:T(8,128)(2,1)S(1)} %get-tuple-element.20), channel_id=1, source_target_pairs={{0,32},{32,0},{1,33},{33,1},{2,34},{34,2},{3,35},{35,3},{4,36},{36... | collective-permute-start | bytes 884744 | tf_op jit(solution)/shard_map/ppermute | solution.py:326
  22.6 16.0 %collective-permute-start.1 = (bf16[144,256]{1,0:T(8,128)(2,1)S(1)}, bf16[144,256]{1,0:T(8,128)(2,1)S(1)}, u32[]{:S(2)}, u32[]{:S(2)}) collective-permute-start(bf16[144,256]{1,0:T(8,128)(2,1)S(1)} %get-tuple-element.22), channel_id=1, source_target_pairs={{0,64},{64,128},{128,192},{192,0},{1,65},{65,129},{129,193},{193,1... | collective-permute-start | bytes 221192 | tf_op jit(solution)/shard_map/ppermute | solution.py:326
  25.8 12.8 %collective-permute-start.2 = (bf16[144,256]{1,0:T(8,128)(2,1)S(1)}, bf16[144,256]{1,0:T(8,128)(2,1)S(1)}, u32[]{:S(2)}, u32[]{:S(2)}) collective-permute-start(bf16[144,256]{1,0:T(8,128)(2,1)S(1)} %get-tuple-element.23), channel_id=1, source_target_pairs={{0,128},{64,192},{128,0},{192,64},{1,129},{65,193},{129,1},{193,65... | collective-permute-start | bytes 221192 | tf_op jit(solution)/shard_map/ppermute | solution.py:326
  30.4 8.2 %collective-permute-start.3 = (bf16[144,256]{1,0:T(8,128)(2,1)S(1)}, bf16[144,256]{1,0:T(8,128)(2,1)S(1)}, u32[]{:S(2)}, u32[]{:S(2)}) collective-permute-start(bf16[144,256]{1,0:T(8,128)(2,1)S(1)} %get-tuple-element.24), channel_id=1, source_target_pairs={{0,192},{64,0},{128,64},{192,128},{1,193},{65,1},{129,65},{193,129... | collective-permute-start | bytes 221192 | tf_op jit(solution)/shard_map/ppermute | solution.py:326
  34.6 12.4 %all-to-all-start.1 = ((bf16[4,8,48,256]{3,2,1,0:T(8,128)(2,1)}), bf16[4,8,48,256]{3,2,1,0:T(8,128)(2,1)S(1)}, u32[]{:S(2)}, u32[]{:S(2)}) async-start(bf16[4,8,48,256]{3,2,1,0:T(8,128)(2,1)} %get-tuple-element.28), calls=%async_computation.1 | async-start | bytes 1572864 | tf_op jit(solution)/shard_map/all_to_all | solution.py:409
  38.9 22.5 %collective-permute-start.4 = (bf16[144,256]{1,0:T(8,128)(2,1)S(1)}, bf16[144,256]{1,0:T(8,128)(2,1)S(1)}, u32[]{:S(2)}, u32[]{:S(2)}) collective-permute-start(bf16[144,256]{1,0:T(8,128)(2,1)S(1)} %get-tuple-element.27), channel_id=1, source_target_pairs={{0,256},{256,0},{1,257},{257,1},{2,258},{258,2},{3,259},{259,3},{4... | collective-permute-start | bytes 221192 | tf_op jit(solution)/shard_map/ppermute | solution.py:326
  46.9 14.7 %collective-permute-start.5 = (bf16[32,48,256]{2,1,0:T(8,128)(2,1)S(1)}, bf16[32,48,256]{2,1,0:T(8,128)(2,1)S(1)}, u32[]{:S(2)}, u32[]{:S(2)}) collective-permute-start(bf16[32,48,256]{2,1,0:T(8,128)(2,1)S(1)} %bitcast.15), channel_id=1, source_target_pairs={{0,32},{32,0},{1,33},{33,1},{2,34},{34,2},{3,35},{35,3},{4,36},{36... | collective-permute-start | bytes 2359304 | tf_op jit(solution)/shard_map/ppermute | solution.py:326
  57.8 15.8 %all-to-all-start.2 = ((bf16[4,8,48,256]{3,2,1,0:T(8,128)(2,1)}), bf16[4,8,48,256]{3,2,1,0:T(8,128)(2,1)S(1)}, u32[]{:S(2)}, u32[]{:S(2)}) async-start(bf16[4,8,48,256]{3,2,1,0:T(8,128)(2,1)} %shard_map.108), calls=%async_computation.2 | async-start | bytes 1572864 | tf_op jit(solution)/shard_map/all_to_all | solution.py:411
  61.4 0.7 copy-start.3
  64.4 12.6 %collective-permute-start.6 = (bf16[64,256]{1,0:T(8,128)(2,1)S(1)}, bf16[64,256]{1,0:T(8,128)(2,1)S(1)}, u32[]{:S(2)}, u32[]{:S(2)}) collective-permute-start(bf16[64,256]{1,0:T(8,128)(2,1)S(1)} %get-tuple-element.30), channel_id=1, source_target_pairs={{1,2},{3,4},{5,6},{2,1},{4,3},{6,5},{7,264},{0,287},{9,10},{11,12}... | collective-permute-start | bytes 98312 | tf_op jit(solution)/shard_map/ppermute | solution.py:429
  71.7 5.3 %collective-permute-start.7 = (bf16[64,256]{1,0:T(8,128)(2,1)S(1)}, bf16[64,256]{1,0:T(8,128)(2,1)S(1)}, u32[]{:S(2)}, u32[]{:S(2)}) collective-permute-start(bf16[64,256]{1,0:T(8,128)(2,1)S(1)} %get-tuple-element.31.refs_0_), channel_id=1, source_target_pairs={{0,1},{1,0},{2,3},{3,2},{4,5},{5,4},{6,7},{7,6},{8,9},{9,8},{10,11... | collective-permute-start | bytes 98312 | tf_op jit(solution)/shard_map/ppermute | solution.py:430
  73.7 5.1 %collective-permute-start.8 = (bf16[32,48,256]{2,1,0:T(8,128)(2,1)S(1)}, bf16[32,48,256]{2,1,0:T(8,128)(2,1)S(1)}, u32[]{:S(2)}, u32[]{:S(2)}) collective-permute-start(bf16[32,48,256]{2,1,0:T(8,128)(2,1)S(1)} %shard_map.109), channel_id=1, source_target_pairs={{0,32},{32,0},{1,33},{33,1},{2,34},{34,2},{3,35},{35,3},{4,36},{36... | collective-permute-start | bytes 2359304 | tf_op jit(solution)/shard_map/ppermute | solution.py:326
  92.1 3.7 %copy-start.2 = (bf16[2,256,128]{2,1,0:T(8,128)(2,1)S(1)}, bf16[2,256,128]{2,1,0:T(8,128)(2,1)}, u32[]{:S(2)}) copy-start(bf16[2,256,128]{2,1,0:T(8,128)(2,1)} %weight.1) | copy-start | bytes 393220

commit v6 on v5

--- a/solution.py
+++ b/solution.py
@@ -292,17 +292,6 @@
             flops=flops, bytes_accessed=2 * (1 + sum(times)) * total * height * width, transcendentals=0
         ),
     )(*parts, *after)
-
-
-def copy_kernel(value, *refs):
-    for k in range(value.shape[0]):
-        refs[-1][k] = value[k]
-
-
-def held_until(value, after):
-    return on_core(copy_kernel, jax.ShapeDtypeStruct(value.shape, value.dtype), moved=2**20)(
-        value, *after
-    )
 
 
 def on_core(kernel, outs, scratch=(), flops=0, moved=0, far=()):
@@ -428,7 +417,7 @@
     near_pairs, far_pairs = swaps()
     from_far = lax.ppermute(to_far, ("zh", "x", "zl"), far_pairs)
     from_near = lax.ppermute(to_near, ("zh", "x", "zl"), near_pairs)
-    other1 = shifted(held_until(mine1, (to_near,)), "core", 2, 1)
+    other1 = shifted(mine1, "core", 2, 1)
     sides = on_core(
         sides_kernel, jax.ShapeDtypeStruct((own, width), BF16), flops=6 * 10**10
     )(from_far, from_near, norm_gains)

time: 97.9 us -> 97.8 us (level)
    pallas_call x9 -> x8, Pallas kernels: 8.72 us -> 8.66 us  [call(): pl.pallas_call(kernel, out_shape=outs, in_specs=[anywhere] * len(far) + [...]
where the time goes in v6:
time: 97.8 us; the launch traced here: 97 us
  starting transfers between devices  64.8 us (66%)
  blocking collectives  13.7 us (14%)
  Pallas kernels  11.3 us (12%)
  waiting for transfers between devices  3.23 us (3%)
  local copies, waits for them, and re-layouts  2.78 us (3%)
    ppermute x7, starting transfers between devices, shifted(): lax.ppermute(value, axes, [(i, (i + steps) % size) for i in range(size)])  34.7 us
    all_to_all x1, starting transfers between devices, body(): near = lax.all_to_all(near.reshape(8, -1, width), 'zl', 0, 0, tiled=True)  13.2 us
    all_to_all x1, blocking collectives, body(): lax.all_to_all(final, 'y', 0, 0, tiled=True)  9.99 us
    pallas_call x8, Pallas kernels, call(): pl.pallas_call(kernel, out_shape=outs, in_specs=[anywhere] * len(far) + [...  8.66 us
    ppermute x1, starting transfers between devices, body(): from_far = lax.ppermute(to_far, ('zh', 'x', 'zl'), far_pairs)  7.36 us
    all_to_all x1, starting transfers between devices, body(): lax.all_to_all(copies0, 'x', 0, 0, tiled=True).reshape(32, -1, width)  4.01 us
    all_gather x1, blocking collectives, body(): lax.all_gather(lax.all_to_all(final, 'y', 0, 0, tiled=True), 'core')  3.74 us
    all_to_all x1, starting transfers between devices, body(): lax.all_to_all(copies1, 'x', 0, 0, tiled=True).reshape(32, -1, width)  3.58 us
  transfers between devices with their start and end apart: 12, of which 4 were waited for; matrix products, arithmetic and copies ran while one was open for 0% of the time, Pallas kernels for 6%

profile of v6, /device:TPU:1, one launch (start us, length us, event | category | flops | bytes accessed | tf_op | source)
XLA Modules:
  0.0 97.0 jit_solution(15857558163140637150)
XLA Ops:
  0.0 0.8 copy-done
  0.8 0.7 copy-done.6
  1.5 0.7 fusion
  2.2 0.8 shard_map.104
  3.0 13.2 %all-to-all-start = ((bf16[8,96,256]{2,1,0:T(8,128)(2,1)}), bf16[8,96,256]{2,1,0:T(8,128)(2,1)S(1)}, u32[]{:S(2)}, u32[]{:S(2)}) async-start(bf16[8,96,256]{2,1,0:T(8,128)(2,1)} %bitcast.6), calls=%async_computation | async-start | bytes 786432 | tf_op jit(solution)/shard_map/all_to_all | solution.py:362
  16.5 0.8 copy-done.1
  17.2 0.9 shard_map.100
  18.1 2.9 %collective-permute-start = (bf16[4,144,256]{2,1,0:T(8,128)(2,1)S(1)}, bf16[4,144,256]{2,1,0:T(8,128)(2,1)S(1)}, u32[]{:S(2)}, u32[]{:S(2)}) collective-permute-start(bf16[4,144,256]{2,1,0:T(8,128)(2,1)S(1)} %get-tuple-element.20), channel_id=1, source_target_pairs={{0,32},{32,0},{1,33},{33,1},{2,34},{34,2},{3,35},{35,3},{4,36},{36... | collective-permute-start | bytes 884744 | tf_op jit(solution)/shard_map/ppermute | solution.py:315
  21.0 1.2 %collective-permute-done.got = bf16[4,144,256]{2,1,0:T(8,128)(2,1)S(1)} collective-permute-done((bf16[4,144,256]{2,1,0:T(8,128)(2,1)S(1)}, bf16[4,144,256]{2,1,0:T(8,128)(2,1)S(1)}, u32[]{:S(2)}, u32[]{:S(2)}) %collective-permute-start) | collective-permute-done | bytes 294944 | tf_op jit(solution)/shard_map/ppermute | solution.py:315
  22.2 0.5 shard_map.101
  22.6 3.2 %collective-permute-start.1 = (bf16[144,256]{1,0:T(8,128)(2,1)S(1)}, bf16[144,256]{1,0:T(8,128)(2,1)S(1)}, u32[]{:S(2)}, u32[]{:S(2)}) collective-permute-start(bf16[144,256]{1,0:T(8,128)(2,1)S(1)} %get-tuple-element.22), channel_id=1, source_target_pairs={{0,64},{64,128},{128,192},{192,0},{1,65},{65,129},{129,193},{193,1... | collective-permute-start | bytes 221192 | tf_op jit(solution)/shard_map/ppermute | solution.py:315
  25.8 4.5 %collective-permute-start.2 = (bf16[144,256]{1,0:T(8,128)(2,1)S(1)}, bf16[144,256]{1,0:T(8,128)(2,1)S(1)}, u32[]{:S(2)}, u32[]{:S(2)}) collective-permute-start(bf16[144,256]{1,0:T(8,128)(2,1)S(1)} %get-tuple-element.23), channel_id=1, source_target_pairs={{0,128},{64,192},{128,0},{192,64},{1,129},{65,193},{129,1},{193,65... | collective-permute-start | bytes 221192 | tf_op jit(solution)/shard_map/ppermute | solution.py:315
  30.4 3.0 %collective-permute-start.3 = (bf16[144,256]{1,0:T(8,128)(2,1)S(1)}, bf16[144,256]{1,0:T(8,128)(2,1)S(1)}, u32[]{:S(2)}, u32[]{:S(2)}) collective-permute-start(bf16[144,256]{1,0:T(8,128)(2,1)S(1)} %get-tuple-element.24), channel_id=1, source_target_pairs={{0,192},{64,0},{128,64},{192,128},{1,193},{65,1},{129,65},{193,129... | collective-permute-start | bytes 221192 | tf_op jit(solution)/shard_map/ppermute | solution.py:315
  33.4 0.3 all-to-all-done.refs_0_
  33.6 1.0 shard_map.105
  34.6 4.0 %all-to-all-start.1 = ((bf16[4,8,48,256]{3,2,1,0:T(8,128)(2,1)}), bf16[4,8,48,256]{3,2,1,0:T(8,128)(2,1)S(1)}, u32[]{:S(2)}, u32[]{:S(2)}) async-start(bf16[4,8,48,256]{3,2,1,0:T(8,128)(2,1)} %get-tuple-element.28), calls=%async_computation.1 | async-start | bytes 1572864 | tf_op jit(solution)/shard_map/all_to_all | solution.py:398
  38.6 0.3 shard_map.102
  38.9 7.9 %collective-permute-start.4 = (bf16[144,256]{1,0:T(8,128)(2,1)S(1)}, bf16[144,256]{1,0:T(8,128)(2,1)S(1)}, u32[]{:S(2)}, u32[]{:S(2)}) collective-permute-start(bf16[144,256]{1,0:T(8,128)(2,1)S(1)} %get-tuple-element.27), channel_id=1, source_target_pairs={{0,256},{256,0},{1,257},{257,1},{2,258},{258,2},{3,259},{259,3},{4... | collective-permute-start | bytes 221192 | tf_op jit(solution)/shard_map/ppermute | solution.py:315
  46.9 10.0 %collective-permute-start.5 = (bf16[32,48,256]{2,1,0:T(8,128)(2,1)S(1)}, bf16[32,48,256]{2,1,0:T(8,128)(2,1)S(1)}, u32[]{:S(2)}, u32[]{:S(2)}) collective-permute-start(bf16[32,48,256]{2,1,0:T(8,128)(2,1)S(1)} %bitcast.15), channel_id=1, source_target_pairs={{0,32},{32,0},{1,33},{33,1},{2,34},{34,2},{3,35},{35,3},{4,36},{36... | collective-permute-start | bytes 2359304 | tf_op jit(solution)/shard_map/ppermute | solution.py:315
  56.9 0.9 shard_map.108
  57.8 3.6 %all-to-all-start.2 = ((bf16[4,8,48,256]{3,2,1,0:T(8,128)(2,1)}), bf16[4,8,48,256]{3,2,1,0:T(8,128)(2,1)S(1)}, u32[]{:S(2)}, u32[]{:S(2)}) async-start(bf16[4,8,48,256]{3,2,1,0:T(8,128)(2,1)} %shard_map.108), calls=%async_computation.2 | async-start | bytes 1572864 | tf_op jit(solution)/shard_map/all_to_all | solution.py:400
  61.4 0.2 shard_map.103.start
  61.7 0.4 copy-done.3
  62.1 2.2 %shard_map.106 = (f32[128,256]{1,0:T(8,128)S(1)}, bf16[64,256]{1,0:T(8,128)(2,1)S(1)}, bf16[64,256]{1,0:T(8,128)(2,1)S(1)}) custom-call(f32[128,256]{1,0:T(8,128)S(1)} %shard_map.103.start, f32[5,256]{1,0:T(8,128)S(1)} %copy-done.3, bf16[32,48,256]{2,1,0:T(8,128)(2,1)S(1)} %bitcast.17, bf16[32,48,256]{2,1,0:T(8,128)(2,1)S(1)} %collective-permute-done.5.other), custom_call_target="tpu_custom_call" | custom-call | flops 201326592 | bytes 4194304 | tf_op jit(solution)/shard_map/pallas_call | solution.py:301
  64.4 7.4 %collective-permute-start.6 = (bf16[64,256]{1,0:T(8,128)(2,1)S(1)}, bf16[64,256]{1,0:T(8,128)(2,1)S(1)}, u32[]{:S(2)}, u32[]{:S(2)}) collective-permute-start(bf16[64,256]{1,0:T(8,128)(2,1)S(1)} %get-tuple-element.30), channel_id=1, source_target_pairs={{1,2},{3,4},{5,6},{2,1},{4,3},{6,5},{7,264},{0,287},{9,10},{11,12}... | collective-permute-start | bytes 98312 | tf_op jit(solution)/shard_map/ppermute | solution.py:418
  71.7 1.9 %collective-permute-start.7 = (bf16[64,256]{1,0:T(8,128)(2,1)S(1)}, bf16[64,256]{1,0:T(8,128)(2,1)S(1)}, u32[]{:S(2)}, u32[]{:S(2)}) collective-permute-start(bf16[64,256]{1,0:T(8,128)(2,1)S(1)} %get-tuple-element.31), channel_id=1, source_target_pairs={{0,1},{1,0},{2,3},{3,2},{4,5},{5,4},{6,7},{7,6},{8,9},{9,8},{10,11... | collective-permute-start | bytes 98312 | tf_op jit(solution)/shard_map/ppermute | solution.py:419
  73.7 3.2 %collective-permute-start.8 = (bf16[32,48,256]{2,1,0:T(8,128)(2,1)S(1)}, bf16[32,48,256]{2,1,0:T(8,128)(2,1)S(1)}, u32[]{:S(2)}, u32[]{:S(2)}) collective-permute-start(bf16[32,48,256]{2,1,0:T(8,128)(2,1)S(1)} %bitcast.18), channel_id=1, source_target_pairs={{0,32},{32,0},{1,33},{33,1},{2,34},{34,2},{3,35},{35,3},{4,36},{36... | collective-permute-start | bytes 2359304 | tf_op jit(solution)/shard_map/ppermute | solution.py:315
  77.1 1.7 %collective-permute-done.8.other = bf16[32,48,256]{2,1,0:T(8,128)(2,1)S(1)} collective-permute-done((bf16[32,48,256]{2,1,0:T(8,128)(2,1)S(1)}, bf16[32,48,256]{2,1,0:T(8,128)(2,1)S(1)}, u32[]{:S(2)}, u32[]{:S(2)}) %collective-permute-start.8) | collective-permute-done | bytes 786464 | tf_op jit(solution)/shard_map/ppermute | solution.py:315
  78.8 3.2 %shard_map.109 = bf16[4,128,256]{2,1,0:T(8,128)(2,1)S(1)} custom-call(f32[128,256]{1,0:T(8,128)S(1)} %get-tuple-element.29.state, bf16[128,256]{1,0:T(8,128)(2,1)S(1)} %shard_map.107.sides, f32[5,256]{1,0:T(8,128)S(1)} %copy-done.3, bf16[32,48,256]{2,1,0:T(8,128)(2,1)S(1)} %bitcast.19, bf16[32,48,256]{2,1,0:T(8,128)(2,1)S(1)} %collective-permute-done.8.other), custom_call_target="tpu_custom_call" | custom-call | flops 201326592 | bytes 4194304 | tf_op jit(solution)/shard_map/pallas_call | solution.py:301
  82.0 10.0 %all_to_all.20 = bf16[4,128,256]{2,1,0:T(8,128)(2,1)S(1)} all-to-all(bf16[4,128,256]{2,1,0:T(8,128)(2,1)S(1)} %shard_map.109), channel_id=1, replica_groups=mesh['zh'=2,'y'=4,'core'=2,'x'=4,'zl'=8] {'y'}, dimensions={0} | all-to-all | bytes 524288 | tf_op jit(solution)/shard_map/all_to_all | solution.py:431
  92.0 3.7 %all-gather = bf16[8,128,256]{2,1,0:T(8,128)(2,1)S(1)} all-gather(bf16[4,128,256]{2,1,0:T(8,128)(2,1)S(1)} %all_to_all.20), channel_id=2, replica_groups=mesh['zh'=2,'y'=4,'core'=2,'x'=4,'zl'=8] {'core'}, dimensions={0}, use_global_device_ids=true | all-gather | bytes 786432 | tf_op jit(solution)/shard_map/all_gather | solution.py:431
  95.7 1.2 %shard_map.110 = bf16[2,1024,128]{2,1,0:T(8,128)(2,1)} custom-call(bf16[2,4,128,256]{3,2,1,0:T(8,128)(2,1)S(1)} %bitcast.20, bf16[2,256,128]{2,1,0:T(8,128)(2,1)S(1)} %copy-done.2), custom_call_target="tpu_custom_call" | custom-call | flops 134217728 | bytes 2097152 | tf_op jit(solution)/shard_map/pallas_call | solution.py:301
  (31 shorter events, 0.5 us)
Async XLA Ops:
  0.0 0.8 copy-start
  0.0 0.8 copy-start.5
  0.8 0.7 copy-start.6
  3.0 13.2 %copy-start.8 = (bf16[2,256]{1,0:T(2,128)(2,1)S(1)}, bf16[2,256]{1,0:T(2,128)(2,1)}, u32[]{:S(2)}) copy-start(bf16[2,256]{1,0:T(2,128)(2,1)} %param.12) | copy-start | bytes 3076
  3.0 13.3 %copy-start.4 = (bf16[2,128,256]{2,1,0:T(8,128)(2,1)S(1)}, bf16[2,128,256]{2,1,0:T(8,128)(2,1)}, u32[]{:S(2)}) copy-start(bf16[2,128,256]{2,1,0:T(8,128)(2,1)} %param.11) | copy-start | bytes 393220
  3.0 13.4 %copy-start.7 = (f32[256]{0:T(256)S(1)}, f32[256]{0:T(256)}, u32[]{:S(2)}) copy-start(f32[256]{0:T(256)} %param.13) | copy-start | bytes 3076
  3.0 30.6 %all-to-all-start = ((bf16[8,96,256]{2,1,0:T(8,128)(2,1)}), bf16[8,96,256]{2,1,0:T(8,128)(2,1)S(1)}, u32[]{:S(2)}, u32[]{:S(2)}) async-start(bf16[8,96,256]{2,1,0:T(8,128)(2,1)} %bitcast.6), calls=%async_computation | async-start | bytes 786432 | tf_op jit(solution)/shard_map/all_to_all | solution.py:362
  16.2 1.0 %copy-start.1 = (bf16[2,128,8,128]{3,2,1,0:T(8,128)(2,1)S(1)}, bf16[2,128,8,128]{3,2,1,0:T(8,128)(2,1)}, u32[]{:S(2)}) copy-start(bf16[2,128,8,128]{3,2,1,0:T(8,128)(2,1)} %param.10) | copy-start | bytes 1572868
  18.1 4.0 %collective-permute-start = (bf16[4,144,256]{2,1,0:T(8,128)(2,1)S(1)}, bf16[4,144,256]{2,1,0:T(8,128)(2,1)S(1)}, u32[]{:S(2)}, u32[]{:S(2)}) collective-permute-start(bf16[4,144,256]{2,1,0:T(8,128)(2,1)S(1)} %get-tuple-element.20), channel_id=1, source_target_pairs={{0,32},{32,0},{1,33},{33,1},{2,34},{34,2},{3,35},{35,3},{4,36},{36... | collective-permute-start | bytes 884744 | tf_op jit(solution)/shard_map/ppermute | solution.py:315
  22.6 16.0 %collective-permute-start.1 = (bf16[144,256]{1,0:T(8,128)(2,1)S(1)}, bf16[144,256]{1,0:T(8,128)(2,1)S(1)}, u32[]{:S(2)}, u32[]{:S(2)}) collective-permute-start(bf16[144,256]{1,0:T(8,128)(2,1)S(1)} %get-tuple-element.22), channel_id=1, source_target_pairs={{0,64},{64,128},{128,192},{192,0},{1,65},{65,129},{129,193},{193,1... | collective-permute-start | bytes 221192 | tf_op jit(solution)/shard_map/ppermute | solution.py:315
  25.8 12.8 %collective-permute-start.2 = (bf16[144,256]{1,0:T(8,128)(2,1)S(1)}, bf16[144,256]{1,0:T(8,128)(2,1)S(1)}, u32[]{:S(2)}, u32[]{:S(2)}) collective-permute-start(bf16[144,256]{1,0:T(8,128)(2,1)S(1)} %get-tuple-element.23), channel_id=1, source_target_pairs={{0,128},{64,192},{128,0},{192,64},{1,129},{65,193},{129,1},{193,65... | collective-permute-start | bytes 221192 | tf_op jit(solution)/shard_map/ppermute | solution.py:315
  30.4 8.2 %collective-permute-start.3 = (bf16[144,256]{1,0:T(8,128)(2,1)S(1)}, bf16[144,256]{1,0:T(8,128)(2,1)S(1)}, u32[]{:S(2)}, u32[]{:S(2)}) collective-permute-start(bf16[144,256]{1,0:T(8,128)(2,1)S(1)} %get-tuple-element.24), channel_id=1, source_target_pairs={{0,192},{64,0},{128,64},{192,128},{1,193},{65,1},{129,65},{193,129... | collective-permute-start | bytes 221192 | tf_op jit(solution)/shard_map/ppermute | solution.py:315
  34.6 12.4 %all-to-all-start.1 = ((bf16[4,8,48,256]{3,2,1,0:T(8,128)(2,1)}), bf16[4,8,48,256]{3,2,1,0:T(8,128)(2,1)S(1)}, u32[]{:S(2)}, u32[]{:S(2)}) async-start(bf16[4,8,48,256]{3,2,1,0:T(8,128)(2,1)} %get-tuple-element.28), calls=%async_computation.1 | async-start | bytes 1572864 | tf_op jit(solution)/shard_map/all_to_all | solution.py:398
  38.9 22.5 %collective-permute-start.4 = (bf16[144,256]{1,0:T(8,128)(2,1)S(1)}, bf16[144,256]{1,0:T(8,128)(2,1)S(1)}, u32[]{:S(2)}, u32[]{:S(2)}) collective-permute-start(bf16[144,256]{1,0:T(8,128)(2,1)S(1)} %get-tuple-element.27), channel_id=1, source_target_pairs={{0,256},{256,0},{1,257},{257,1},{2,258},{258,2},{3,259},{259,3},{4... | collective-permute-start | bytes 221192 | tf_op jit(solution)/shard_map/ppermute | solution.py:315
  46.9 14.7 %collective-permute-start.5 = (bf16[32,48,256]{2,1,0:T(8,128)(2,1)S(1)}, bf16[32,48,256]{2,1,0:T(8,128)(2,1)S(1)}, u32[]{:S(2)}, u32[]{:S(2)}) collective-permute-start(bf16[32,48,256]{2,1,0:T(8,128)(2,1)S(1)} %bitcast.15), channel_id=1, source_target_pairs={{0,32},{32,0},{1,33},{33,1},{2,34},{34,2},{3,35},{35,3},{4,36},{36... | collective-permute-start | bytes 2359304 | tf_op jit(solution)/shard_map/ppermute | solution.py:315
  57.8 15.8 %all-to-all-start.2 = ((bf16[4,8,48,256]{3,2,1,0:T(8,128)(2,1)}), bf16[4,8,48,256]{3,2,1,0:T(8,128)(2,1)S(1)}, u32[]{:S(2)}, u32[]{:S(2)}) async-start(bf16[4,8,48,256]{3,2,1,0:T(8,128)(2,1)} %shard_map.108), calls=%async_computation.2 | async-start | bytes 1572864 | tf_op jit(solution)/shard_map/all_to_all | solution.py:400
  61.4 0.7 copy-start.3
  64.4 12.6 %collective-permute-start.6 = (bf16[64,256]{1,0:T(8,128)(2,1)S(1)}, bf16[64,256]{1,0:T(8,128)(2,1)S(1)}, u32[]{:S(2)}, u32[]{:S(2)}) collective-permute-start(bf16[64,256]{1,0:T(8,128)(2,1)S(1)} %get-tuple-element.30), channel_id=1, source_target_pairs={{1,2},{3,4},{5,6},{2,1},{4,3},{6,5},{7,264},{0,287},{9,10},{11,12}... | collective-permute-start | bytes 98312 | tf_op jit(solution)/shard_map/ppermute | solution.py:418
  71.7 5.2 %collective-permute-start.7 = (bf16[64,256]{1,0:T(8,128)(2,1)S(1)}, bf16[64,256]{1,0:T(8,128)(2,1)S(1)}, u32[]{:S(2)}, u32[]{:S(2)}) collective-permute-start(bf16[64,256]{1,0:T(8,128)(2,1)S(1)} %get-tuple-element.31), channel_id=1, source_target_pairs={{0,1},{1,0},{2,3},{3,2},{4,5},{5,4},{6,7},{7,6},{8,9},{9,8},{10,11... | collective-permute-start | bytes 98312 | tf_op jit(solution)/shard_map/ppermute | solution.py:419
  73.7 5.1 %collective-permute-start.8 = (bf16[32,48,256]{2,1,0:T(8,128)(2,1)S(1)}, bf16[32,48,256]{2,1,0:T(8,128)(2,1)S(1)}, u32[]{:S(2)}, u32[]{:S(2)}) collective-permute-start(bf16[32,48,256]{2,1,0:T(8,128)(2,1)S(1)} %bitcast.18), channel_id=1, source_target_pairs={{0,32},{32,0},{1,33},{33,1},{2,34},{34,2},{3,35},{35,3},{4,36},{36... | collective-permute-start | bytes 2359304 | tf_op jit(solution)/shard_map/ppermute | solution.py:315
  92.0 3.7 %copy-start.2 = (bf16[2,256,128]{2,1,0:T(8,128)(2,1)S(1)}, bf16[2,256,128]{2,1,0:T(8,128)(2,1)}, u32[]{:S(2)}) copy-start(bf16[2,256,128]{2,1,0:T(8,128)(2,1)} %weight.1) | copy-start | bytes 393220
